TPU v7x, 32 devices: a whole 2x2x4 slice. The times are simulated.
32 devices in a mesh: clus: 8 (over y, x, core), sub: 4 (over z).
Axes of the slice: x: 2, y: 2, z: 4, core: 2. Of those that a mesh axis runs over, the one named last changes fastest.
Arguments:
- schur: bfloat16 [8, 4, 512, 512], P('clus', 'sub'), as said below
- load: float32 [8, 4, 4, 16, 128], P('clus', 'sub')
- rigid: float32 [8, 4, 4, 6, 128], P('clus', 'sub')
- lengths: int32 [8, 4, 4], P('clus', 'sub'), may hold values from 0 to 128, as said below
- partner: int32 [8, 4, 4, 128], P('clus', 'sub'), may hold values from 0 to 127, as said below
- coarse_inverse: float32 [48, 48], replicated, as said below
Outputs:
- multipliers: float32 [8, 4, 4, 16, 128], P('clus', 'sub')
- residual: float32 [8, 4, 4, 16, 128], P('clus', 'sub')
Inputs may be any that keep to these rules, and one draw needn't show every extreme that they name: `schur`: each subdomain's matrix is symmetric. `coarse_inverse`: symmetric. `lengths`: both sides of a neighbour pair hold the same length; 0 exactly where no neighbour exists; some pair has 128. On used rows, partner maps the used rows of a pair one to one onto the neighbour's used rows of the opposite direction, and the neighbour's partner maps them back; unused rows hold their own index.
All inputs are finite; a program needn't handle non-finite values.
Results may differ from a plain program's by a relative error of at most 0.0039.
Values sent between devices are 32-bit elements; how exact they have to be, the bound alone decides.
No kernel may reach another device: no remote copies, remote signals or barrier semaphores. Data moves between devices by JAX's collectives and lax.ppermute only.
A program may use at most 64 MiB of HBM per device.

v0:
```python
import jax
import jax.numpy as jnp
from jax import lax
from jax.sharding import PartitionSpec as P

ITERS = 2


FULL_PRECISION = lax.Precision.HIGHEST


def extended(block, sides, width):
    for axis, dim in sides:
        count = lax.axis_size(axis)
        forward = [(i, i + 1) for i in range(count - 1)]
        backward = [(target, source) for source, target in forward]
        low = lax.ppermute(
            lax.slice_in_dim(block, block.shape[dim] - width, None, axis=dim), axis, forward
        )
        high = lax.ppermute(lax.slice_in_dim(block, 0, width, axis=dim), axis, backward)
        block = jnp.concatenate([low, block, high], axis=dim)
    return block


def partner_rows(values, table):
    return jnp.einsum("djq,dkq->djk", values, table, precision=FULL_PRECISION)


def across(values, table):
    sub_rim = extended(values[0:2], (("sub", 0),), 1)
    clus_rim = extended(values[2:4], (("clus", 0),), 1)
    arrived = jnp.stack([sub_rim[0], sub_rim[3], clus_rim[0], clus_rim[3]])
    return partner_rows(arrived, table)


def coarse_reduce(local_part):
    within = lax.psum(local_part, "sub")
    return lax.all_gather(within[None], "clus", axis=0, tiled=True)


def inner_total(partial_value):
    return lax.psum(partial_value, ("clus", "sub"))


def half_dot(left_vec, right_vec):
    return 0.5 * jnp.sum(left_vec * right_vec, axis=(0, 2))


def shards(schur, load, rigid, lengths, partner, coarse_inverse):
    own_load = load[0, 0]
    case_count = own_load.shape[1]
    pair_rows = own_load.shape[2]
    rig_own = rigid[0, 0]
    mode_count = rig_own.shape[1]
    column_ids = lax.broadcasted_iota(jnp.int32, (4, pair_rows, pair_rows), 2)
    partner_map = (partner[0, 0][:, :, None] == column_ids).astype(jnp.float32)
    matrix = schur[0, 0]
    blocks = matrix.reshape(4, pair_rows, 4, pair_rows)
    clusters = lax.axis_size("clus")
    cluster_at = lax.axis_index("clus")
    slot_index = lax.broadcasted_iota(jnp.int32, (4, pair_rows), 1)
    live_rows = (slot_index < lengths[0, 0][:, None]).astype(jnp.float32)
    sign_table = jnp.array([-1.0, 1.0, -1.0, 1.0], jnp.float32)
    sign_live = (sign_table[:, None] * live_rows)[:, None, :]
    diag_own = jnp.diagonal(matrix).astype(jnp.float32).reshape(4, 1, pair_rows)
    signed_rigid = rig_own * sign_live
    arrived = across(jnp.concatenate([own_load, diag_own], axis=1), partner_map)

    def expand(coeffs):
        own_coeff = lax.dynamic_index_in_dim(coeffs, cluster_at, 0, keepdims=False)
        near_part = jnp.einsum("dmp,mj->djp", rig_own, own_coeff, precision=FULL_PRECISION)
        return sign_live * (near_part - across(near_part, partner_map))

    dual_rhs = sign_live * (own_load - arrived[:, :case_count])
    weight = live_rows[:, None, :] / (diag_own + arrived[:, case_count : case_count + 1])

    def coarse_local(vector):
        return jnp.einsum("dmp,djp->mj", signed_rigid, vector, precision=FULL_PRECISION)

    def coarse_solve(gathered):
        flattened = gathered.reshape(clusters * mode_count, case_count)
        coeffs = jnp.dot(coarse_inverse, flattened, precision=FULL_PRECISION)
        return coeffs.reshape(clusters, mode_count, case_count)

    multipliers = jnp.zeros_like(own_load)
    residual = dual_rhs
    direction = jnp.zeros_like(own_load)
    rho_old = jnp.ones((case_count,), jnp.float32)
    for iteration in range(ITERS):
        projected = residual - expand(coarse_solve(coarse_reduce(coarse_local(residual))))
        scaled = weight * projected
        precond = scaled - expand(coarse_solve(coarse_reduce(coarse_local(scaled))))
        rho_now = inner_total(half_dot(projected, precond))
        if iteration == 0:
            direction = precond
        else:
            direction = precond + (rho_now / rho_old)[:, None] * direction
        operand = (sign_live * direction).astype(jnp.bfloat16)
        image_rows = jnp.einsum(
            "dcp,dpeq->ecq", operand, blocks, preferred_element_type=jnp.float32
        )
        image_rows = sign_live * (image_rows - across(image_rows, partner_map))
        step_size = rho_now / inner_total(half_dot(direction, image_rows))
        multipliers = multipliers + step_size[:, None] * direction
        residual = residual - step_size[:, None] * image_rows
        rho_old = rho_now
    return (multipliers[None, None], residual[None, None])


def solution(mesh):
    in_specs = (
        P("clus", "sub", None, None),
        P("clus", "sub", None, None, None),
        P("clus", "sub", None, None, None),
        P("clus", "sub", None),
        P("clus", "sub", None, None),
        P(),
    )
    out_specs = (P("clus", "sub", None, None, None), P("clus", "sub", None, None, None))
    return jax.shard_map(shards, mesh=mesh, in_specs=in_specs, out_specs=out_specs, check_vma=False)
```

profile of v0, /device:TPU:0, one launch (start us, length us, event | category | flops | bytes accessed | tf_op | source)
XLA Modules:
  0.0 301.2 jit_solution(9127464888947192286)
XLA Ops:
  0.7 8.2 %gather_fusion = bf16[512]{0:T(512)(128)(2,1)S(1)} fusion(bf16[512,512]{1,0:T(8,128)(2,1)} %bitcast.87, s32[512]{0:T(512)S(1)} %bitcast.86), kind=kCustom, calls=%fused_computation | custom fusion | bytes 6144 | tf_op jit(solution)/shard_map/jit(diagonal)/cond/branch_0_fun/gather | solution.py:65
  9.0 4.9 %collective-permute-start = (f32[1,17,128]{2,1,0:T(8,128)S(1)}, f32[1,17,128]{2,1,0:T(8,128)S(1)}, u32[]{:S(2)}, u32[]{:S(2)}) collective-permute-start(f32[1,17,128]{2,1,0:T(8,128)S(1)} %get-tuple-element.6), channel_id=1, source_target_pairs={{0,1},{1,2},{2,3},{4,5},{5,6},{6,7},{8,9},{9,10},{10,11},{12,13},{... | collective-permute-start | bytes 26120 | tf_op jit(solution)/shard_map/ppermute | solution.py:17
  13.9 1.3 collective-permute-start.1
  15.2 1.3 collective-permute-start.3
  16.5 3.0 %collective-permute-start.2 = (f32[1,17,128]{2,1,0:T(8,128)S(1)}, f32[1,17,128]{2,1,0:T(8,128)S(1)}, u32[]{:S(2)}, u32[]{:S(2)}) collective-permute-start(f32[1,17,128]{2,1,0:T(8,128)S(1)} %get-tuple-element.9), channel_id=1, source_target_pairs={{0,4},{4,8},{8,12},{12,16},{16,20},{20,24},{24,28},{1,5},{5,9},{9,... | collective-permute-start | bytes 26120 | tf_op jit(solution)/shard_map/ppermute | solution.py:17
  19.7 0.7 collective-permute-done.2
  20.9 13.0 %psum.56 = f32[1,6,16]{2,1,0:T(8,128)S(1)} all-reduce(f32[1,6,16]{2,1,0:T(8,128)S(1)} %convolution_bitcast_fusion.13), channel_id=1, replica_groups=mesh['clus'=8,'sub'=4] {'sub'}, use_global_device_ids=true, to_apply=%region_0.1 | all-reduce | flops 96 | bytes 768 | tf_op jit(solution)/shard_map/psum | solution.py:37
  34.0 12.1 %all_gather.12 = f32[8,6,16]{2,1,0:T(8,128)S(1)} all-gather(f32[1,6,16]{2,1,0:T(8,128)S(1)} %psum.56), channel_id=1, replica_groups=mesh['clus'=8,'sub'=4] {'clus'}, dimensions={0}, use_global_device_ids=true | all-gather | bytes 3456 | tf_op jit(solution)/shard_map/all_gather | solution.py:38
  46.6 1.3 collective-permute-start.4
  47.9 1.3 collective-permute-start.7
  49.2 3.0 %collective-permute-start.6 = (f32[1,16,128]{2,1,0:T(8,128)S(1)}, f32[1,16,128]{2,1,0:T(8,128)S(1)}, u32[]{:S(2)}, u32[]{:S(2)}) collective-permute-start(f32[1,16,128]{2,1,0:T(8,128)S(1)} %get-tuple-element.32), channel_id=1, source_target_pairs={{0,4},{4,8},{8,12},{12,16},{16,20},{20,24},{24,28},{1,5},{5,9},{9,... | collective-permute-start | bytes 24584 | tf_op jit(solution)/shard_map/ppermute | solution.py:17
  52.2 1.3 collective-permute-start.5
  53.6 4.2 %collective-permute-done.5 = f32[1,16,128]{2,1,0:T(8,128)S(1)} collective-permute-done((f32[1,16,128]{2,1,0:T(8,128)S(1)}, f32[1,16,128]{2,1,0:T(8,128)S(1)}, u32[]{:S(2)}, u32[]{:S(2)}) %collective-permute-start.5) | collective-permute-done | bytes 8224 | tf_op jit(solution)/shard_map/ppermute | solution.py:20
  58.3 9.2 %psum.57 = f32[1,6,16]{2,1,0:T(8,128)S(1)} all-reduce(f32[1,6,16]{2,1,0:T(8,128)S(1)} %convolution_bitcast_fusion.12), channel_id=1, replica_groups=mesh['clus'=8,'sub'=4] {'sub'}, use_global_device_ids=true, to_apply=%region_1.2 | all-reduce | flops 96 | bytes 768 | tf_op jit(solution)/shard_map/psum | solution.py:37
  67.5 8.8 %all_gather.13 = f32[8,6,16]{2,1,0:T(8,128)S(1)} all-gather(f32[1,6,16]{2,1,0:T(8,128)S(1)} %psum.57), channel_id=1, replica_groups=mesh['clus'=8,'sub'=4] {'clus'}, dimensions={0}, use_global_device_ids=true | all-gather | bytes 3456 | tf_op jit(solution)/shard_map/all_gather | solution.py:38
  76.8 3.3 %collective-permute-start.8 = (f32[1,16,128]{2,1,0:T(8,128)S(1)}, f32[1,16,128]{2,1,0:T(8,128)S(1)}, u32[]{:S(2)}, u32[]{:S(2)}) collective-permute-start(f32[1,16,128]{2,1,0:T(8,128)S(1)} %get-tuple-element.26), channel_id=1, source_target_pairs={{0,1},{1,2},{2,3},{4,5},{5,6},{6,7},{8,9},{9,10},{10,11},{12,13},{... | collective-permute-start | bytes 24584 | tf_op jit(solution)/shard_map/ppermute | solution.py:17
  80.1 1.3 collective-permute-start.11
  81.4 3.0 %collective-permute-start.10 = (f32[1,16,128]{2,1,0:T(8,128)S(1)}, f32[1,16,128]{2,1,0:T(8,128)S(1)}, u32[]{:S(2)}, u32[]{:S(2)}) collective-permute-start(f32[1,16,128]{2,1,0:T(8,128)S(1)} %get-tuple-element.28), channel_id=1, source_target_pairs={{0,4},{4,8},{8,12},{12,16},{16,20},{20,24},{24,28},{1,5},{5,9},{9,... | collective-permute-start | bytes 24584 | tf_op jit(solution)/shard_map/ppermute | solution.py:17
  84.5 1.3 collective-permute-start.9
  85.9 4.1 %collective-permute-done.9 = f32[1,16,128]{2,1,0:T(8,128)S(1)} collective-permute-done((f32[1,16,128]{2,1,0:T(8,128)S(1)}, f32[1,16,128]{2,1,0:T(8,128)S(1)}, u32[]{:S(2)}, u32[]{:S(2)}) %collective-permute-start.9) | collective-permute-done | bytes 8224 | tf_op jit(solution)/shard_map/ppermute | solution.py:20
  90.6 1.9 collective-permute-start.12
  92.5 1.3 collective-permute-start.15
  93.8 3.0 %collective-permute-start.14 = (f32[1,16,128]{2,1,0:T(8,128)S(1)}, f32[1,16,128]{2,1,0:T(8,128)S(1)}, u32[]{:S(2)}, u32[]{:S(2)}) collective-permute-start(f32[1,16,128]{2,1,0:T(8,128)S(1)} %get-tuple-element.24), channel_id=1, source_target_pairs={{0,4},{4,8},{8,12},{12,16},{16,20},{20,24},{24,28},{1,5},{5,9},{9,... | collective-permute-start | bytes 24584 | tf_op jit(solution)/shard_map/ppermute | solution.py:17
  96.8 1.3 collective-permute-start.13
  98.2 4.2 %collective-permute-done.13 = f32[1,16,128]{2,1,0:T(8,128)S(1)} collective-permute-done((f32[1,16,128]{2,1,0:T(8,128)S(1)}, f32[1,16,128]{2,1,0:T(8,128)S(1)}, u32[]{:S(2)}, u32[]{:S(2)}) %collective-permute-start.13) | collective-permute-done | bytes 8224 | tf_op jit(solution)/shard_map/ppermute | solution.py:20
  102.9 39.2 %all-reduce = (f32[16]{0:T(128)S(1)}, f32[16]{0:T(128)S(1)}) all-reduce(f32[16]{0:T(128)S(1)} %get-tuple-element.42, f32[16]{0:T(128)S(1)} %get-tuple-element.41), channel_id=1, replica_groups=mesh['clus'=8,'sub'=4] {'clus','sub'}, use_global_device_ids=true, to_apply=%region_3.4 | all-reduce | flops 32 | bytes 256 | tf_op jit(solution)/shard_map/psum | solution.py:42
  142.3 9.9 %psum.60 = f32[1,6,16]{2,1,0:T(8,128)S(1)} all-reduce(f32[1,6,16]{2,1,0:T(8,128)S(1)} %convolution_bitcast_fusion.11), channel_id=1, replica_groups=mesh['clus'=8,'sub'=4] {'sub'}, use_global_device_ids=true, to_apply=%region_6.7 | all-reduce | flops 96 | bytes 768 | tf_op jit(solution)/shard_map/psum | solution.py:37
  152.2 9.8 %all_gather.14 = f32[8,6,16]{2,1,0:T(8,128)S(1)} all-gather(f32[1,6,16]{2,1,0:T(8,128)S(1)} %psum.60), channel_id=1, replica_groups=mesh['clus'=8,'sub'=4] {'clus'}, dimensions={0}, use_global_device_ids=true | all-gather | bytes 3456 | tf_op jit(solution)/shard_map/all_gather | solution.py:38
  162.6 2.3 collective-permute-start.16
  165.0 1.3 collective-permute-start.19
  166.3 3.0 %collective-permute-start.18 = (f32[1,16,128]{2,1,0:T(8,128)S(1)}, f32[1,16,128]{2,1,0:T(8,128)S(1)}, u32[]{:S(2)}, u32[]{:S(2)}) collective-permute-start(f32[1,16,128]{2,1,0:T(8,128)S(1)} %get-tuple-element.20), channel_id=1, source_target_pairs={{0,4},{4,8},{8,12},{12,16},{16,20},{20,24},{24,28},{1,5},{5,9},{9,... | collective-permute-start | bytes 24584 | tf_op jit(solution)/shard_map/ppermute | solution.py:17
  169.3 1.3 collective-permute-start.17
  170.6 4.2 %collective-permute-done.17 = f32[1,16,128]{2,1,0:T(8,128)S(1)} collective-permute-done((f32[1,16,128]{2,1,0:T(8,128)S(1)}, f32[1,16,128]{2,1,0:T(8,128)S(1)}, u32[]{:S(2)}, u32[]{:S(2)}) %collective-permute-start.17) | collective-permute-done | bytes 8224 | tf_op jit(solution)/shard_map/ppermute | solution.py:20
  175.4 8.4 %psum.61 = f32[1,6,16]{2,1,0:T(8,128)S(1)} all-reduce(f32[1,6,16]{2,1,0:T(8,128)S(1)} %convolution_bitcast_fusion.10), channel_id=1, replica_groups=mesh['clus'=8,'sub'=4] {'sub'}, use_global_device_ids=true, to_apply=%region_7.8 | all-reduce | flops 96 | bytes 768 | tf_op jit(solution)/shard_map/psum | solution.py:37
  183.7 10.1 %all_gather.15 = f32[8,6,16]{2,1,0:T(8,128)S(1)} all-gather(f32[1,6,16]{2,1,0:T(8,128)S(1)} %psum.61), channel_id=1, replica_groups=mesh['clus'=8,'sub'=4] {'clus'}, dimensions={0}, use_global_device_ids=true | all-gather | bytes 3456 | tf_op jit(solution)/shard_map/all_gather | solution.py:38
  194.4 3.6 %collective-permute-start.20 = (f32[1,16,128]{2,1,0:T(8,128)S(1)}, f32[1,16,128]{2,1,0:T(8,128)S(1)}, u32[]{:S(2)}, u32[]{:S(2)}) collective-permute-start(f32[1,16,128]{2,1,0:T(8,128)S(1)} %get-tuple-element.14), channel_id=1, source_target_pairs={{0,1},{1,2},{2,3},{4,5},{5,6},{6,7},{8,9},{9,10},{10,11},{12,13},{... | collective-permute-start | bytes 24584 | tf_op jit(solution)/shard_map/ppermute | solution.py:17
  198.0 1.3 collective-permute-start.23
  199.3 3.0 %collective-permute-start.22 = (f32[1,16,128]{2,1,0:T(8,128)S(1)}, f32[1,16,128]{2,1,0:T(8,128)S(1)}, u32[]{:S(2)}, u32[]{:S(2)}) collective-permute-start(f32[1,16,128]{2,1,0:T(8,128)S(1)} %get-tuple-element.16), channel_id=1, source_target_pairs={{0,4},{4,8},{8,12},{12,16},{16,20},{20,24},{24,28},{1,5},{5,9},{9,... | collective-permute-start | bytes 24584 | tf_op jit(solution)/shard_map/ppermute | solution.py:17
  202.3 1.3 collective-permute-start.21
  203.6 4.2 %collective-permute-done.21 = f32[1,16,128]{2,1,0:T(8,128)S(1)} collective-permute-done((f32[1,16,128]{2,1,0:T(8,128)S(1)}, f32[1,16,128]{2,1,0:T(8,128)S(1)}, u32[]{:S(2)}, u32[]{:S(2)}) %collective-permute-start.21) | collective-permute-done | bytes 8224 | tf_op jit(solution)/shard_map/ppermute | solution.py:20
  208.4 37.7 %psum.62 = f32[16]{0:T(128)S(1)} all-reduce(f32[16]{0:T(128)S(1)} %broadcast_multiply_fusion.2), channel_id=1, replica_groups=mesh['clus'=8,'sub'=4] {'clus','sub'}, use_global_device_ids=true, to_apply=%region_9.10 | all-reduce | flops 16 | bytes 128 | tf_op jit(solution)/shard_map/psum | solution.py:42
  246.3 3.9 %collective-permute-start.24 = (f32[1,16,128]{2,1,0:T(8,128)S(1)}, f32[1,16,128]{2,1,0:T(8,128)S(1)}, u32[]{:S(2)}, u32[]{:S(2)}) collective-permute-start(f32[1,16,128]{2,1,0:T(8,128)S(1)} %get-tuple-element.10), channel_id=1, source_target_pairs={{0,1},{1,2},{2,3},{4,5},{5,6},{6,7},{8,9},{9,10},{10,11},{12,13},{... | collective-permute-start | bytes 24584 | tf_op jit(solution)/shard_map/ppermute | solution.py:17
  250.3 1.3 collective-permute-start.27
  251.6 3.0 %collective-permute-start.26 = (f32[1,16,128]{2,1,0:T(8,128)S(1)}, f32[1,16,128]{2,1,0:T(8,128)S(1)}, u32[]{:S(2)}, u32[]{:S(2)}) collective-permute-start(f32[1,16,128]{2,1,0:T(8,128)S(1)} %get-tuple-element.12), channel_id=1, source_target_pairs={{0,4},{4,8},{8,12},{12,16},{16,20},{20,24},{24,28},{1,5},{5,9},{9,... | collective-permute-start | bytes 24584 | tf_op jit(solution)/shard_map/ppermute | solution.py:17
  254.6 1.3 collective-permute-start.25
  256.0 4.2 %collective-permute-done.25 = f32[1,16,128]{2,1,0:T(8,128)S(1)} collective-permute-done((f32[1,16,128]{2,1,0:T(8,128)S(1)}, f32[1,16,128]{2,1,0:T(8,128)S(1)}, u32[]{:S(2)}, u32[]{:S(2)}) %collective-permute-start.25) | collective-permute-done | bytes 8224 | tf_op jit(solution)/shard_map/ppermute | solution.py:20
  260.7 39.8 %psum.63 = f32[16]{0:T(128)S(1)} all-reduce(f32[16]{0:T(128)S(1)} %broadcast_multiply_fusion.1), channel_id=1, replica_groups=mesh['clus'=8,'sub'=4] {'clus','sub'}, use_global_device_ids=true, to_apply=%region_11.12 | all-reduce | flops 16 | bytes 128 | tf_op jit(solution)/shard_map/psum | solution.py:42
  300.5 0.7 subtract_bitcast_fusion
  (89 shorter events, 6.7 us)
Async XLA Ops:
  0.6 45.4 %copy-start = (f32[48,48]{1,0:T(8,128)S(1)}, f32[48,48]{1,0:T(8,128)}, u32[]{:S(2)}) copy-start(f32[48,48]{1,0:T(8,128)} %param.12) | copy-start | bytes 27652
  0.7 8.3 %copy-start.3 = (f32[1,1,4,16,128]{4,3,2,1,0:T(8,128)S(1)}, f32[1,1,4,16,128]{4,3,2,1,0:T(8,128)}, u32[]{:S(2)}) copy-start(f32[1,1,4,16,128]{4,3,2,1,0:T(8,128)} %param.8) | copy-start | bytes 98308
  8.9 10.6 %copy-start.4 = (s32[1,1,4]{2,1,0:T(1,128)S(1)}, s32[1,1,4]{2,1,0:T(1,128)}, u32[]{:S(2)}) copy-start(s32[1,1,4]{2,1,0:T(1,128)} %param.10) | copy-start | bytes 52
  8.9 10.6 %copy-start.5 = (f32[4]{0:T(128)S(1)}, f32[4]{0:T(128)}, u32[]{:S(2)}) copy-start(f32[4]{0:T(128)} %constant.30.clone) | copy-start | bytes 52
  9.0 10.7 %copy-start.2 = (f32[1,1,4,6,128]{4,2,3,1,0:T(4,128)S(1)}, f32[1,1,4,6,128]{4,2,3,1,0:T(4,128)}, u32[]{:S(2)}) copy-start(f32[1,1,4,6,128]{4,2,3,1,0:T(4,128)} %param.9) | copy-start | bytes 36868
  9.0 10.7 %collective-permute-start = (f32[1,17,128]{2,1,0:T(8,128)S(1)}, f32[1,17,128]{2,1,0:T(8,128)S(1)}, u32[]{:S(2)}, u32[]{:S(2)}) collective-permute-start(f32[1,17,128]{2,1,0:T(8,128)S(1)} %get-tuple-element.6), channel_id=1, source_target_pairs={{0,1},{1,2},{2,3},{4,5},{5,6},{6,7},{8,9},{9,10},{10,11},{12,13},{... | collective-permute-start | bytes 26120 | tf_op jit(solution)/shard_map/ppermute | solution.py:17
  13.9 5.8 %collective-permute-start.1 = (f32[1,17,128]{2,1,0:T(8,128)S(1)}, f32[1,17,128]{2,1,0:T(8,128)S(1)}, u32[]{:S(2)}, u32[]{:S(2)}) collective-permute-start(f32[1,17,128]{2,1,0:T(8,128)S(1)} %get-tuple-element.7), channel_id=1, source_target_pairs={{1,0},{2,1},{3,2},{5,4},{6,5},{7,6},{9,8},{10,9},{11,10},{13,12},{... | collective-permute-start | bytes 26120 | tf_op jit(solution)/shard_map/ppermute | solution.py:20
  15.2 4.5 %collective-permute-start.3 = (f32[1,17,128]{2,1,0:T(8,128)S(1)}, f32[1,17,128]{2,1,0:T(8,128)S(1)}, u32[]{:S(2)}, u32[]{:S(2)}) collective-permute-start(f32[1,17,128]{2,1,0:T(8,128)S(1)} %get-tuple-element.8), channel_id=1, source_target_pairs={{4,0},{8,4},{12,8},{16,12},{20,16},{24,20},{28,24},{5,1},{9,5},{13... | collective-permute-start | bytes 26120 | tf_op jit(solution)/shard_map/ppermute | solution.py:20
  16.5 3.9 %collective-permute-start.2 = (f32[1,17,128]{2,1,0:T(8,128)S(1)}, f32[1,17,128]{2,1,0:T(8,128)S(1)}, u32[]{:S(2)}, u32[]{:S(2)}) collective-permute-start(f32[1,17,128]{2,1,0:T(8,128)S(1)} %get-tuple-element.9), channel_id=1, source_target_pairs={{0,4},{4,8},{8,12},{12,16},{16,20},{20,24},{24,28},{1,5},{5,9},{9,... | collective-permute-start | bytes 26120 | tf_op jit(solution)/shard_map/ppermute | solution.py:17
  19.7 0.7 copy-start.6
  20.8 65.0 %copy-start.1 = (bf16[1,1,512,512]{3,2,1,0:T(8,128)(2,1)S(1)}, bf16[1,1,512,512]{3,2,1,0:T(8,128)(2,1)}, u32[]{:S(2)}) copy-start(bf16[1,1,512,512]{3,2,1,0:T(8,128)(2,1)} %param.7) | copy-start | bytes 1572868
  46.6 7.0 %collective-permute-start.4 = (f32[1,16,128]{2,1,0:T(8,128)S(1)}, f32[1,16,128]{2,1,0:T(8,128)S(1)}, u32[]{:S(2)}, u32[]{:S(2)}) collective-permute-start(f32[1,16,128]{2,1,0:T(8,128)S(1)} %get-tuple-element.30), channel_id=1, source_target_pairs={{0,1},{1,2},{2,3},{4,5},{5,6},{6,7},{8,9},{9,10},{10,11},{12,13},{... | collective-permute-start | bytes 24584 | tf_op jit(solution)/shard_map/ppermute | solution.py:17
  47.9 5.7 %collective-permute-start.7 = (f32[1,16,128]{2,1,0:T(8,128)S(1)}, f32[1,16,128]{2,1,0:T(8,128)S(1)}, u32[]{:S(2)}, u32[]{:S(2)}) collective-permute-start(f32[1,16,128]{2,1,0:T(8,128)S(1)} %get-tuple-element.31), channel_id=1, source_target_pairs={{4,0},{8,4},{12,8},{16,12},{20,16},{24,20},{28,24},{5,1},{9,5},{13... | collective-permute-start | bytes 24584 | tf_op jit(solution)/shard_map/ppermute | solution.py:20
  49.2 4.4 %collective-permute-start.6 = (f32[1,16,128]{2,1,0:T(8,128)S(1)}, f32[1,16,128]{2,1,0:T(8,128)S(1)}, u32[]{:S(2)}, u32[]{:S(2)}) collective-permute-start(f32[1,16,128]{2,1,0:T(8,128)S(1)} %get-tuple-element.32), channel_id=1, source_target_pairs={{0,4},{4,8},{8,12},{12,16},{16,20},{20,24},{24,28},{1,5},{5,9},{9,... | collective-permute-start | bytes 24584 | tf_op jit(solution)/shard_map/ppermute | solution.py:17
  52.2 5.5 %collective-permute-start.5 = (f32[1,16,128]{2,1,0:T(8,128)S(1)}, f32[1,16,128]{2,1,0:T(8,128)S(1)}, u32[]{:S(2)}, u32[]{:S(2)}) collective-permute-start(f32[1,16,128]{2,1,0:T(8,128)S(1)} %get-tuple-element.33), channel_id=1, source_target_pairs={{1,0},{2,1},{3,2},{5,4},{6,5},{7,6},{9,8},{10,9},{11,10},{13,12},{... | collective-permute-start | bytes 24584 | tf_op jit(solution)/shard_map/ppermute | solution.py:20
  76.8 9.1 %collective-permute-start.8 = (f32[1,16,128]{2,1,0:T(8,128)S(1)}, f32[1,16,128]{2,1,0:T(8,128)S(1)}, u32[]{:S(2)}, u32[]{:S(2)}) collective-permute-start(f32[1,16,128]{2,1,0:T(8,128)S(1)} %get-tuple-element.26), channel_id=1, source_target_pairs={{0,1},{1,2},{2,3},{4,5},{5,6},{6,7},{8,9},{9,10},{10,11},{12,13},{... | collective-permute-start | bytes 24584 | tf_op jit(solution)/shard_map/ppermute | solution.py:17
  80.1 5.8 %collective-permute-start.11 = (f32[1,16,128]{2,1,0:T(8,128)S(1)}, f32[1,16,128]{2,1,0:T(8,128)S(1)}, u32[]{:S(2)}, u32[]{:S(2)}) collective-permute-start(f32[1,16,128]{2,1,0:T(8,128)S(1)} %get-tuple-element.27), channel_id=1, source_target_pairs={{4,0},{8,4},{12,8},{16,12},{20,16},{24,20},{28,24},{5,1},{9,5},{13... | collective-permute-start | bytes 24584 | tf_op jit(solution)/shard_map/ppermute | solution.py:20
  81.4 4.5 %collective-permute-start.10 = (f32[1,16,128]{2,1,0:T(8,128)S(1)}, f32[1,16,128]{2,1,0:T(8,128)S(1)}, u32[]{:S(2)}, u32[]{:S(2)}) collective-permute-start(f32[1,16,128]{2,1,0:T(8,128)S(1)} %get-tuple-element.28), channel_id=1, source_target_pairs={{0,4},{4,8},{8,12},{12,16},{16,20},{20,24},{24,28},{1,5},{5,9},{9,... | collective-permute-start | bytes 24584 | tf_op jit(solution)/shard_map/ppermute | solution.py:17
  84.5 5.5 %collective-permute-start.9 = (f32[1,16,128]{2,1,0:T(8,128)S(1)}, f32[1,16,128]{2,1,0:T(8,128)S(1)}, u32[]{:S(2)}, u32[]{:S(2)}) collective-permute-start(f32[1,16,128]{2,1,0:T(8,128)S(1)} %get-tuple-element.29), channel_id=1, source_target_pairs={{1,0},{2,1},{3,2},{5,4},{6,5},{7,6},{9,8},{10,9},{11,10},{13,12},{... | collective-permute-start | bytes 24584 | tf_op jit(solution)/shard_map/ppermute | solution.py:20
  90.6 7.6 %collective-permute-start.12 = (f32[1,16,128]{2,1,0:T(8,128)S(1)}, f32[1,16,128]{2,1,0:T(8,128)S(1)}, u32[]{:S(2)}, u32[]{:S(2)}) collective-permute-start(f32[1,16,128]{2,1,0:T(8,128)S(1)} %get-tuple-element.22), channel_id=1, source_target_pairs={{0,1},{1,2},{2,3},{4,5},{5,6},{6,7},{8,9},{9,10},{10,11},{12,13},{... | collective-permute-start | bytes 24584 | tf_op jit(solution)/shard_map/ppermute | solution.py:17
  92.5 5.7 %collective-permute-start.15 = (f32[1,16,128]{2,1,0:T(8,128)S(1)}, f32[1,16,128]{2,1,0:T(8,128)S(1)}, u32[]{:S(2)}, u32[]{:S(2)}) collective-permute-start(f32[1,16,128]{2,1,0:T(8,128)S(1)} %get-tuple-element.23), channel_id=1, source_target_pairs={{4,0},{8,4},{12,8},{16,12},{20,16},{24,20},{28,24},{5,1},{9,5},{13... | collective-permute-start | bytes 24584 | tf_op jit(solution)/shard_map/ppermute | solution.py:20
  93.8 4.4 %collective-permute-start.14 = (f32[1,16,128]{2,1,0:T(8,128)S(1)}, f32[1,16,128]{2,1,0:T(8,128)S(1)}, u32[]{:S(2)}, u32[]{:S(2)}) collective-permute-start(f32[1,16,128]{2,1,0:T(8,128)S(1)} %get-tuple-element.24), channel_id=1, source_target_pairs={{0,4},{4,8},{8,12},{12,16},{16,20},{20,24},{24,28},{1,5},{5,9},{9,... | collective-permute-start | bytes 24584 | tf_op jit(solution)/shard_map/ppermute | solution.py:17
  96.8 5.5 %collective-permute-start.13 = (f32[1,16,128]{2,1,0:T(8,128)S(1)}, f32[1,16,128]{2,1,0:T(8,128)S(1)}, u32[]{:S(2)}, u32[]{:S(2)}) collective-permute-start(f32[1,16,128]{2,1,0:T(8,128)S(1)} %get-tuple-element.25), channel_id=1, source_target_pairs={{1,0},{2,1},{3,2},{5,4},{6,5},{7,6},{9,8},{10,9},{11,10},{13,12},{... | collective-permute-start | bytes 24584 | tf_op jit(solution)/shard_map/ppermute | solution.py:20
  162.6 8.0 %collective-permute-start.16 = (f32[1,16,128]{2,1,0:T(8,128)S(1)}, f32[1,16,128]{2,1,0:T(8,128)S(1)}, u32[]{:S(2)}, u32[]{:S(2)}) collective-permute-start(f32[1,16,128]{2,1,0:T(8,128)S(1)} %get-tuple-element.18), channel_id=1, source_target_pairs={{0,1},{1,2},{2,3},{4,5},{5,6},{6,7},{8,9},{9,10},{10,11},{12,13},{... | collective-permute-start | bytes 24584 | tf_op jit(solution)/shard_map/ppermute | solution.py:17
  165.0 5.7 %collective-permute-start.19 = (f32[1,16,128]{2,1,0:T(8,128)S(1)}, f32[1,16,128]{2,1,0:T(8,128)S(1)}, u32[]{:S(2)}, u32[]{:S(2)}) collective-permute-start(f32[1,16,128]{2,1,0:T(8,128)S(1)} %get-tuple-element.19), channel_id=1, source_target_pairs={{4,0},{8,4},{12,8},{16,12},{20,16},{24,20},{28,24},{5,1},{9,5},{13... | collective-permute-start | bytes 24584 | tf_op jit(solution)/shard_map/ppermute | solution.py:20
  166.3 4.4 %collective-permute-start.18 = (f32[1,16,128]{2,1,0:T(8,128)S(1)}, f32[1,16,128]{2,1,0:T(8,128)S(1)}, u32[]{:S(2)}, u32[]{:S(2)}) collective-permute-start(f32[1,16,128]{2,1,0:T(8,128)S(1)} %get-tuple-element.20), channel_id=1, source_target_pairs={{0,4},{4,8},{8,12},{12,16},{16,20},{20,24},{24,28},{1,5},{5,9},{9,... | collective-permute-start | bytes 24584 | tf_op jit(solution)/shard_map/ppermute | solution.py:17
  169.3 5.5 %collective-permute-start.17 = (f32[1,16,128]{2,1,0:T(8,128)S(1)}, f32[1,16,128]{2,1,0:T(8,128)S(1)}, u32[]{:S(2)}, u32[]{:S(2)}) collective-permute-start(f32[1,16,128]{2,1,0:T(8,128)S(1)} %get-tuple-element.21), channel_id=1, source_target_pairs={{1,0},{2,1},{3,2},{5,4},{6,5},{7,6},{9,8},{10,9},{11,10},{13,12},{... | collective-permute-start | bytes 24584 | tf_op jit(solution)/shard_map/ppermute | solution.py:20
  194.4 9.2 %collective-permute-start.20 = (f32[1,16,128]{2,1,0:T(8,128)S(1)}, f32[1,16,128]{2,1,0:T(8,128)S(1)}, u32[]{:S(2)}, u32[]{:S(2)}) collective-permute-start(f32[1,16,128]{2,1,0:T(8,128)S(1)} %get-tuple-element.14), channel_id=1, source_target_pairs={{0,1},{1,2},{2,3},{4,5},{5,6},{6,7},{8,9},{9,10},{10,11},{12,13},{... | collective-permute-start | bytes 24584 | tf_op jit(solution)/shard_map/ppermute | solution.py:17
  198.0 5.7 %collective-permute-start.23 = (f32[1,16,128]{2,1,0:T(8,128)S(1)}, f32[1,16,128]{2,1,0:T(8,128)S(1)}, u32[]{:S(2)}, u32[]{:S(2)}) collective-permute-start(f32[1,16,128]{2,1,0:T(8,128)S(1)} %get-tuple-element.15), channel_id=1, source_target_pairs={{4,0},{8,4},{12,8},{16,12},{20,16},{24,20},{28,24},{5,1},{9,5},{13... | collective-permute-start | bytes 24584 | tf_op jit(solution)/shard_map/ppermute | solution.py:20
  199.3 4.4 %collective-permute-start.22 = (f32[1,16,128]{2,1,0:T(8,128)S(1)}, f32[1,16,128]{2,1,0:T(8,128)S(1)}, u32[]{:S(2)}, u32[]{:S(2)}) collective-permute-start(f32[1,16,128]{2,1,0:T(8,128)S(1)} %get-tuple-element.16), channel_id=1, source_target_pairs={{0,4},{4,8},{8,12},{12,16},{16,20},{20,24},{24,28},{1,5},{5,9},{9,... | collective-permute-start | bytes 24584 | tf_op jit(solution)/shard_map/ppermute | solution.py:17
  202.3 5.5 %collective-permute-start.21 = (f32[1,16,128]{2,1,0:T(8,128)S(1)}, f32[1,16,128]{2,1,0:T(8,128)S(1)}, u32[]{:S(2)}, u32[]{:S(2)}) collective-permute-start(f32[1,16,128]{2,1,0:T(8,128)S(1)} %get-tuple-element.17), channel_id=1, source_target_pairs={{1,0},{2,1},{3,2},{5,4},{6,5},{7,6},{9,8},{10,9},{11,10},{13,12},{... | collective-permute-start | bytes 24584 | tf_op jit(solution)/shard_map/ppermute | solution.py:20
  246.3 9.6 %collective-permute-start.24 = (f32[1,16,128]{2,1,0:T(8,128)S(1)}, f32[1,16,128]{2,1,0:T(8,128)S(1)}, u32[]{:S(2)}, u32[]{:S(2)}) collective-permute-start(f32[1,16,128]{2,1,0:T(8,128)S(1)} %get-tuple-element.10), channel_id=1, source_target_pairs={{0,1},{1,2},{2,3},{4,5},{5,6},{6,7},{8,9},{9,10},{10,11},{12,13},{... | collective-permute-start | bytes 24584 | tf_op jit(solution)/shard_map/ppermute | solution.py:17
  250.3 5.7 %collective-permute-start.27 = (f32[1,16,128]{2,1,0:T(8,128)S(1)}, f32[1,16,128]{2,1,0:T(8,128)S(1)}, u32[]{:S(2)}, u32[]{:S(2)}) collective-permute-start(f32[1,16,128]{2,1,0:T(8,128)S(1)} %get-tuple-element.11), channel_id=1, source_target_pairs={{4,0},{8,4},{12,8},{16,12},{20,16},{24,20},{28,24},{5,1},{9,5},{13... | collective-permute-start | bytes 24584 | tf_op jit(solution)/shard_map/ppermute | solution.py:20
  251.6 4.4 %collective-permute-start.26 = (f32[1,16,128]{2,1,0:T(8,128)S(1)}, f32[1,16,128]{2,1,0:T(8,128)S(1)}, u32[]{:S(2)}, u32[]{:S(2)}) collective-permute-start(f32[1,16,128]{2,1,0:T(8,128)S(1)} %get-tuple-element.12), channel_id=1, source_target_pairs={{0,4},{4,8},{8,12},{12,16},{16,20},{20,24},{24,28},{1,5},{5,9},{9,... | collective-permute-start | bytes 24584 | tf_op jit(solution)/shard_map/ppermute | solution.py:17
  254.6 5.5 %collective-permute-start.25 = (f32[1,16,128]{2,1,0:T(8,128)S(1)}, f32[1,16,128]{2,1,0:T(8,128)S(1)}, u32[]{:S(2)}, u32[]{:S(2)}) collective-permute-start(f32[1,16,128]{2,1,0:T(8,128)S(1)} %get-tuple-element.13), channel_id=1, source_target_pairs={{1,0},{2,1},{3,2},{5,4},{6,5},{7,6},{9,8},{10,9},{11,10},{13,12},{... | collective-permute-start | bytes 24584 | tf_op jit(solution)/shard_map/ppermute | solution.py:20
where the time goes:
time: 303 us; the launch traced here: 301 us
  blocking collectives  198 us (65%)
  starting transfers between devices  60.6 us (20%)
  waiting for transfers between devices  25.8 us (9%)
  local copies, waits for them, and re-layouts  8.86 us (3%)
  matrix products  5.73 us (2%)
    psum x3, blocking collectives, inner_total(): return lax.psum(partial_value, ('clus', 'sub'))  117 us
    ppermute x14, starting transfers between devices, extended(): lax.ppermute(lax.slice_in_dim(block, block.shape[dim] - width, None, axis...  42.5 us
    all_gather x4, blocking collectives, coarse_reduce(): return lax.all_gather(within[None], 'clus', axis=0, tiled=True)  40.7 us
    psum x4, blocking collectives, coarse_reduce(): within = lax.psum(local_part, 'sub')  40.5 us
    ppermute x14, waiting for transfers between devices, extended(): lax.ppermute(lax.slice_in_dim(block, 0, width, axis=dim), axis, backward)  25.1 us
    ppermute x14, starting transfers between devices, extended(): lax.ppermute(lax.slice_in_dim(block, 0, width, axis=dim), axis, backward)  18.1 us
    gather x1, local copies, waits for them, and re-layouts, shards(): diag_own = jnp.diagonal(matrix).astype(jnp.float32).reshape(4, 1, pair_rows)  8.24 us
  transfers between devices with their start and end apart: 28, of which 7 were waited for; matrix products, arithmetic and copies ran while one was open for 0% of the time, Pallas kernels for 0%

commit v1 on v0

v1 whole, which is shorter than its diff:
```python
import jax
import jax.numpy as jnp
from jax import lax
from jax.sharding import PartitionSpec as P

AXES = ("clus", "sub")
PRECISION = lax.Precision.HIGHEST


def pair_even(index, count):
    other = index ^ 1
    return other if other < count else index


def pair_odd(index, count):
    other = ((index - 1) ^ 1) + 1
    return other if index > 0 and other < count else index


def swap_tables(clusters, subs):
    clus_even, clus_odd, sub_even, sub_odd = [], [], [], []
    for c in range(clusters):
        for s in range(subs):
            here = c * subs + s
            clus_even.append((here, pair_even(c, clusters) * subs + s))
            odd = pair_odd(c, clusters)
            target = odd * subs + s if odd != c else c * subs + pair_even(s, subs)
            clus_odd.append((here, target))
            sub_even.append((here, c * subs + pair_even(s, subs)))
            odd = pair_odd(s, subs)
            target = c * subs + odd if odd != s else pair_even(c, clusters) * subs + s
            sub_odd.append((here, target))
    return clus_even, clus_odd, sub_even, sub_odd


def exchange(values):
    clusters, subs = lax.axis_size("clus"), lax.axis_size("sub")
    clus_even, clus_odd, sub_even, sub_odd = swap_tables(clusters, subs)
    even_c = lax.axis_index("clus") % 2 == 0
    even_s = lax.axis_index("sub") % 2 == 0
    by_sub_even = lax.ppermute(jnp.where(even_s, values[1], values[0]), AXES, sub_even)
    by_sub_odd = lax.ppermute(jnp.where(even_s, values[0], values[1]), AXES, sub_odd)
    by_clus_odd = lax.ppermute(jnp.where(even_c, values[2], values[3]), AXES, clus_odd)
    by_clus_even = lax.ppermute(jnp.where(even_c, values[3], values[2]), AXES, clus_even)
    return jnp.stack([
        jnp.where(even_s, by_sub_odd, by_sub_even),
        jnp.where(even_s, by_sub_even, by_sub_odd),
        jnp.where(even_c, by_clus_odd, by_clus_even),
        jnp.where(even_c, by_clus_even, by_clus_odd),
    ])


def dot(left, right):
    return jnp.dot(left, right, precision=PRECISION)


def to_all(packed):
    count = lax.axis_size("clus") * lax.axis_size("sub")
    copies = jnp.broadcast_to(packed[None], (count, packed.shape[0]))
    return lax.all_to_all(copies, AXES, 0, 0, tiled=True)


def shards(schur, load, rigid, lengths, partner, coarse_inverse):
    own_load = load[0, 0]
    cases, pair_rows = own_load.shape[1], own_load.shape[2]
    rig_own = rigid[0, 0]
    modes = rig_own.shape[1]
    matrix = schur[0, 0]
    clusters, subs = lax.axis_size("clus"), lax.axis_size("sub")
    cluster_at = lax.axis_index("clus")
    rows = 4 * pair_rows

    table = (partner[0, 0][:, :, None] == lax.broadcasted_iota(jnp.int32, (4, pair_rows, pair_rows), 2))
    table = table.astype(jnp.float32)
    live = (lax.broadcasted_iota(jnp.int32, (4, pair_rows), 1) < lengths[0, 0][:, None])[:, None, :]
    sign = jnp.array([-1.0, 1.0, -1.0, 1.0], jnp.float32)[:, None, None]
    sign_live = sign * live.astype(jnp.float32)
    diag_mask = lax.broadcasted_iota(jnp.int32, (rows, rows), 0) == lax.broadcasted_iota(jnp.int32, (rows, rows), 1)
    diag_own = jnp.sum(jnp.where(diag_mask, matrix, 0).astype(jnp.float32), axis=0).reshape(4, 1, pair_rows)

    def far(values):
        return jnp.einsum("djq,dkq->djk", exchange(values), table, precision=PRECISION)

    def flat(values):
        return jnp.swapaxes(values, 0, 1).reshape(values.shape[1], rows)

    def unflat(values):
        return jnp.swapaxes(values.reshape(values.shape[0], 4, pair_rows), 0, 1)

    matrix32 = matrix.astype(jnp.float32)

    far_first = far(jnp.concatenate([own_load, rig_own, diag_own], axis=1))
    far_load = far_first[:, :cases]
    far_rigid = far_first[:, cases:cases + modes]
    far_diag = far_first[:, cases + modes:]
    weight = jnp.where(live, 1.0 / jnp.where(live, diag_own + far_diag, 1.0), 0.0)
    rhs = sign_live * (own_load - far_load)
    zero = jnp.zeros_like(rig_own[0])
    near = jnp.concatenate([rig_own[:2] - far_rigid[:2], rig_own[2:]])
    low = jnp.stack([zero, zero, -far_rigid[2], zero])
    high = jnp.stack([zero, zero, zero, -far_rigid[3]])
    basis = sign_live * jnp.concatenate([low, near, high], axis=1)
    weighted_basis = weight * basis
    weighted_rhs = weight * rhs

    operand = flat(sign_live * jnp.concatenate([weighted_basis, basis, weighted_rhs], axis=1))
    image = dot(operand, matrix32)
    span = 3 * modes
    gram = dot(operand[:2 * span], image.T)
    signed_rigid = flat(sign_live * rig_own)
    coarse_parts = dot(signed_rigid, flat(jnp.concatenate([rhs, weighted_rhs, weighted_basis], axis=1)).T)

    packed = jnp.concatenate([gram.reshape(-1), coarse_parts.reshape(-1)])
    gathered = to_all(packed).reshape(clusters, subs, -1)
    image_far = far(unflat(image))

    sums = jnp.sum(gathered, axis=1)
    gram_all = sums[:, :gram.size].reshape(clusters, 2 * span, 2 * span + cases)
    coarse_all = sums[:, gram.size:].reshape(clusters, modes, 2 * cases + span)

    order = clusters * modes
    tall = (clusters + 2) * modes

    def solve(values):
        return dot(coarse_inverse, values)

    def padded(values):
        return jnp.pad(values, ((modes, modes), (0, 0)))

    def near_coeffs(values):
        return jnp.stack([values[c * modes:c * modes + span] for c in range(clusters)])

    coupling = coarse_all[:, :, 2 * cases:]

    def couple(values):
        product = jnp.einsum("cmk,ckj->cmj", coupling, near_coeffs(padded(values)), precision=PRECISION)
        return product.reshape(order, cases)

    first_a = solve(coarse_all[:, :, :cases].reshape(order, cases))
    first_b = solve(coarse_all[:, :, cases:2 * cases].reshape(order, cases) - couple(first_a))
    near_first = jnp.concatenate([near_coeffs(padded(first_a)), near_coeffs(padded(first_b))], axis=1)
    parts = gram_all[:, :, 2 * span:] - jnp.einsum(
        "cik,ckj->cij", gram_all[:, :, :2 * span], near_first, precision=PRECISION
    )

    def assemble(values):
        total = jnp.zeros((tall, cases), jnp.float32)
        for c in range(clusters):
            total = total.at[c * modes:c * modes + span].add(values[c])
        return total[modes:modes + order]

    second_a = solve(assemble(parts[:, span:]))
    second_b = solve(assemble(parts[:, :span]) - couple(second_a))

    def local(values, shift):
        wide = jnp.pad(values, ((2 * modes, 2 * modes), (0, 0)))
        return lax.dynamic_slice_in_dim(wide, (cluster_at + 1 + shift) * modes, span, 0)

    def combine(coeffs, block):
        return jnp.einsum("kj,dkp->djp", coeffs, block, precision=PRECISION)

    def combine_one(coeffs, block):
        return jnp.einsum("kj,kp->jp", coeffs, block, precision=PRECISION)

    a_zero, b_zero = local(first_a, 0), local(first_b, 0)
    c_zero = jnp.concatenate([a_zero, b_zero])
    c_low = jnp.concatenate([local(first_a, -1), local(first_b, -1)])
    c_high = jnp.concatenate([local(first_a, 1), local(first_b, 1)])
    a_one, b_one = local(second_a, 0), local(second_b, 0)

    projected = rhs - combine(a_zero, basis)
    first = weight * projected - combine(b_zero, basis)
    image_own = unflat(image)
    pair = 2 * span
    own_part = image_own[:, pair:] - combine(c_zero, image_own[:, :pair])
    far_sum = jnp.stack([
        combine_one(c_zero, image_far[0, :pair]),
        combine_one(c_zero, image_far[1, :pair]),
        combine_one(c_low, image_far[2, :pair]),
        combine_one(c_high, image_far[3, :pair]),
    ])
    far_part = image_far[:, pair:] - far_sum
    applied = sign_live * (own_part - far_part)
    applied_projected = applied - combine(a_one, basis)
    second = weight * applied_projected - combine(b_one, basis)

    second_operand = sign_live * second
    second_image = unflat(dot(flat(second_operand), matrix32))

    def half_dot(left, right):
        return 0.5 * jnp.sum(left * right, axis=(0, 2))

    scalars = jnp.concatenate([
        half_dot(projected, first),
        half_dot(first, applied),
        half_dot(projected, second) + half_dot(applied_projected, first),
        half_dot(applied_projected, second),
        half_dot(applied, second),
        jnp.sum(second_operand * second_image, axis=(0, 2)),
    ])
    totals = jnp.sum(to_all(scalars), axis=0).reshape(6, cases)
    second_far = far(second_image)
    rho_one, delta_one, cross, square, mixed, delta_second = [totals[i] for i in range(6)]
    second_applied = sign_live * (second_image - second_far)

    alpha_one = rho_one / delta_one
    rho_two = rho_one - alpha_one * cross + alpha_one * alpha_one * square
    beta = rho_two / rho_one
    grow = 1.0 + beta
    delta_two = grow * grow * delta_one - 2.0 * grow * alpha_one * mixed + alpha_one * alpha_one * delta_second
    alpha_two = rho_two / delta_two
    keep = (alpha_one + alpha_two * grow)[:, None]
    drop = (alpha_two * alpha_one)[:, None]
    multipliers = keep * first - drop * second
    residual = rhs - keep * applied + drop * second_applied
    return (multipliers[None, None], residual[None, None])


def solution(mesh):
    in_specs = (
        P("clus", "sub", None, None),
        P("clus", "sub", None, None, None),
        P("clus", "sub", None, None, None),
        P("clus", "sub", None),
        P("clus", "sub", None, None),
        P(),
    )
    out_specs = (P("clus", "sub", None, None, None), P("clus", "sub", None, None, None))
    return jax.shard_map(shards, mesh=mesh, in_specs=in_specs, out_specs=out_specs, check_vma=False)
```

time: 303 us -> 66.7 us (0.22)
  blocking collectives: 198 us -> 0 us
  starting transfers between devices: 60.6 us -> 19.6 us
  waiting for transfers between devices: 25.8 us -> 16.1 us
  other arithmetic: 1.01 us -> 8.4 us
  local copies, waits for them, and re-layouts: 8.86 us -> 13.1 us
    psum x7 -> x0, blocking collectives: 157 us -> none  [the longest x3 117 us: inner_total(): return lax.psum(partial_value, ('clus', 'sub'))]
    ppermute x28 -> x12, starting transfers between devices: 60.6 us -> 12.7 us  [the longest x3 6.87 us: exchange(): lax.ppermute(jnp.where(even_s, values[1], values[0]), AXES, sub_even)]
    all_gather x4 -> x0, blocking collectives: 40.7 us -> none  [coarse_reduce(): return lax.all_gather(within[None], 'clus', axis=0, tiled=True)]
    ppermute x28 -> x12, waiting for transfers between devices: 25.8 us -> 4.79 us  [the longest x3 4.76 us: exchange(): lax.ppermute(jnp.where(even_c, values[2], values[3]), AXES, clus_odd)]
    all_to_all x0 -> x2, waiting for transfers between devices: none -> 11.3 us  [to_all(): return lax.all_to_all(copies, AXES, 0, 0, tiled=True)]
    gather x1 -> x0, local copies, waits for them, and re-layouts: 8.24 us -> none  [shards(): diag_own = jnp.diagonal(matrix).astype(jnp.float32).reshape(4, 1, pair_rows)]
    all_to_all x0 -> x2, starting transfers between devices: none -> 6.9 us  [to_all(): return lax.all_to_all(copies, AXES, 0, 0, tiled=True)]
    unnamed x14 -> x47, local copies, waits for them, and re-layouts: 0.05 us -> 5.76 us
  transfers between devices with their start and end apart: 28 -> 14, of which waited for: 7 -> 4; matrix products, arithmetic and copies ran while one was open for 0% -> 4% of each run, Pallas kernels for 0% -> 0%
where the time goes in v1:
time: 66.7 us; the launch traced here: 65.5 us
  starting transfers between devices  19.6 us (29%)
  waiting for transfers between devices  16.1 us (24%)
  local copies, waits for them, and re-layouts  13.1 us (20%)
  other arithmetic  8.4 us (13%)
  matrix products  7.04 us (11%)
  between operations  1.2 us (2%)
    all_to_all x2, waiting for transfers between devices, to_all(): return lax.all_to_all(copies, AXES, 0, 0, tiled=True)  11.3 us
    all_to_all x2, starting transfers between devices, to_all(): return lax.all_to_all(copies, AXES, 0, 0, tiled=True)  6.9 us
    ppermute x3, starting transfers between devices, exchange(): lax.ppermute(jnp.where(even_s, values[1], values[0]), AXES, sub_even)  6.87 us
    unnamed x47, local copies, waits for them, and re-layouts  5.76 us
    add x7, other arithmetic, assemble(): total = total.at[c * modes:c * modes + span].add(values[c])  5.18 us
    ppermute x3, waiting for transfers between devices, exchange(): lax.ppermute(jnp.where(even_c, values[2], values[3]), AXES, clus_odd)  4.76 us
    scatter-add x16, local copies, waits for them, and re-layouts, assemble(): total = total.at[c * modes:c * modes + span].add(values[c])  3.46 us
    ppermute x3, starting transfers between devices, exchange(): lax.ppermute(jnp.where(even_c, values[2], values[3]), AXES, clus_odd)  2.82 us
  transfers between devices with their start and end apart: 14, of which 4 were waited for; matrix products, arithmetic and copies ran while one was open for 4% of the time, Pallas kernels for 0%

profile of v1, /device:TPU:0, one launch (start us, length us, event | category | flops | bytes accessed | tf_op | source)
XLA Modules:
  0.0 65.5 jit_solution(12778694179251849559)
XLA Ops:
  0.7 0.8 %copy.72 = f32[1,1,4,6,128]{4,3,2,1,0:T(8,128)S(1)} copy(f32[1,1,4,6,128]{4,2,3,1,0:T(4,128)} %param.41) | data formatting | bytes 24576 | tf_op args[2]
  1.4 1.1 %convert_reduce_fusion = f32[512]{0:T(512)S(1)} fusion(bf16[1,1,512,512]{3,2,1,0:T(8,128)(2,1)} %param.39), kind=kLoop, calls=%fused_computation.29 | loop fusion | flops 1048064 | bytes 526336 | tf_op jit(solution)/shard_map/reduce_sum | solution.py:79
  2.6 0.5 collective-permute-start
  3.1 4.1 %collective-permute-start.1 = (f32[23,128]{1,0:T(8,128)S(1)}, f32[23,128]{1,0:T(8,128)S(1)}, u32[]{:S(2)}, u32[]{:S(2)}) collective-permute-start(f32[23,128]{1,0:T(8,128)S(1)} %get-tuple-element.237), channel_id=1, source_target_pairs={{0,1},{1,0},{2,3},{3,2},{4,5},{5,4},{6,7},{7,6},{8,9},{9,8},{10,11... | collective-permute-start | bytes 35336 | tf_op jit(solution)/shard_map/ppermute | solution.py:41
  7.3 1.6 %collective-permute-start.3 = (f32[23,128]{1,0:T(8,128)S(1)}, f32[23,128]{1,0:T(8,128)S(1)}, u32[]{:S(2)}, u32[]{:S(2)}) collective-permute-start(f32[23,128]{1,0:T(8,128)S(1)} %get-tuple-element.236), channel_id=1, source_target_pairs={{0,4},{1,5},{2,6},{3,7},{4,0},{5,1},{6,2},{7,3},{8,12},{9,13},{10,... | collective-permute-start | bytes 35336 | tf_op jit(solution)/shard_map/ppermute | solution.py:44
  8.9 0.7 copy-done.7
  9.9 1.1 %collective-permute-done.2 = f32[23,128]{1,0:T(8,128)S(1)} collective-permute-done((f32[23,128]{1,0:T(8,128)S(1)}, f32[23,128]{1,0:T(8,128)S(1)}, u32[]{:S(2)}, u32[]{:S(2)}) %collective-permute-start.2) | collective-permute-done | bytes 11808 | tf_op jit(solution)/shard_map/ppermute | solution.py:43
  11.0 0.7 %copy-done.9 = s32[1,1,4,128]{3,2,1,0:T(4,128)S(1)} copy-done((s32[1,1,4,128]{3,2,1,0:T(4,128)S(1)}, s32[1,1,4,128]{3,2,1,0:T(4,128)}, u32[]{:S(2)}) %copy-start.9) | copy-done | bytes 2072
  11.7 0.4 fusion.15
  12.3 0.6 copy-done.2
  12.9 0.4 fusion.12
  13.3 0.5 slice-done
  14.3 0.6 copy-done.6
  15.3 1.6 %collective-permute-start.5 = (f32[52,128]{1,0:T(8,128)S(1)}, f32[52,128]{1,0:T(8,128)S(1)}, u32[]{:S(2)}, u32[]{:S(2)}) collective-permute-start(f32[52,128]{1,0:T(8,128)S(1)} %get-tuple-element.210), channel_id=1, source_target_pairs={{0,1},{1,0},{2,3},{3,2},{4,5},{5,4},{6,7},{7,6},{8,9},{9,8},{10,11... | collective-permute-start | bytes 79880 | tf_op jit(solution)/shard_map/ppermute | solution.py:41
  17.0 0.8 %broadcast_in_dim.28 = f32[32,1,2172]{2,1,0:T(1,128)} broadcast(f32[2172]{0:T(1024)S(1)} %pad_maximum_fusion.1), dimensions={2} | broadcast | bytes 286704 | tf_op jit(solution)/shard_map/broadcast_in_dim | solution.py:59
  17.8 3.5 %all-to-all-start = ((f32[32,1,2172]{2,1,0:T(1,128)}), f32[32,1,2172]{2,1,0:T(1,128)S(1)}, u32[]{:S(2)}, u32[]{:S(2)}) async-start(f32[32,1,2172]{2,1,0:T(1,128)} %broadcast_in_dim.28), calls=%async_computation | async-start | bytes 557056 | tf_op jit(solution)/shard_map/all_to_all | solution.py:60
  21.4 1.8 %collective-permute-start.6 = (f32[52,128]{1,0:T(8,128)S(1)}, f32[52,128]{1,0:T(8,128)S(1)}, u32[]{:S(2)}, u32[]{:S(2)}) collective-permute-start(f32[52,128]{1,0:T(8,128)S(1)} %get-tuple-element.211), channel_id=1, source_target_pairs={{0,1},{1,0},{2,3},{3,2},{4,8},{5,9},{6,10},{7,11},{8,4},{9,5},{10,... | collective-permute-start | bytes 79880 | tf_op jit(solution)/shard_map/ppermute | solution.py:43
  23.3 3.7 %collective-permute-done.6 = f32[52,128]{1,0:T(8,128)S(1)} collective-permute-done((f32[52,128]{1,0:T(8,128)S(1)}, f32[52,128]{1,0:T(8,128)S(1)}, u32[]{:S(2)}, u32[]{:S(2)}) %collective-permute-start.6) | collective-permute-done | bytes 26656 | tf_op jit(solution)/shard_map/ppermute | solution.py:43
  27.0 0.5 fusion.14
  27.5 4.3 %all-to-all-done = f32[32,1,2172]{2,1,0:T(1,128)S(1)} async-done(((f32[32,1,2172]{2,1,0:T(1,128)}), f32[32,1,2172]{2,1,0:T(1,128)S(1)}, u32[]{:S(2)}, u32[]{:S(2)}) %all-to-all-start) | async-done | bytes 278048 | tf_op jit(solution)/shard_map/all_to_all | solution.py:60
  31.8 0.7 reduce.33
  32.8 0.5 copy-done.4
  34.2 0.3 convolution_subtract_fusion.2
  35.2 0.4 slice-done.1
  36.0 0.4 convolution_subtract_fusion
  36.7 0.3 copy-done.3
  37.6 0.3 scatter-add.69
  37.9 0.3 scatter-add.55
  38.2 0.9 %fusion.61 = (f32[18,16]{0,1:T(8,128)S(1)}, f32[18,16]{0,1:T(8,128)S(1)}) fusion(f32[8,36,16]{1,2,0:T(8,128)} %copy-done.3, f32[60,16]{0,1:T(8,128)S(1)} %scatter-add.69, f32[60,16]{0,1:T(8,128)S(1)} %scatter-add.55), kind=kLoop, calls=%fused_computation.158 | loop fusion | flops 576 | bytes 6912 | tf_op jit(solution)/shard_map/add | solution.py:149
  39.3 0.3 scatter-add.56
  39.5 0.9 %fusion.60 = (f32[18,16]{0,1:T(8,128)S(1)}, f32[18,16]{0,1:T(8,128)S(1)}) fusion(f32[8,36,16]{1,2,0:T(8,128)} %copy-done.3, f32[60,16]{0,1:T(8,128)S(1)} %scatter-add.70, f32[60,16]{0,1:T(8,128)S(1)} %scatter-add.56), kind=kLoop, calls=%fused_computation.156 | loop fusion | flops 576 | bytes 6912 | tf_op jit(solution)/shard_map/add | solution.py:149
  40.9 0.9 %fusion.59 = (f32[18,16]{0,1:T(8,128)S(1)}, f32[18,16]{0,1:T(8,128)S(1)}) fusion(f32[8,36,16]{1,2,0:T(8,128)} %copy-done.3, f32[60,16]{0,1:T(8,128)S(1)} %scatter-add.71, f32[60,16]{0,1:T(8,128)S(1)} %scatter-add.59), kind=kLoop, calls=%fused_computation.154 | loop fusion | flops 576 | bytes 6912 | tf_op jit(solution)/shard_map/add | solution.py:149
  41.9 0.3 scatter-add.60
  42.2 0.9 %fusion.58 = (f32[18,16]{0,1:T(8,128)S(1)}, f32[18,16]{0,1:T(8,128)S(1)}) fusion(f32[8,36,16]{1,2,0:T(8,128)} %copy-done.3, f32[60,16]{0,1:T(8,128)S(1)} %scatter-add.74, f32[60,16]{0,1:T(8,128)S(1)} %scatter-add.60), kind=kLoop, calls=%fused_computation.152 | loop fusion | flops 576 | bytes 6912 | tf_op jit(solution)/shard_map/add | solution.py:149
  43.5 0.9 %fusion.57 = (f32[18,16]{0,1:T(8,128)S(1)}, f32[18,16]{0,1:T(8,128)S(1)}) fusion(f32[8,36,16]{1,2,0:T(8,128)} %copy-done.3, f32[60,16]{0,1:T(8,128)S(1)} %scatter-add.75, f32[60,16]{0,1:T(8,128)S(1)} %scatter-add.61), kind=kLoop, calls=%fused_computation.150 | loop fusion | flops 576 | bytes 6912 | tf_op jit(solution)/shard_map/add | solution.py:149
  44.9 0.9 %fusion.56 = (f32[18,16]{0,1:T(8,128)S(1)}, f32[18,16]{0,1:T(8,128)S(1)}) fusion(f32[8,36,16]{1,2,0:T(8,128)} %copy-done.3, f32[60,16]{0,1:T(8,128)S(1)} %scatter-add.76, f32[60,16]{0,1:T(8,128)S(1)} %scatter-add.64), kind=kLoop, calls=%fused_computation.148 | loop fusion | flops 576 | bytes 6912 | tf_op jit(solution)/shard_map/add | solution.py:149
  46.9 0.3 fusion.51
  48.4 0.3 fusion.4
  49.0 0.7 %multiply_reduce_fusion = (f32[16]{0:T(128)S(1)}, f32[16]{0:T(128)S(1)}, f32[16]{0:T(128)S(1)}, f32[16]{0:T(128)S(1)}, f32[16]{0:T(128)S(1)}, /*index=5*/f32[16]...) fusion(f32[4,16,128]{2,1,0:T(8,128)S(1)} %fusion.4, f32[4,128]{1,0:T(4,128)S(1)} %fusion.89, ...), kind=kOutput, calls=%fused_computation.104 | convolution fusion | flops 50454416 | bytes 756160 | tf_op jit(solution)/shard_map/dot_general | solution.py:54
  49.6 0.3 collective-permute-start.8
  50.0 1.1 %collective-permute-start.9 = (f32[16,128]{1,0:T(8,128)S(1)}, f32[16,128]{1,0:T(8,128)S(1)}, u32[]{:S(2)}, u32[]{:S(2)}) collective-permute-start(f32[16,128]{1,0:T(8,128)S(1)} %get-tuple-element.243), channel_id=1, source_target_pairs={{0,1},{1,0},{2,3},{3,2},{4,5},{5,4},{6,7},{7,6},{8,9},{9,8},{10,11... | collective-permute-start | bytes 24584 | tf_op jit(solution)/shard_map/ppermute | solution.py:41
  51.0 0.9 %collective-permute-start.10 = (f32[16,128]{1,0:T(8,128)S(1)}, f32[16,128]{1,0:T(8,128)S(1)}, u32[]{:S(2)}, u32[]{:S(2)}) collective-permute-start(f32[16,128]{1,0:T(8,128)S(1)} %get-tuple-element.241), channel_id=1, source_target_pairs={{0,1},{1,0},{2,3},{3,2},{4,8},{5,9},{6,10},{7,11},{8,4},{9,5},{10,... | collective-permute-start | bytes 24584 | tf_op jit(solution)/shard_map/ppermute | solution.py:43
  52.0 0.4 collective-permute-start.11
  52.5 0.6 broadcast_in_dim.29
  53.1 3.4 %all-to-all-start.1 = ((f32[32,1,96]{2,1,0:T(1,128)}), f32[32,1,96]{2,1,0:T(1,128)S(1)}, u32[]{:S(2)}, u32[]{:S(2)}) async-start(f32[32,1,96]{2,1,0:T(1,128)} %broadcast_in_dim.29), calls=%async_computation.1 | async-start | bytes 32768 | tf_op jit(solution)/shard_map/all_to_all | solution.py:60
  56.6 7.0 %all-to-all-done.1 = f32[32,1,96]{2,1,0:T(1,128)S(1)} async-done(((f32[32,1,96]{2,1,0:T(1,128)}), f32[32,1,96]{2,1,0:T(1,128)S(1)}, u32[]{:S(2)}, u32[]{:S(2)}) %all-to-all-start.1) | async-done | bytes 12320 | tf_op jit(solution)/shard_map/all_to_all | solution.py:60
  63.8 0.7 %subtract_bitcast_fusion = f32[1,1,4,16,128]{4,3,2,1,0:T(8,128)} fusion(f32[4,16,128]{2,1,0:T(8,128)S(1)} %fusion.4, f32[4,16,128]{2,1,0:T(8,128)S(1)} %fusion.9, f32[16]{0:T(128)S(1)} %mul.247, f32[16]{0:T(128)S(1)} %get-tuple-element.201), kind=kLoop, calls=%fused_computation.103 | loop fusion | flops 24576 | bytes 98432 | tf_op jit(solution)/shard_map/broadcast_in_dim | solution.py:216
  64.5 1.0 %fusion.3 = f32[1,1,4,16,128]{4,3,2,1,0:T(8,128)} fusion(f32[4,16,128]{2,1,0:T(8,128)S(1)} %get-tuple-element.260, s32[4,128]{1,0:T(4,128)S(1)} %bitcast.348, f32[1,16,128]{2,1,0:T(8,128)S(1)} %get-tuple-element.251, f32[1,16,128]{2,1,0:T(8,128)S(1)} %get-tuple-element.250, f32[1,16,128]{2,1,0:T(8,128)S(1)} %get-tuple-element.249, ...), kind=kOutput, calls=%fused_computation.5 | convolution fusion | flops 12722176 | bytes 168064 | tf_op jit(solution)/shard_map/djq,dkq->djk/dot_general | solution.py:82
  (138 shorter events, 9.5 us)
Async XLA Ops:
  0.6 32.8 %copy-start = (f32[48,48]{1,0:T(8,128)S(1)}, f32[48,48]{1,0:T(8,128)}, u32[]{:S(2)}) copy-start(f32[48,48]{1,0:T(8,128)} %param.44) | copy-start | bytes 27652
  0.6 9.0 %copy-start.1 = (bf16[1,1,512,512]{3,2,1,0:T(8,128)(2,1)S(1)}, bf16[1,1,512,512]{3,2,1,0:T(8,128)(2,1)}, u32[]{:S(2)}) copy-start(bf16[1,1,512,512]{3,2,1,0:T(8,128)(2,1)} %param.39) | copy-start | bytes 1572868
  1.4 1.1 %copy-start.5 = (f32[1,1,4,16,128]{4,3,2,1,0:T(8,128)S(1)}, f32[1,1,4,16,128]{4,3,2,1,0:T(8,128)}, u32[]{:S(2)}) copy-start(f32[1,1,4,16,128]{4,3,2,1,0:T(8,128)} %param.40) | copy-start | bytes 98308
  2.6 7.2 %collective-permute-start = (f32[23,128]{1,0:T(8,128)S(1)}, f32[23,128]{1,0:T(8,128)S(1)}, u32[]{:S(2)}, u32[]{:S(2)}) collective-permute-start(f32[23,128]{1,0:T(8,128)S(1)} %get-tuple-element.234), channel_id=1, source_target_pairs={{0,4},{1,2},{2,1},{3,7},{4,0},{5,6},{6,5},{7,3},{8,12},{9,10},{10,... | collective-permute-start | bytes 35336 | tf_op jit(solution)/shard_map/ppermute | solution.py:42
  3.1 6.7 %collective-permute-start.1 = (f32[23,128]{1,0:T(8,128)S(1)}, f32[23,128]{1,0:T(8,128)S(1)}, u32[]{:S(2)}, u32[]{:S(2)}) collective-permute-start(f32[23,128]{1,0:T(8,128)S(1)} %get-tuple-element.237), channel_id=1, source_target_pairs={{0,1},{1,0},{2,3},{3,2},{4,5},{5,4},{6,7},{7,6},{8,9},{9,8},{10,11... | collective-permute-start | bytes 35336 | tf_op jit(solution)/shard_map/ppermute | solution.py:41
  7.3 3.7 %collective-permute-start.2 = (f32[23,128]{1,0:T(8,128)S(1)}, f32[23,128]{1,0:T(8,128)S(1)}, u32[]{:S(2)}, u32[]{:S(2)}) collective-permute-start(f32[23,128]{1,0:T(8,128)S(1)} %get-tuple-element.235), channel_id=1, source_target_pairs={{0,1},{1,0},{2,3},{3,2},{4,8},{5,9},{6,10},{7,11},{8,4},{9,5},{10,... | collective-permute-start | bytes 35336 | tf_op jit(solution)/shard_map/ppermute | solution.py:43
  7.3 3.7 %collective-permute-start.3 = (f32[23,128]{1,0:T(8,128)S(1)}, f32[23,128]{1,0:T(8,128)S(1)}, u32[]{:S(2)}, u32[]{:S(2)}) collective-permute-start(f32[23,128]{1,0:T(8,128)S(1)} %get-tuple-element.236), channel_id=1, source_target_pairs={{0,4},{1,5},{2,6},{3,7},{4,0},{5,1},{6,2},{7,3},{8,12},{9,13},{10,... | collective-permute-start | bytes 35336 | tf_op jit(solution)/shard_map/ppermute | solution.py:44
  8.9 0.7 %copy-start.7 = (s32[1,1,4]{2,1,0:T(1,128)S(1)}, s32[1,1,4]{2,1,0:T(1,128)}, u32[]{:S(2)}) copy-start(s32[1,1,4]{2,1,0:T(1,128)} %param.42) | copy-start | bytes 52
  8.9 0.7 %copy-start.8 = (f32[4]{0:T(128)S(1)}, f32[4]{0:T(128)}, u32[]{:S(2)}) copy-start(f32[4]{0:T(128)} %constant.442.clone) | copy-start | bytes 52
  11.0 0.7 %copy-start.9 = (s32[1,1,4,128]{3,2,1,0:T(4,128)S(1)}, s32[1,1,4,128]{3,2,1,0:T(4,128)}, u32[]{:S(2)}) copy-start(s32[1,1,4,128]{3,2,1,0:T(4,128)} %param.43) | copy-start | bytes 6148
  12.2 0.6 copy-start.2
  12.9 0.9 %slice-start = ((f32[52,4,128]{2,0,1:T(8,128)}), f32[36,4,128]{2,0,1:T(8,128)S(1)}, s32[]{:S(2)}) async-start(f32[52,4,128]{2,0,1:T(8,128)} %copy-done.2), calls=%async_computation.2 | async-start | bytes 163840 | tf_op jit(solution)/shard_map/slice | solution.py:109
  14.1 0.7 %copy-start.6 = (f32[1,1,4,6,128]{4,2,3,1,0:T(4,128)S(1)}, f32[1,1,4,6,128]{4,2,3,1,0:T(4,128)}, u32[]{:S(2)}) copy-start(f32[1,1,4,6,128]{4,2,3,1,0:T(4,128)} %param.41) | copy-start | bytes 36868
  15.2 8.1 %collective-permute-start.4 = (f32[52,128]{1,0:T(8,128)S(1)}, f32[52,128]{1,0:T(8,128)S(1)}, u32[]{:S(2)}, u32[]{:S(2)}) collective-permute-start(f32[52,128]{1,0:T(8,128)S(1)} %get-tuple-element.208), channel_id=1, source_target_pairs={{0,4},{1,2},{2,1},{3,7},{4,0},{5,6},{6,5},{7,3},{8,12},{9,10},{10,... | collective-permute-start | bytes 79880 | tf_op jit(solution)/shard_map/ppermute | solution.py:42
  15.3 8.1 %collective-permute-start.5 = (f32[52,128]{1,0:T(8,128)S(1)}, f32[52,128]{1,0:T(8,128)S(1)}, u32[]{:S(2)}, u32[]{:S(2)}) collective-permute-start(f32[52,128]{1,0:T(8,128)S(1)} %get-tuple-element.210), channel_id=1, source_target_pairs={{0,1},{1,0},{2,3},{3,2},{4,5},{5,4},{6,7},{7,6},{8,9},{9,8},{10,11... | collective-permute-start | bytes 79880 | tf_op jit(solution)/shard_map/ppermute | solution.py:41
  17.8 14.0 %all-to-all-start = ((f32[32,1,2172]{2,1,0:T(1,128)}), f32[32,1,2172]{2,1,0:T(1,128)S(1)}, u32[]{:S(2)}, u32[]{:S(2)}) async-start(f32[32,1,2172]{2,1,0:T(1,128)} %broadcast_in_dim.28), calls=%async_computation | async-start | bytes 557056 | tf_op jit(solution)/shard_map/all_to_all | solution.py:60
  21.4 5.6 %collective-permute-start.6 = (f32[52,128]{1,0:T(8,128)S(1)}, f32[52,128]{1,0:T(8,128)S(1)}, u32[]{:S(2)}, u32[]{:S(2)}) collective-permute-start(f32[52,128]{1,0:T(8,128)S(1)} %get-tuple-element.211), channel_id=1, source_target_pairs={{0,1},{1,0},{2,3},{3,2},{4,8},{5,9},{6,10},{7,11},{8,4},{9,5},{10,... | collective-permute-start | bytes 79880 | tf_op jit(solution)/shard_map/ppermute | solution.py:43
  23.2 3.8 %collective-permute-start.7 = (f32[52,128]{1,0:T(8,128)S(1)}, f32[52,128]{1,0:T(8,128)S(1)}, u32[]{:S(2)}, u32[]{:S(2)}) collective-permute-start(f32[52,128]{1,0:T(8,128)S(1)} %get-tuple-element.209), channel_id=1, source_target_pairs={{0,4},{1,5},{2,6},{3,7},{4,0},{5,1},{6,2},{7,3},{8,12},{9,13},{10,... | collective-permute-start | bytes 79880 | tf_op jit(solution)/shard_map/ppermute | solution.py:44
  32.7 0.6 copy-start.4
  34.8 0.8 %slice-start.1 = ((f32[8,2172]{1,0:T(8,128)}), f32[8,1872]{1,0:T(8,128)S(1)}, s32[]{:S(2)}) async-start(f32[8,2172]{1,0:T(8,128)} %copy-done.4), calls=%async_computation.3 | async-start | bytes 122880 | tf_op jit(solution)/shard_map/slice | solution.py:118
  36.4 0.6 copy-start.3
  49.6 6.9 %collective-permute-start.8 = (f32[16,128]{1,0:T(8,128)S(1)}, f32[16,128]{1,0:T(8,128)S(1)}, u32[]{:S(2)}, u32[]{:S(2)}) collective-permute-start(f32[16,128]{1,0:T(8,128)S(1)} %get-tuple-element.240), channel_id=1, source_target_pairs={{0,4},{1,2},{2,1},{3,7},{4,0},{5,6},{6,5},{7,3},{8,12},{9,10},{10,... | collective-permute-start | bytes 24584 | tf_op jit(solution)/shard_map/ppermute | solution.py:42
  50.0 6.6 %collective-permute-start.9 = (f32[16,128]{1,0:T(8,128)S(1)}, f32[16,128]{1,0:T(8,128)S(1)}, u32[]{:S(2)}, u32[]{:S(2)}) collective-permute-start(f32[16,128]{1,0:T(8,128)S(1)} %get-tuple-element.243), channel_id=1, source_target_pairs={{0,1},{1,0},{2,3},{3,2},{4,5},{5,4},{6,7},{7,6},{8,9},{9,8},{10,11... | collective-permute-start | bytes 24584 | tf_op jit(solution)/shard_map/ppermute | solution.py:41
  51.0 5.5 %collective-permute-start.10 = (f32[16,128]{1,0:T(8,128)S(1)}, f32[16,128]{1,0:T(8,128)S(1)}, u32[]{:S(2)}, u32[]{:S(2)}) collective-permute-start(f32[16,128]{1,0:T(8,128)S(1)} %get-tuple-element.241), channel_id=1, source_target_pairs={{0,1},{1,0},{2,3},{3,2},{4,8},{5,9},{6,10},{7,11},{8,4},{9,5},{10,... | collective-permute-start | bytes 24584 | tf_op jit(solution)/shard_map/ppermute | solution.py:43
  52.0 4.6 %collective-permute-start.11 = (f32[16,128]{1,0:T(8,128)S(1)}, f32[16,128]{1,0:T(8,128)S(1)}, u32[]{:S(2)}, u32[]{:S(2)}) collective-permute-start(f32[16,128]{1,0:T(8,128)S(1)} %get-tuple-element.242), channel_id=1, source_target_pairs={{0,4},{1,5},{2,6},{3,7},{4,0},{5,1},{6,2},{7,3},{8,12},{9,13},{10,... | collective-permute-start | bytes 24584 | tf_op jit(solution)/shard_map/ppermute | solution.py:44
  53.1 10.5 %all-to-all-start.1 = ((f32[32,1,96]{2,1,0:T(1,128)}), f32[32,1,96]{2,1,0:T(1,128)S(1)}, u32[]{:S(2)}, u32[]{:S(2)}) async-start(f32[32,1,96]{2,1,0:T(1,128)} %broadcast_in_dim.29), calls=%async_computation.1 | async-start | bytes 32768 | tf_op jit(solution)/shard_map/all_to_all | solution.py:60

commit v2 on v0

v2 whole, which is shorter than its diff:
```python
import functools

import jax
import jax.numpy as jnp
from jax import lax
from jax.experimental import pallas as pl
from jax.experimental.pallas import tpu as pltpu
from jax.sharding import PartitionSpec as P

AXES = ("clus", "sub")
F32 = jnp.float32
BF16 = jnp.bfloat16
FULL = lax.Precision.HIGHEST
STRIP = 8
PACK = 16
VMEM_LIMIT = 48 * 1024 * 1024


def pair_even(index, count):
    other = index ^ 1
    return other if other < count else index


def pair_odd(index, count):
    other = ((index - 1) ^ 1) + 1
    return other if index > 0 and other < count else index


def swap_tables(clusters, subs):
    sub_even, sub_odd, clus_odd, clus_even = [], [], [], []
    for c in range(clusters):
        for s in range(subs):
            here = c * subs + s
            sub_even.append((here, c * subs + pair_even(s, subs)))
            odd = pair_odd(s, subs)
            target = c * subs + odd if odd != s else pair_even(c, clusters) * subs + s
            sub_odd.append((here, target))
            odd = pair_odd(c, clusters)
            target = odd * subs + s if odd != c else c * subs + pair_even(s, subs)
            clus_odd.append((here, target))
            clus_even.append((here, pair_even(c, clusters) * subs + s))
    return sub_even, sub_odd, clus_odd, clus_even


def swap(buffers):
    tables = swap_tables(lax.axis_size("clus"), lax.axis_size("sub"))
    return [lax.ppermute(buffer, AXES, table) for buffer, table in zip(buffers, tables)]


def parities():
    even_c = lax.rem(lax.axis_index("clus"), 2) == 0
    even_s = lax.rem(lax.axis_index("sub"), 2) == 0
    return even_c, even_s


def by_swap(values):
    even_c, even_s = parities()
    return [
        jnp.where(even_s, values[1], values[0]),
        jnp.where(even_s, values[0], values[1]),
        jnp.where(even_c, values[2], values[3]),
        jnp.where(even_c, values[3], values[2]),
    ]


def by_direction(values):
    even_c, even_s = parities()
    return [
        jnp.where(even_s, values[1], values[0]),
        jnp.where(even_s, values[0], values[1]),
        jnp.where(even_c, values[2], values[3]),
        jnp.where(even_c, values[3], values[2]),
    ]


def halves(values):
    high = values.astype(BF16)
    return high, (values - high.astype(F32)).astype(BF16)


def product(left, right):
    return jnp.dot(left, right, preferred_element_type=F32)


def full_product(left, right):
    return jnp.dot(left, right, preferred_element_type=F32, precision=FULL)


def full_product_t(left, right):
    return lax.dot_general(left, right, (((1,), (1,)), ((), ())), preferred_element_type=F32, precision=FULL)


def reorder(values, table):
    count = values.shape[0]
    high, rest = halves(values)
    low = (values - high.astype(F32) - rest.astype(F32)).astype(BF16)
    moved = product(jnp.concatenate([high, rest, low]), table)
    return moved[:count] + moved[count:2 * count] + moved[2 * count:]


def times_matrix(values, matrix):
    count = values.shape[0]
    high, low = halves(values)
    both = product(jnp.concatenate([high, low]), matrix)
    return both[:count] + both[count:]


def start_kernel(pair, modes, load, rigid, schur, to_a, to_b, to_c, to_d, diag_out, buffer):
    cases = load.shape[1]
    eye = lax.broadcasted_iota(jnp.int32, (pair, pair), 0) == lax.broadcasted_iota(jnp.int32, (pair, pair), 1)
    buffer[...] = jnp.zeros_like(buffer)
    for d in range(4):
        span = slice(d * pair, (d + 1) * pair)
        diag = jnp.sum(jnp.where(eye, schur[span, span].astype(F32), 0.0), axis=0, keepdims=True)
        diag_out[:, span] = diag
        buffer[d, 0:cases] = load[d]
        buffer[d, cases:cases + modes] = rigid[d]
        buffer[d, cases + STRIP - 1:cases + STRIP] = diag
    for out, values in zip((to_a, to_b, to_c, to_d), by_swap([buffer[d] for d in range(4)])):
        out[...] = values


def gram_kernel(
    pair, modes, devices, load, rigid, schur, diag_own, sign_live, tables, from_a, from_b, from_c, from_d,
    packed, to_a, to_b, to_c, to_d, rhs, first, weight, basis, image, operand, right
):
    cases = load.shape[1]
    span = 3 * STRIP
    arrived = by_direction([from_a[...], from_b[...], from_c[...], from_d[...]])
    basis[...] = jnp.zeros_like(basis)
    right[...] = jnp.zeros_like(right)
    for d in range(4):
        lanes = slice(d * pair, (d + 1) * pair)
        sign = sign_live[:, lanes]
        distant = reorder(arrived[d], tables[d])
        distant_rigid = distant[cases:cases + modes]
        own_rigid = rigid[d]
        both = diag_own[:, lanes] + distant[cases + STRIP - 1:cases + STRIP]
        is_live = sign != 0.0
        inverse = jnp.where(is_live, 1.0 / jnp.where(is_live, both, 1.0), 0.0)
        weight[:, lanes] = inverse
        own_rhs = sign * (load[d] - distant[:cases])
        rhs[:, lanes] = own_rhs
        first[:, lanes] = inverse * own_rhs
        near = own_rigid - distant_rigid if d < 2 else own_rigid
        basis[span + STRIP:span + STRIP + modes, lanes] = sign * near
        if d >= 2:
            at = span if d == 2 else span + 2 * STRIP
            basis[at:at + modes, lanes] = -sign * distant_rigid
        right[6 * modes:7 * modes, lanes] = own_rigid
    basis[0:span] = weight[...] * basis[span:2 * span]
    signs = sign_live[...]
    operand[0:2 * span] = signs * basis[...]
    operand[2 * span:2 * span + cases] = signs * first[...]
    operand[2 * span + cases:2 * span + 2 * cases] = signs * rhs[...]
    image[...] = times_matrix(operand[0:2 * span + cases], schur[...])
    for g in range(6):
        right[g * modes:(g + 1) * modes] = image[g * STRIP:g * STRIP + modes]
    gram = full_product_t(operand[...], right[...])
    lane = lax.broadcasted_iota(jnp.int32, (STRIP, gram.shape[1]), 1)
    strips = []
    for g in range(6):
        strip = gram[g * STRIP:(g + 1) * STRIP]
        own = (lane >= g * modes) & (lane < (g + 1) * modes)
        strips.append(jnp.where(own, 0.5 * strip, strip))
    rows = []
    for row in pack_places(modes):
        total = jnp.zeros_like(strips[0])
        for g, begin, end, at in row:
            piece = strips[g] if at == begin else pltpu.roll(strips[g], (at - begin) % lane.shape[1], 1)
            total = jnp.where((lane >= at) & (lane < at + end - begin), piece, total)
        rows.append(total)
    total = jnp.concatenate(rows)
    lane = lax.broadcasted_iota(jnp.int32, total.shape, 1)
    at = 12 * modes
    with_first = gram[2 * span:2 * span + cases]
    with_rhs = gram[2 * span + cases:2 * span + 2 * cases]
    total = jnp.where(lane >= at, pltpu.roll(with_first, at, 1), total)
    total = jnp.where(lane >= at + 7 * modes, pltpu.roll(with_rhs, at + modes, 1), total)

    def spread(i, carry):
        packed[pl.ds(pl.multiple_of(i * PACK, PACK), PACK)] = total
        return carry

    lax.fori_loop(0, devices, spread, 0, unroll=min(devices, 32))
    parts = [image[:, d * pair:(d + 1) * pair] for d in range(4)]
    for out, values in zip((to_a, to_b, to_c, to_d), by_swap(parts)):
        out[...] = values


def pack_places(modes):
    upper = [(0, 0, 7 * modes, 0), (2, 2 * modes, 7 * modes, 7 * modes)]
    lower = [
        (1, modes, 7 * modes, 0), (3, 3 * modes, 6 * modes, 6 * modes),
        (4, 4 * modes, 6 * modes, 9 * modes), (5, 5 * modes, 6 * modes, 11 * modes),
    ]
    return upper, lower


def basis_kernel(
    pair, clusters, basis, image, sign_live, tables, from_a, from_b, from_c, from_d, stacked, applied_first, wide
):
    span = 3 * STRIP
    rows = 4 * pair
    width = clusters * STRIP
    cluster_at = lax.axis_index("clus")
    arrived = by_direction([from_a[...], from_b[...], from_c[...], from_d[...]])
    wide[...] = jnp.zeros_like(wide)
    near = pl.ds(pl.multiple_of((cluster_at + 1) * STRIP, STRIP), span)
    signs = sign_live[...]
    wide[near, 0:rows] = basis[span:2 * span]
    wide[near, rows:2 * rows] = basis[0:span]
    wide[near, 2 * rows:3 * rows] = signs * image[0:span]
    wide[near, 3 * rows:4 * rows] = signs * image[span:2 * span]
    for d in range(4):
        lanes = slice(d * pair, (d + 1) * pair)
        sign = sign_live[:, lanes]
        distant = sign * reorder(arrived[d], tables[d])
        at = pl.ds(pl.multiple_of((cluster_at + (1, 1, 0, 2)[d]) * STRIP, STRIP), span)
        for k in range(2):
            begin = (2 + k) * rows + d * pair
            wide[at, begin:begin + pair] -= distant[k * span:(k + 1) * span]
        applied_first[:, lanes] = sign * image[2 * span:, lanes] - distant[2 * span:]
    high, low = halves(wide[2 * STRIP:2 * STRIP + width])
    stacked[0:width] = high
    stacked[width:2 * width] = low
    stacked[2 * width:3 * width] = high


def unpack(sums, modes, clusters, cases):
    width = clusters * STRIP
    lane = lax.broadcasted_iota(jnp.int32, (PACK, 128), 1)
    upper, coupling, with_first, tails = {}, {}, {}, {}

    def put(store, key, values, begin, column):
        tile, offset = divmod(column, 128)
        shift = (offset - begin) % 128
        moved = pltpu.roll(values, shift, 1) if shift else values
        mask = lane[:values.shape[0]]
        piece = jnp.where((mask >= offset) & (mask < offset + modes), moved, 0.0)
        key = key + (tile,)
        store[key] = store[key] + piece if key in store else piece

    def group(c, h):
        other = c - 1 + h % 3
        return other, (h // 3) * width + other * STRIP

    for c in range(clusters):
        for half, row in enumerate(pack_places(modes)):
            values = sums[c][half * STRIP:(half + 1) * STRIP]
            for g, begin, end, at in row:
                row_cluster, row_at = group(c, g)
                if not 0 <= row_cluster < clusters:
                    continue
                for h in range(begin // modes, end // modes):
                    source = at + h * modes - begin
                    if h == 6:
                        put(coupling, (row_at // STRIP,), values, source, c * STRIP)
                        continue
                    other, column = group(c, h)
                    if 0 <= other < clusters:
                        put(upper, (row_at // STRIP,), values, source, column)
        for h in range(6):
            other, column = group(c, h)
            if 0 <= other < clusters:
                put(with_first, (), sums[c], 12 * modes + h * modes, column)
        put(tails, (0,), sums[c], 19 * modes, c * STRIP)
        put(tails, (1,), sums[c], 18 * modes, c * STRIP)
    return upper, coupling, with_first, tails


def solve_kernel(
    pair, modes, clusters, subs, cases, gathered, inverse, stacked, rhs, first_part, applied_first, weight, sign_live,
    schur, scalars, to_a, to_b, to_c, to_d, first, applied, second, second_image, upper_ref, couple_ref, row_ref,
    tail_ref
):
    width = clusters * STRIP
    rows = 4 * pair
    sums = []
    for c in range(clusters):
        total = gathered[c * subs * PACK:(c * subs + 1) * PACK]
        for s in range(1, subs):
            total = total + gathered[(c * subs + s) * PACK:(c * subs + s + 1) * PACK]
        sums.append(total)
    upper, coupling, with_first, tails = unpack(sums, modes, clusters, cases)

    def fill(ref, store, height):
        for i in range(ref.shape[0] // height):
            for t in range(ref.shape[1] // 128):
                key = (i, t) if len(next(iter(store))) == 2 else (t,)
                values = store[key] if key in store else jnp.zeros((height, 128), F32)
                ref[i * height:(i + 1) * height, t * 128:(t + 1) * 128] = values

    fill(upper_ref, upper, STRIP)
    fill(couple_ref, coupling, STRIP)
    fill(row_ref, with_first, PACK)
    fill(tail_ref, tails, PACK)

    solver = inverse[...]
    couple_solver = full_product(couple_ref[:, :width], solver)

    def coeffs(straight, weighted):
        both = full_product(jnp.concatenate([straight, weighted]), solver)
        a = both[:PACK]
        return a, both[PACK:] - full_product(a, couple_solver)

    tail = tail_ref[:, :width]
    a_first, b_first = coeffs(tail[:PACK], tail[PACK:])
    c_first = jnp.concatenate([a_first, b_first], axis=1)
    upper_matrix = upper_ref[:, :2 * width]
    parts = row_ref[:, :2 * width] - full_product(c_first, upper_matrix) - full_product_t(c_first, upper_matrix)
    a_second, b_second = coeffs(parts[:, width:], parts[:, :width])

    high, low = halves(jnp.concatenate([a_first, a_second, b_first, b_second]))
    moved = product(jnp.concatenate([high, high, low], axis=1), stacked[...])
    block = [moved[i * PACK:(i + 1) * PACK] for i in range(4)]
    plain, heavy = slice(0, rows), slice(rows, 2 * rows)
    projected = rhs[...] - block[0][:, plain]
    direction = first_part[...] - block[0][:, heavy] - block[2][:, plain]
    image = applied_first[...] - block[0][:, 2 * rows:3 * rows] - block[2][:, 3 * rows:]
    image_projected = image - block[1][:, plain]
    last = weight[...] * image - block[1][:, heavy] - block[3][:, plain]
    first[...] = direction
    applied[...] = image
    second[...] = last
    last_operand = sign_live[...] * last
    last_image = times_matrix(last_operand, schur[...])
    second_image[...] = last_image
    parts = [last_image[:, d * pair:(d + 1) * pair] for d in range(4)]
    for out, values in zip((to_a, to_b, to_c, to_d), by_swap(parts)):
        out[...] = values

    def folded(values):
        return sum(values[:, d * pair:(d + 1) * pair] for d in range(4))

    terms = jnp.concatenate([
        folded(0.5 * (projected * direction)),
        folded(0.5 * (direction * image)),
        folded(0.5 * (projected * last + image_projected * direction)),
        folded(0.5 * (image_projected * last)),
        folded(0.5 * (image * last)),
        folded(last_operand * last_image),
        jnp.zeros((128 - 6 * PACK, pair), F32),
    ])
    row = full_product_t(jnp.ones((STRIP, pair), F32), terms)[0:1]
    scalars[...] = jnp.broadcast_to(row[:, None, :], scalars.shape)


def far_kernel(pair, image, sign_live, tables, from_a, from_b, from_c, from_d, applied):
    arrived = by_direction([from_a[...], from_b[...], from_c[...], from_d[...]])
    for d in range(4):
        lanes = slice(d * pair, (d + 1) * pair)
        applied[:, lanes] = sign_live[:, lanes] * (image[:, lanes] - reorder(arrived[d], tables[d]))


def end_kernel(pair, scalars, rhs, first, applied, second, second_applied, multipliers, residual):
    total = jnp.sum(scalars[...], axis=0)
    rho_one, delta_one, cross, square, mixed, delta_last = [
        total if i == 0 else pltpu.roll(total, 128 - i * PACK, 1) for i in range(6)
    ]
    alpha_one = rho_one / delta_one
    rho_two = rho_one - alpha_one * cross + alpha_one * alpha_one * square
    grow = 1.0 + rho_two / rho_one
    delta_two = grow * grow * delta_one - 2.0 * grow * alpha_one * mixed + alpha_one * alpha_one * delta_last
    alpha_two = rho_two / delta_two
    eye = lax.broadcasted_iota(jnp.int32, (PACK, 128), 0) == lax.broadcasted_iota(jnp.int32, (PACK, 128), 1)

    def column(values):
        return jnp.sum(jnp.where(eye, values, 0.0), axis=1, keepdims=True)

    keep = column(alpha_one + alpha_two * grow)
    drop = column(alpha_two * alpha_one)
    new_multipliers = keep * first[...] - drop * second[...]
    new_residual = rhs[...] - keep * applied[...] + drop * second_applied[...]
    for d in range(4):
        lanes = slice(d * pair, (d + 1) * pair)
        multipliers[d] = new_multipliers[:, lanes]
        residual[d] = new_residual[:, lanes]


def call(kernel, outs, scratch, *args):
    return pl.pallas_call(
        kernel,
        out_shape=[jax.ShapeDtypeStruct(shape, dtype) for shape, dtype in outs],
        in_specs=[pl.BlockSpec(memory_space=pltpu.VMEM)] * len(args),
        out_specs=[pl.BlockSpec(memory_space=pltpu.VMEM)] * len(outs),
        scratch_shapes=[pltpu.VMEM(shape, dtype) for shape, dtype in scratch],
        compiler_params=pltpu.CompilerParams(vmem_limit_bytes=VMEM_LIMIT),
    )(*args)


def shards(schur, load, rigid, lengths, partner, coarse_inverse):
    own_load, own_rigid, matrix = load[0, 0], rigid[0, 0], schur[0, 0]
    cases, pair = own_load.shape[1:]
    modes = own_rigid.shape[1]
    clusters, subs = lax.axis_size("clus"), lax.axis_size("sub")
    devices = clusters * subs
    rows = 4 * pair
    width = clusters * STRIP
    lanes = max(width, 128)
    span = 3 * STRIP

    tables = (partner[0, 0][:, None, :] == lax.broadcasted_iota(jnp.int32, (4, pair, pair), 1)).astype(BF16)
    live = lax.broadcasted_iota(jnp.int32, (4, pair), 1) < lengths[0, 0][:, None]
    sign = jnp.array([-1.0, 1.0, -1.0, 1.0], F32)[:, None]
    sign_live = jnp.where(live, sign, 0.0).reshape(1, rows)
    wide_inverse = jnp.pad(
        coarse_inverse.reshape(clusters, modes, clusters, modes),
        ((0, 0), (0, STRIP - modes), (0, 0), (0, STRIP - modes)),
    ).reshape(width, width)

    flat = ((cases, rows), F32)
    *sent, diag_own = call(
        functools.partial(start_kernel, pair, modes),
        [((cases + STRIP, pair), F32)] * 4 + [((1, rows), F32)],
        [((4, cases + STRIP, pair), F32)],
        own_load, own_rigid, matrix,
    )
    arrived = swap(sent)

    packed, *sent, rhs, first_part, weight, basis, image = call(
        functools.partial(gram_kernel, pair, modes, devices),
        [((devices * PACK, 128), F32)] + [((2 * span + cases, pair), F32)] * 4
        + [flat, flat, ((1, rows), F32), ((2 * span, rows), F32), ((2 * span + cases, rows), F32)],
        [((2 * span + 2 * cases, rows), F32), ((128, rows), F32)],
        own_load, own_rigid, matrix, diag_own, sign_live, tables, *arrived,
    )
    gathered = lax.all_to_all(packed, AXES, 0, 0, tiled=True)
    arrived = swap(sent)
    stacked, applied_first = call(
        functools.partial(basis_kernel, pair, clusters),
        [((3 * width, 4 * rows), BF16), flat],
        [((width + 4 * STRIP, 4 * rows), F32)],
        basis, image, sign_live, tables, *arrived,
    )

    scalars, *sent, first, applied, second, second_image = call(
        functools.partial(solve_kernel, pair, modes, clusters, subs, cases),
        [((devices, 1, 128), F32)] + [((cases, pair), F32)] * 4 + [flat] * 4,
        [((2 * width, max(2 * width, 128)), F32), ((width, lanes), F32), ((PACK, max(2 * width, 128)), F32),
         ((2 * PACK, lanes), F32)],
        gathered, wide_inverse, stacked, rhs, first_part, applied_first, weight, sign_live, matrix,
    )
    gathered = lax.all_to_all(scalars, AXES, 0, 0, tiled=True)
    arrived = swap(sent)
    (second_applied,) = call(
        functools.partial(far_kernel, pair), [flat], [], second_image, sign_live, tables, *arrived
    )
    multipliers, residual = call(
        functools.partial(end_kernel, pair), [((4, cases, pair), F32)] * 2, [],
        gathered, rhs, first, applied, second, second_applied,
    )
    return (multipliers[None, None], residual[None, None])


def solution(mesh):
    in_specs = (
        P("clus", "sub", None, None),
        P("clus", "sub", None, None, None),
        P("clus", "sub", None, None, None),
        P("clus", "sub", None),
        P("clus", "sub", None, None),
        P(),
    )
    out_specs = (P("clus", "sub", None, None, None), P("clus", "sub", None, None, None))
    return jax.shard_map(shards, mesh=mesh, in_specs=in_specs, out_specs=out_specs, check_vma=False)
```

time: 303 us -> 39.9 us (0.13)
  blocking collectives: 198 us -> 0 us
  starting transfers between devices: 60.6 us -> 22.6 us
  waiting for transfers between devices: 25.8 us -> 7.71 us
  local copies, waits for them, and re-layouts: 8.86 us -> 2.71 us
  matrix products: 5.73 us -> 0 us
  Pallas kernels: 0 us -> 5.58 us
    psum x7 -> x0, blocking collectives: 157 us -> none  [the longest x3 117 us: inner_total(): return lax.psum(partial_value, ('clus', 'sub'))]
    ppermute x28 -> x12, starting transfers between devices: 60.6 us -> 15.9 us  [swap(): lax.ppermute(buffer, AXES, table)]
    all_gather x4 -> x0, blocking collectives: 40.7 us -> none  [coarse_reduce(): return lax.all_gather(within[None], 'clus', axis=0, tiled=True)]
    ppermute x28 -> x12, waiting for transfers between devices: 25.8 us -> 4.4 us  [swap(): lax.ppermute(buffer, AXES, table)]
    gather x1 -> x0, local copies, waits for them, and re-layouts: 8.24 us -> none  [shards(): diag_own = jnp.diagonal(matrix).astype(jnp.float32).reshape(4, 1, pair_rows)]
    all_to_all x0 -> x2, starting transfers between devices: none -> 6.78 us  [the longest x1 3.71 us: shards(): gathered = lax.all_to_all(packed, AXES, 0, 0, tiled=True)]
    dot_general x21 -> x0, matrix products: 5.73 us -> none  [the longest x7 2.99 us: partner_rows(): return jnp.einsum('djq,dkq->djk', values, table, precision=FULL_PRECISION)]
    pallas_call x0 -> x6, Pallas kernels: none -> 5.58 us  [call(): pl.pallas_call(kernel, out_shape=[jax.ShapeDtypeStruct(shape, dtype) for...]
  transfers between devices with their start and end apart: 28 -> 14, of which waited for: 7 -> 6; matrix products, arithmetic and copies ran while one was open for 0% -> 1% of each run, Pallas kernels for 0% -> 1%
where the time goes in v2:
time: 39.9 us; the launch traced here: 39.5 us
  starting transfers between devices  22.6 us (57%)
  waiting for transfers between devices  7.71 us (19%)
  Pallas kernels  5.58 us (14%)
  local copies, waits for them, and re-layouts  2.71 us (7%)
  between operations  0.74 us (2%)
    ppermute x12, starting transfers between devices, swap(): lax.ppermute(buffer, AXES, table)  15.9 us
    pallas_call x6, Pallas kernels, call(): pl.pallas_call(kernel, out_shape=[jax.ShapeDtypeStruct(shape, dtype) for...  5.58 us
    ppermute x12, waiting for transfers between devices, swap(): lax.ppermute(buffer, AXES, table)  4.4 us
    all_to_all x1, starting transfers between devices, shards(): gathered = lax.all_to_all(packed, AXES, 0, 0, tiled=True)  3.71 us
    all_to_all x1, starting transfers between devices, shards(): gathered = lax.all_to_all(scalars, AXES, 0, 0, tiled=True)  3.07 us
    all_to_all x1, waiting for transfers between devices, shards(): gathered = lax.all_to_all(packed, AXES, 0, 0, tiled=True)  2.81 us
    unnamed x15, local copies, waits for them, and re-layouts  2.46 us
  transfers between devices with their start and end apart: 14, of which 6 were waited for; matrix products, arithmetic and copies ran while one was open for 1% of the time, Pallas kernels for 1%

profile of v2, /device:TPU:0, one launch (start us, length us, event | category | flops | bytes accessed | tf_op | source)
XLA Modules:
  0.0 39.5 jit_solution(5097932710112249423)
XLA Ops:
  0.6 0.0 copy-start.2
  0.6 0.7 %copy.12 = f32[1,1,4,6,128]{4,3,2,1,0:T(8,128)S(1)} copy(f32[1,1,4,6,128]{4,2,3,1,0:T(4,128)} %param.9) | data formatting | bytes 24576 | tf_op args[2]
  1.4 0.0 copy-done.2
  1.4 1.0 %copy-done = bf16[1,1,512,512]{3,2,1,0:T(8,128)(2,1)S(1)} copy-done((bf16[1,1,512,512]{3,2,1,0:T(8,128)(2,1)S(1)}, bf16[1,1,512,512]{3,2,1,0:T(8,128)(2,1)}, u32[]{:S(2)}) %copy-start) | copy-done | bytes 524312
  2.4 0.1 shard_map.86
  2.5 3.1 %collective-permute-start = (f32[24,128]{1,0:T(8,128)S(1)}, f32[24,128]{1,0:T(8,128)S(1)}, u32[]{:S(2)}, u32[]{:S(2)}) collective-permute-start(f32[24,128]{1,0:T(8,128)S(1)} %get-tuple-element.31), channel_id=1, source_target_pairs={{0,1},{1,0},{2,3},{3,2},{4,5},{5,4},{6,7},{7,6},{8,9},{9,8},{10,11... | collective-permute-start | bytes 36872 | tf_op jit(solution)/shard_map/ppermute | solution.py:47
  5.6 0.0 collective-permute-start.1
  5.6 3.1 %collective-permute-start.2 = (f32[24,128]{1,0:T(8,128)S(1)}, f32[24,128]{1,0:T(8,128)S(1)}, u32[]{:S(2)}, u32[]{:S(2)}) collective-permute-start(f32[24,128]{1,0:T(8,128)S(1)} %get-tuple-element.33), channel_id=1, source_target_pairs={{0,1},{1,0},{2,3},{3,2},{4,8},{5,9},{6,10},{7,11},{8,4},{9,5},{10,... | collective-permute-start | bytes 36872 | tf_op jit(solution)/shard_map/ppermute | solution.py:47
  8.7 0.0 collective-permute-start.3
  8.7 0.0 copy-done.4
  8.8 0.0 copy-start.5
  8.8 0.0 copy-start.6
  8.8 0.6 %copy-done.5 = s32[1,1,4]{2,1,0:T(1,128)S(1)} copy-done((s32[1,1,4]{2,1,0:T(1,128)S(1)}, s32[1,1,4]{2,1,0:T(1,128)}, u32[]{:S(2)}) %copy-start.5) | copy-done | bytes 40
  9.4 0.0 copy-done.6
  9.4 0.1 fusion.1
  9.5 0.0 collective-permute-done.from_a
  9.5 0.0 collective-permute-done.1.from_b
  9.5 0.9 %collective-permute-done.2.from_c = f32[24,128]{1,0:T(8,128)S(1)} collective-permute-done((f32[24,128]{1,0:T(8,128)S(1)}, f32[24,128]{1,0:T(8,128)S(1)}, u32[]{:S(2)}, u32[]{:S(2)}) %collective-permute-start.2) | collective-permute-done | bytes 12320 | tf_op jit(solution)/shard_map/ppermute | solution.py:47
  10.4 0.0 collective-permute-done.3.from_d
  10.4 1.6 %shard_map.87 = (f32[512,128]{1,0:T(8,128)}, f32[64,128]{1,0:T(8,128)S(1)}, f32[64,128]{1,0:T(8,128)S(1)}, f32[64,128]{1,0:T(8,128)S(1)}, f32[64,128]{1,0:T(8,12...) custom-call(f32[4,16,128]{2,1,0:T(8,128)S(1)} %bitcast.21, ...), custom_call_target="tpu_custom_call" | custom-call | tf_op jit(solution)/shard_map/pallas_call | solution.py:382
  12.0 3.7 %all-to-all-start = ((f32[32,16,128]{2,1,0:T(8,128)}), f32[32,16,128]{2,1,0:T(8,128)S(1)}, u32[]{:S(2)}, u32[]{:S(2)}) async-start(f32[32,16,128]{2,1,0:T(8,128)} %bitcast.6), calls=%async_computation | async-start | bytes 524288 | tf_op jit(solution)/shard_map/all_to_all | solution.py:428
  15.8 1.8 %collective-permute-start.4 = (f32[64,128]{1,0:T(8,128)S(1)}, f32[64,128]{1,0:T(8,128)S(1)}, u32[]{:S(2)}, u32[]{:S(2)}) collective-permute-start(f32[64,128]{1,0:T(8,128)S(1)} %get-tuple-element.38), channel_id=1, source_target_pairs={{0,1},{1,0},{2,3},{3,2},{4,5},{5,4},{6,7},{7,6},{8,9},{9,8},{10,11... | collective-permute-start | bytes 98312 | tf_op jit(solution)/shard_map/ppermute | solution.py:47
  17.6 0.0 collective-permute-start.5
  17.6 3.0 %collective-permute-start.6 = (f32[64,128]{1,0:T(8,128)S(1)}, f32[64,128]{1,0:T(8,128)S(1)}, u32[]{:S(2)}, u32[]{:S(2)}) collective-permute-start(f32[64,128]{1,0:T(8,128)S(1)} %get-tuple-element.40), channel_id=1, source_target_pairs={{0,1},{1,0},{2,3},{3,2},{4,8},{5,9},{6,10},{7,11},{8,4},{9,5},{10,... | collective-permute-start | bytes 98312 | tf_op jit(solution)/shard_map/ppermute | solution.py:47
  20.6 0.0 collective-permute-start.7
  20.6 0.0 copy-done.3
  20.6 0.1 reshape.52
  20.7 0.0 copy-start.1
  20.7 0.1 reshape.53.inverse
  20.9 1.1 %collective-permute-done.4.from_a = f32[64,128]{1,0:T(8,128)S(1)} collective-permute-done((f32[64,128]{1,0:T(8,128)S(1)}, f32[64,128]{1,0:T(8,128)S(1)}, u32[]{:S(2)}, u32[]{:S(2)}) %collective-permute-start.4) | collective-permute-done | bytes 32800 | tf_op jit(solution)/shard_map/ppermute | solution.py:47
  21.9 0.0 collective-permute-done.5.from_b
  21.9 0.8 %collective-permute-done.6.from_c = f32[64,128]{1,0:T(8,128)S(1)} collective-permute-done((f32[64,128]{1,0:T(8,128)S(1)}, f32[64,128]{1,0:T(8,128)S(1)}, u32[]{:S(2)}, u32[]{:S(2)}) %collective-permute-start.6) | collective-permute-done | bytes 32800 | tf_op jit(solution)/shard_map/ppermute | solution.py:47
  22.8 0.0 collective-permute-done.7.from_d
  22.8 0.4 shard_map.88
  23.1 2.8 %all-to-all-done = f32[32,16,128]{2,1,0:T(8,128)S(1)} async-done(((f32[32,16,128]{2,1,0:T(8,128)}), f32[32,16,128]{2,1,0:T(8,128)S(1)}, u32[]{:S(2)}, u32[]{:S(2)}) %all-to-all-start) | async-done | bytes 262176 | tf_op jit(solution)/shard_map/all_to_all | solution.py:428
  26.0 2.5 %shard_map.89 = (f32[32,1,128]{2,1,0:T(1,128)}, f32[16,128]{1,0:T(8,128)S(1)}, f32[16,128]{1,0:T(8,128)S(1)}, f32[16,128]{1,0:T(8,128)S(1)}, f32[16,128]{1,0:T(8...) custom-call(f32[512,128]{1,0:T(8,128)S(1)} %bitcast.17, ...), custom_call_target="tpu_custom_call" | custom-call | tf_op jit(solution)/shard_map/pallas_call | solution.py:382
  28.5 3.1 %all-to-all-start.1 = ((f32[32,1,128]{2,1,0:T(1,128)}), f32[32,1,128]{2,1,0:T(1,128)S(1)}, u32[]{:S(2)}, u32[]{:S(2)}) async-start(f32[32,1,128]{2,1,0:T(1,128)} %get-tuple-element.47), calls=%async_computation.1 | async-start | bytes 32768 | tf_op jit(solution)/shard_map/all_to_all | solution.py:444
  31.6 1.8 %collective-permute-start.8 = (f32[16,128]{1,0:T(8,128)S(1)}, f32[16,128]{1,0:T(8,128)S(1)}, u32[]{:S(2)}, u32[]{:S(2)}) collective-permute-start(f32[16,128]{1,0:T(8,128)S(1)} %get-tuple-element.52), channel_id=1, source_target_pairs={{0,1},{1,0},{2,3},{3,2},{4,5},{5,4},{6,7},{7,6},{8,9},{9,8},{10,11... | collective-permute-start | bytes 24584 | tf_op jit(solution)/shard_map/ppermute | solution.py:47
  33.4 0.0 collective-permute-start.9
  33.4 3.0 %collective-permute-start.10 = (f32[16,128]{1,0:T(8,128)S(1)}, f32[16,128]{1,0:T(8,128)S(1)}, u32[]{:S(2)}, u32[]{:S(2)}) collective-permute-start(f32[16,128]{1,0:T(8,128)S(1)} %get-tuple-element.54), channel_id=1, source_target_pairs={{0,1},{1,0},{2,3},{3,2},{4,8},{5,9},{6,10},{7,11},{8,4},{9,5},{10,... | collective-permute-start | bytes 24584 | tf_op jit(solution)/shard_map/ppermute | solution.py:47
  36.4 0.0 collective-permute-start.11
  36.4 0.0 collective-permute-done.8.from_a
  36.4 0.0 collective-permute-done.9.from_b
  36.4 1.6 %collective-permute-done.10.from_c = f32[16,128]{1,0:T(8,128)S(1)} collective-permute-done((f32[16,128]{1,0:T(8,128)S(1)}, f32[16,128]{1,0:T(8,128)S(1)}, u32[]{:S(2)}, u32[]{:S(2)}) %collective-permute-start.10) | collective-permute-done | bytes 8224 | tf_op jit(solution)/shard_map/ppermute | solution.py:47
  38.0 0.0 collective-permute-done.11.from_d
  38.0 0.2 shard_map.90.second_applied
  38.2 0.5 %all-to-all-done.1.scalars = f32[32,1,128]{2,1,0:T(1,128)S(1)} async-done(((f32[32,1,128]{2,1,0:T(1,128)}), f32[32,1,128]{2,1,0:T(1,128)S(1)}, u32[]{:S(2)}, u32[]{:S(2)}) %all-to-all-start.1) | async-done | bytes 16416 | tf_op jit(solution)/shard_map/all_to_all | solution.py:444
  38.7 0.8 %shard_map.91 = (f32[4,16,128]{2,1,0:T(8,128)}, f32[4,16,128]{2,1,0:T(8,128)}) custom-call(f32[32,1,128]{2,1,0:T(1,128)S(1)} %all-to-all-done.1.scalars, f32[16,512]{1,0:T(8,128)S(1)} %get-tuple-element.43.rhs, f32[16,512]{1,0:T(8,128)S(1)} %get-tuple-element.48.first, f32[16,512]{1,0:T(8,128)S(1)} %get-tuple-element.49.applied, ...), custom_call_target="tpu_custom_call" | custom-call | tf_op jit(solution)/shard_map/pallas_call | solution.py:382
  (6 shorter events, 0.1 us)
Async XLA Ops:
  0.6 0.8 %copy-start.2 = (f32[1,1,4,16,128]{4,3,2,1,0:T(8,128)S(1)}, f32[1,1,4,16,128]{4,3,2,1,0:T(8,128)}, u32[]{:S(2)}) copy-start(f32[1,1,4,16,128]{4,3,2,1,0:T(8,128)} %param.8) | copy-start | bytes 98308
  1.4 1.0 %copy-start = (bf16[1,1,512,512]{3,2,1,0:T(8,128)(2,1)S(1)}, bf16[1,1,512,512]{3,2,1,0:T(8,128)(2,1)}, u32[]{:S(2)}) copy-start(bf16[1,1,512,512]{3,2,1,0:T(8,128)(2,1)} %param.7) | copy-start | bytes 1572868
  2.5 7.0 %collective-permute-start = (f32[24,128]{1,0:T(8,128)S(1)}, f32[24,128]{1,0:T(8,128)S(1)}, u32[]{:S(2)}, u32[]{:S(2)}) collective-permute-start(f32[24,128]{1,0:T(8,128)S(1)} %get-tuple-element.31), channel_id=1, source_target_pairs={{0,1},{1,0},{2,3},{3,2},{4,5},{5,4},{6,7},{7,6},{8,9},{9,8},{10,11... | collective-permute-start | bytes 36872 | tf_op jit(solution)/shard_map/ppermute | solution.py:47
  5.6 3.9 %collective-permute-start.1 = (f32[24,128]{1,0:T(8,128)S(1)}, f32[24,128]{1,0:T(8,128)S(1)}, u32[]{:S(2)}, u32[]{:S(2)}) collective-permute-start(f32[24,128]{1,0:T(8,128)S(1)} %get-tuple-element.32), channel_id=1, source_target_pairs={{0,4},{1,2},{2,1},{3,7},{4,0},{5,6},{6,5},{7,3},{8,12},{9,10},{10,... | collective-permute-start | bytes 36872 | tf_op jit(solution)/shard_map/ppermute | solution.py:47
  5.6 3.2 %copy-start.4 = (s32[1,1,4,128]{3,2,1,0:T(4,128)S(1)}, s32[1,1,4,128]{3,2,1,0:T(4,128)}, u32[]{:S(2)}) copy-start(s32[1,1,4,128]{3,2,1,0:T(4,128)} %param.11) | copy-start | bytes 6148
  5.6 4.8 %collective-permute-start.2 = (f32[24,128]{1,0:T(8,128)S(1)}, f32[24,128]{1,0:T(8,128)S(1)}, u32[]{:S(2)}, u32[]{:S(2)}) collective-permute-start(f32[24,128]{1,0:T(8,128)S(1)} %get-tuple-element.33), channel_id=1, source_target_pairs={{0,1},{1,0},{2,3},{3,2},{4,8},{5,9},{6,10},{7,11},{8,4},{9,5},{10,... | collective-permute-start | bytes 36872 | tf_op jit(solution)/shard_map/ppermute | solution.py:47
  8.7 1.7 %collective-permute-start.3 = (f32[24,128]{1,0:T(8,128)S(1)}, f32[24,128]{1,0:T(8,128)S(1)}, u32[]{:S(2)}, u32[]{:S(2)}) collective-permute-start(f32[24,128]{1,0:T(8,128)S(1)} %get-tuple-element.34), channel_id=1, source_target_pairs={{0,4},{1,5},{2,6},{3,7},{4,0},{5,1},{6,2},{7,3},{8,12},{9,13},{10,... | collective-permute-start | bytes 36872 | tf_op jit(solution)/shard_map/ppermute | solution.py:47
  8.8 0.7 %copy-start.5 = (s32[1,1,4]{2,1,0:T(1,128)S(1)}, s32[1,1,4]{2,1,0:T(1,128)}, u32[]{:S(2)}) copy-start(s32[1,1,4]{2,1,0:T(1,128)} %param.10) | copy-start | bytes 52
  8.8 0.7 %copy-start.6 = (f32[4]{0:T(128)S(1)}, f32[4]{0:T(128)}, u32[]{:S(2)}) copy-start(f32[4]{0:T(128)} %constant.6.clone) | copy-start | bytes 52
  12.0 8.5 %copy-start.3 = (f32[48,48]{1,0:T(8,128)S(1)}, f32[48,48]{1,0:T(8,128)}, u32[]{:S(2)}) copy-start(f32[48,48]{1,0:T(8,128)} %param.12) | copy-start | bytes 27652
  12.0 13.9 %all-to-all-start = ((f32[32,16,128]{2,1,0:T(8,128)}), f32[32,16,128]{2,1,0:T(8,128)S(1)}, u32[]{:S(2)}, u32[]{:S(2)}) async-start(f32[32,16,128]{2,1,0:T(8,128)} %bitcast.6), calls=%async_computation | async-start | bytes 524288 | tf_op jit(solution)/shard_map/all_to_all | solution.py:428
  15.8 6.2 %collective-permute-start.4 = (f32[64,128]{1,0:T(8,128)S(1)}, f32[64,128]{1,0:T(8,128)S(1)}, u32[]{:S(2)}, u32[]{:S(2)}) collective-permute-start(f32[64,128]{1,0:T(8,128)S(1)} %get-tuple-element.38), channel_id=1, source_target_pairs={{0,1},{1,0},{2,3},{3,2},{4,5},{5,4},{6,7},{7,6},{8,9},{9,8},{10,11... | collective-permute-start | bytes 98312 | tf_op jit(solution)/shard_map/ppermute | solution.py:47
  17.6 4.4 %collective-permute-start.5 = (f32[64,128]{1,0:T(8,128)S(1)}, f32[64,128]{1,0:T(8,128)S(1)}, u32[]{:S(2)}, u32[]{:S(2)}) collective-permute-start(f32[64,128]{1,0:T(8,128)S(1)} %get-tuple-element.39), channel_id=1, source_target_pairs={{0,4},{1,2},{2,1},{3,7},{4,0},{5,6},{6,5},{7,3},{8,12},{9,10},{10,... | collective-permute-start | bytes 98312 | tf_op jit(solution)/shard_map/ppermute | solution.py:47
  17.6 5.2 %collective-permute-start.6 = (f32[64,128]{1,0:T(8,128)S(1)}, f32[64,128]{1,0:T(8,128)S(1)}, u32[]{:S(2)}, u32[]{:S(2)}) collective-permute-start(f32[64,128]{1,0:T(8,128)S(1)} %get-tuple-element.40), channel_id=1, source_target_pairs={{0,1},{1,0},{2,3},{3,2},{4,8},{5,9},{6,10},{7,11},{8,4},{9,5},{10,... | collective-permute-start | bytes 98312 | tf_op jit(solution)/shard_map/ppermute | solution.py:47
  20.6 2.2 %collective-permute-start.7 = (f32[64,128]{1,0:T(8,128)S(1)}, f32[64,128]{1,0:T(8,128)S(1)}, u32[]{:S(2)}, u32[]{:S(2)}) collective-permute-start(f32[64,128]{1,0:T(8,128)S(1)} %get-tuple-element.41), channel_id=1, source_target_pairs={{0,4},{1,5},{2,6},{3,7},{4,0},{5,1},{6,2},{7,3},{8,12},{9,13},{10,... | collective-permute-start | bytes 98312 | tf_op jit(solution)/shard_map/ppermute | solution.py:47
  20.7 5.3 %copy-start.1 = (bf16[1,1,512,512]{3,2,1,0:T(8,128)(2,1)S(1)}, bf16[1,1,512,512]{3,2,1,0:T(8,128)(2,1)}, u32[]{:S(2)}) copy-start(bf16[1,1,512,512]{3,2,1,0:T(8,128)(2,1)} %param.7) | copy-start | bytes 1572868
  28.5 10.2 %all-to-all-start.1 = ((f32[32,1,128]{2,1,0:T(1,128)}), f32[32,1,128]{2,1,0:T(1,128)S(1)}, u32[]{:S(2)}, u32[]{:S(2)}) async-start(f32[32,1,128]{2,1,0:T(1,128)} %get-tuple-element.47), calls=%async_computation.1 | async-start | bytes 32768 | tf_op jit(solution)/shard_map/all_to_all | solution.py:444
  31.6 4.8 %collective-permute-start.8 = (f32[16,128]{1,0:T(8,128)S(1)}, f32[16,128]{1,0:T(8,128)S(1)}, u32[]{:S(2)}, u32[]{:S(2)}) collective-permute-start(f32[16,128]{1,0:T(8,128)S(1)} %get-tuple-element.52), channel_id=1, source_target_pairs={{0,1},{1,0},{2,3},{3,2},{4,5},{5,4},{6,7},{7,6},{8,9},{9,8},{10,11... | collective-permute-start | bytes 24584 | tf_op jit(solution)/shard_map/ppermute | solution.py:47
  33.4 3.0 %collective-permute-start.9 = (f32[16,128]{1,0:T(8,128)S(1)}, f32[16,128]{1,0:T(8,128)S(1)}, u32[]{:S(2)}, u32[]{:S(2)}) collective-permute-start(f32[16,128]{1,0:T(8,128)S(1)} %get-tuple-element.53), channel_id=1, source_target_pairs={{0,4},{1,2},{2,1},{3,7},{4,0},{5,6},{6,5},{7,3},{8,12},{9,10},{10,... | collective-permute-start | bytes 24584 | tf_op jit(solution)/shard_map/ppermute | solution.py:47
  33.4 4.6 %collective-permute-start.10 = (f32[16,128]{1,0:T(8,128)S(1)}, f32[16,128]{1,0:T(8,128)S(1)}, u32[]{:S(2)}, u32[]{:S(2)}) collective-permute-start(f32[16,128]{1,0:T(8,128)S(1)} %get-tuple-element.54), channel_id=1, source_target_pairs={{0,1},{1,0},{2,3},{3,2},{4,8},{5,9},{6,10},{7,11},{8,4},{9,5},{10,... | collective-permute-start | bytes 24584 | tf_op jit(solution)/shard_map/ppermute | solution.py:47
  36.4 1.6 %collective-permute-start.11 = (f32[16,128]{1,0:T(8,128)S(1)}, f32[16,128]{1,0:T(8,128)S(1)}, u32[]{:S(2)}, u32[]{:S(2)}) collective-permute-start(f32[16,128]{1,0:T(8,128)S(1)} %get-tuple-element.55), channel_id=1, source_target_pairs={{0,4},{1,5},{2,6},{3,7},{4,0},{5,1},{6,2},{7,3},{8,12},{9,13},{10,... | collective-permute-start | bytes 24584 | tf_op jit(solution)/shard_map/ppermute | solution.py:47

commit v3 on v2

--- a/solution.py
+++ b/solution.py
@@ -105,23 +105,36 @@
     return both[:count] + both[count:]
 
 
-def start_kernel(pair, modes, load, rigid, schur, to_a, to_b, to_c, to_d, diag_out, buffer):
+def start_kernel(
+    pair, modes, load_hbm, rigid_hbm, schur_hbm, to_a, to_b, to_c, to_d, diag_out, load, rigid, buffer, blocks, arrivals
+):
     cases = load.shape[1]
+    copies = [
+        pltpu.make_async_copy(load_hbm, load, arrivals.at[0]),
+        pltpu.make_async_copy(rigid_hbm, rigid, arrivals.at[1]),
+    ]
+    for d in range(4):
+        span = slice(d * pair, (d + 1) * pair)
+        copies.append(pltpu.make_async_copy(schur_hbm.at[span, span], blocks.at[d], arrivals.at[2 + d]))
+    for copy in copies:
+        copy.start()
     eye = lax.broadcasted_iota(jnp.int32, (pair, pair), 0) == lax.broadcasted_iota(jnp.int32, (pair, pair), 1)
     buffer[...] = jnp.zeros_like(buffer)
+    for copy in copies:
+        copy.wait()
     for d in range(4):
         span = slice(d * pair, (d + 1) * pair)
-        diag = jnp.sum(jnp.where(eye, schur[span, span].astype(F32), 0.0), axis=0, keepdims=True)
+        diag = jnp.sum(jnp.where(eye, blocks[d].astype(F32), 0.0), axis=0, keepdims=True)
         diag_out[:, span] = diag
         buffer[d, 0:cases] = load[d]
-        buffer[d, cases:cases + modes] = rigid[d]
+        buffer[d, cases:cases + modes] = rigid[:, d]
         buffer[d, cases + STRIP - 1:cases + STRIP] = diag
     for out, values in zip((to_a, to_b, to_c, to_d), by_swap([buffer[d] for d in range(4)])):
         out[...] = values
 
 
 def gram_kernel(
-    pair, modes, devices, load, rigid, schur, diag_own, sign_live, tables, from_a, from_b, from_c, from_d,
+    pair, modes, clusters, subs, load, rigid, schur, diag_own, sign_live, tables, from_a, from_b, from_c, from_d,
     packed, to_a, to_b, to_c, to_d, rhs, first, weight, basis, image, operand, right
 ):
     cases = load.shape[1]
@@ -134,7 +147,7 @@
         sign = sign_live[:, lanes]
         distant = reorder(arrived[d], tables[d])
         distant_rigid = distant[cases:cases + modes]
-        own_rigid = rigid[d]
+        own_rigid = rigid[:, d]
         both = diag_own[:, lanes] + distant[cases + STRIP - 1:cases + STRIP]
         is_live = sign != 0.0
         inverse = jnp.where(is_live, 1.0 / jnp.where(is_live, both, 1.0), 0.0)
@@ -178,11 +191,9 @@
     total = jnp.where(lane >= at, pltpu.roll(with_first, at, 1), total)
     total = jnp.where(lane >= at + 7 * modes, pltpu.roll(with_rhs, at + modes, 1), total)
 
-    def spread(i, carry):
-        packed[pl.ds(pl.multiple_of(i * PACK, PACK), PACK)] = total
-        return carry
-
-    lax.fori_loop(0, devices, spread, 0, unroll=min(devices, 32))
+    halves_out = [jnp.concatenate([total[h * STRIP:(h + 1) * STRIP]] * subs) for h in range(2)]
+    for c in range(clusters):
+        packed[c * subs * STRIP:(c + 1) * subs * STRIP] = halves_out[c % 2]
     parts = [image[:, d * pair:(d + 1) * pair] for d in range(4)]
     for out, values in zip((to_a, to_b, to_c, to_d), by_swap(parts)):
         out[...] = values
@@ -227,7 +238,7 @@
     stacked[2 * width:3 * width] = high
 
 
-def unpack(sums, modes, clusters, cases):
+def unpack(strips, modes, clusters):
     width = clusters * STRIP
     lane = lax.broadcasted_iota(jnp.int32, (PACK, 128), 1)
     upper, coupling, with_first, tails = {}, {}, {}, {}
@@ -246,8 +257,9 @@
         return other, (h // 3) * width + other * STRIP
 
     for c in range(clusters):
+        whole = jnp.concatenate(strips[c])
         for half, row in enumerate(pack_places(modes)):
-            values = sums[c][half * STRIP:(half + 1) * STRIP]
+            values = strips[c][half]
             for g, begin, end, at in row:
                 row_cluster, row_at = group(c, g)
                 if not 0 <= row_cluster < clusters:
@@ -263,26 +275,25 @@
         for h in range(6):
             other, column = group(c, h)
             if 0 <= other < clusters:
-                put(with_first, (), sums[c], 12 * modes + h * modes, column)
-        put(tails, (0,), sums[c], 19 * modes, c * STRIP)
-        put(tails, (1,), sums[c], 18 * modes, c * STRIP)
+                put(with_first, (), whole, 12 * modes + h * modes, column)
+        put(tails, (0,), whole, 19 * modes, c * STRIP)
+        put(tails, (1,), whole, 18 * modes, c * STRIP)
     return upper, coupling, with_first, tails
 
 
 def solve_kernel(
-    pair, modes, clusters, subs, cases, gathered, inverse, stacked, rhs, first_part, applied_first, weight, sign_live,
+    pair, modes, clusters, mine, other, inverse, stacked, rhs, first_part, applied_first, weight, sign_live,
     schur, scalars, to_a, to_b, to_c, to_d, first, applied, second, second_image, upper_ref, couple_ref, row_ref,
     tail_ref
 ):
     width = clusters * STRIP
     rows = 4 * pair
-    sums = []
+    even_c, _ = parities()
+    strips = []
     for c in range(clusters):
-        total = gathered[c * subs * PACK:(c * subs + 1) * PACK]
-        for s in range(1, subs):
-            total = total + gathered[(c * subs + s) * PACK:(c * subs + s + 1) * PACK]
-        sums.append(total)
-    upper, coupling, with_first, tails = unpack(sums, modes, clusters, cases)
+        span = slice(c * STRIP, (c + 1) * STRIP)
+        strips.append((jnp.where(even_c, mine[span], other[span]), jnp.where(even_c, other[span], mine[span])))
+    upper, coupling, with_first, tails = unpack(strips, modes, clusters)
 
     def fill(ref, store, height):
         for i in range(ref.shape[0] // height):
@@ -378,21 +389,22 @@
         residual[d] = new_residual[:, lanes]
 
 
-def call(kernel, outs, scratch, *args):
+def call(kernel, outs, scratch, *args, place=pltpu.VMEM):
     return pl.pallas_call(
         kernel,
         out_shape=[jax.ShapeDtypeStruct(shape, dtype) for shape, dtype in outs],
-        in_specs=[pl.BlockSpec(memory_space=pltpu.VMEM)] * len(args),
+        in_specs=[pl.BlockSpec(memory_space=place)] * len(args),
         out_specs=[pl.BlockSpec(memory_space=pltpu.VMEM)] * len(outs),
-        scratch_shapes=[pltpu.VMEM(shape, dtype) for shape, dtype in scratch],
+        scratch_shapes=scratch,
         compiler_params=pltpu.CompilerParams(vmem_limit_bytes=VMEM_LIMIT),
     )(*args)
 
 
 def shards(schur, load, rigid, lengths, partner, coarse_inverse):
-    own_load, own_rigid, matrix = load[0, 0], rigid[0, 0], schur[0, 0]
+    own_load, matrix = load[0, 0], schur[0, 0]
+    own_rigid = jnp.swapaxes(rigid[0, 0], 0, 1)
     cases, pair = own_load.shape[1:]
-    modes = own_rigid.shape[1]
+    modes = own_rigid.shape[0]
     clusters, subs = lax.axis_size("clus"), lax.axis_size("sub")
     devices = clusters * subs
     rows = 4 * pair
@@ -410,19 +422,19 @@
     ).reshape(width, width)
 
     flat = ((cases, rows), F32)
-    *sent, diag_own = call(
+    *sent, diag_own, own_load, own_rigid = call(
         functools.partial(start_kernel, pair, modes),
-        [((cases + STRIP, pair), F32)] * 4 + [((1, rows), F32)],
-        [((4, cases + STRIP, pair), F32)],
-        own_load, own_rigid, matrix,
+        [((cases + STRIP, pair), F32)] * 4 + [((1, rows), F32), (own_load.shape, F32), (own_rigid.shape, F32)],
+        [pltpu.VMEM((4, cases + STRIP, pair), F32), pltpu.VMEM((4, pair, pair), BF16), pltpu.SemaphoreType.DMA((6,))],
+        own_load, own_rigid, matrix, place=pltpu.HBM,
     )
     arrived = swap(sent)
 
     packed, *sent, rhs, first_part, weight, basis, image = call(
-        functools.partial(gram_kernel, pair, modes, devices),
-        [((devices * PACK, 128), F32)] + [((2 * span + cases, pair), F32)] * 4
+        functools.partial(gram_kernel, pair, modes, clusters, subs),
+        [((devices * STRIP, 128), F32)] + [((2 * span + cases, pair), F32)] * 4
         + [flat, flat, ((1, rows), F32), ((2 * span, rows), F32), ((2 * span + cases, rows), F32)],
-        [((2 * span + 2 * cases, rows), F32), ((128, rows), F32)],
+        [pltpu.VMEM((2 * span + 2 * cases, rows), F32), pltpu.VMEM((128, rows), F32)],
         own_load, own_rigid, matrix, diag_own, sign_live, tables, *arrived,
     )
     gathered = lax.all_to_all(packed, AXES, 0, 0, tiled=True)
@@ -430,16 +442,18 @@
     stacked, applied_first = call(
         functools.partial(basis_kernel, pair, clusters),
         [((3 * width, 4 * rows), BF16), flat],
-        [((width + 4 * STRIP, 4 * rows), F32)],
+        [pltpu.VMEM((width + 4 * STRIP, 4 * rows), F32)],
         basis, image, sign_live, tables, *arrived,
     )
 
+    mine = jnp.sum(gathered.reshape(clusters, subs, STRIP, 128), axis=1).reshape(width, 128)
+    other = lax.ppermute(mine, AXES, swap_tables(clusters, subs)[3])
     scalars, *sent, first, applied, second, second_image = call(
-        functools.partial(solve_kernel, pair, modes, clusters, subs, cases),
+        functools.partial(solve_kernel, pair, modes, clusters),
         [((devices, 1, 128), F32)] + [((cases, pair), F32)] * 4 + [flat] * 4,
-        [((2 * width, max(2 * width, 128)), F32), ((width, lanes), F32), ((PACK, max(2 * width, 128)), F32),
-         ((2 * PACK, lanes), F32)],
-        gathered, wide_inverse, stacked, rhs, first_part, applied_first, weight, sign_live, matrix,
+        [pltpu.VMEM(shape, F32) for shape in
+         ((2 * width, max(2 * width, 128)), (width, lanes), (PACK, max(2 * width, 128)), (2 * PACK, lanes))],
+        mine, other, wide_inverse, stacked, rhs, first_part, applied_first, weight, sign_live, matrix,
     )
     gathered = lax.all_to_all(scalars, AXES, 0, 0, tiled=True)
     arrived = swap(sent)

time: 39.9 us -> 39.9 us (level)
  local copies, waits for them, and re-layouts: 2.71 us -> 3.42 us
  waiting for transfers between devices: 7.71 us -> 7.3 us
  starting transfers between devices: 22.6 us -> 22.2 us
    ppermute x12, waiting for transfers between devices: 4.4 us -> 2.52 us  [swap(): lax.ppermute(buffer, AXES, table)]
    all_to_all x1, waiting for transfers between devices: 2.81 us -> 3.8 us  [shards(): gathered = lax.all_to_all(packed, AXES, 0, 0, tiled=True)]
    unnamed x15 -> x16, local copies, waits for them, and re-layouts: 2.46 us -> 3.17 us
    all_to_all x1, starting transfers between devices: 3.07 us -> 2.54 us  [shards(): gathered = lax.all_to_all(scalars, AXES, 0, 0, tiled=True)]
    ppermute x0 -> x1, waiting for transfers between devices: none -> 0.48 us  [shards(): other = lax.ppermute(mine, AXES, swap_tables(clusters, subs)[3])]
  transfers between devices with their start and end apart: 14 -> 15, of which waited for: 6 -> 5; matrix products, arithmetic and copies ran while one was open for 1% -> 1% of each run, Pallas kernels for 1% -> 1%
where the time goes in v3:
time: 39.9 us; the launch traced here: 39.5 us
  starting transfers between devices  22.2 us (56%)
  waiting for transfers between devices  7.3 us (18%)
  Pallas kernels  5.68 us (14%)
  local copies, waits for them, and re-layouts  3.42 us (9%)
  between operations  0.79 us (2%)
    ppermute x12, starting transfers between devices, swap(): lax.ppermute(buffer, AXES, table)  15.9 us
    pallas_call x6, Pallas kernels, call(): pl.pallas_call(kernel, out_shape=[jax.ShapeDtypeStruct(shape, dtype) for...  5.68 us
    all_to_all x1, waiting for transfers between devices, shards(): gathered = lax.all_to_all(packed, AXES, 0, 0, tiled=True)  3.8 us
    all_to_all x1, starting transfers between devices, shards(): gathered = lax.all_to_all(packed, AXES, 0, 0, tiled=True)  3.72 us
    unnamed x16, local copies, waits for them, and re-layouts  3.17 us
    all_to_all x1, starting transfers between devices, shards(): gathered = lax.all_to_all(scalars, AXES, 0, 0, tiled=True)  2.54 us
    ppermute x12, waiting for transfers between devices, swap(): lax.ppermute(buffer, AXES, table)  2.52 us
  transfers between devices with their start and end apart: 15, of which 5 were waited for; matrix products, arithmetic and copies ran while one was open for 1% of the time, Pallas kernels for 1%

profile of v3, /device:TPU:0, one launch (start us, length us, event | category | flops | bytes accessed | tf_op | source)
XLA Modules:
  0.0 39.5 jit_solution(11001114621563500850)
XLA Ops:
  0.6 0.0 copy-start
  0.6 1.0 %copy-done = bf16[1,1,512,512]{3,2,1,0:T(8,128)(2,1)S(1)} copy-done((bf16[1,1,512,512]{3,2,1,0:T(8,128)(2,1)S(1)}, bf16[1,1,512,512]{3,2,1,0:T(8,128)(2,1)}, u32[]{:S(2)}) %copy-start) | copy-done | bytes 524312
  1.7 0.8 %copy-done.2 = f32[1,1,4,16,128]{4,3,2,1,0:T(8,128)S(1)} copy-done((f32[1,1,4,16,128]{4,3,2,1,0:T(8,128)S(1)}, f32[1,1,4,16,128]{4,3,2,1,0:T(8,128)}, u32[]{:S(2)}) %copy-start.2) | copy-done | bytes 32792
  2.4 0.7 %copy-done.3 = f32[1,1,4,6,128]{4,2,3,1,0:T(4,128)S(1)} copy-done((f32[1,1,4,6,128]{4,2,3,1,0:T(4,128)S(1)}, f32[1,1,4,6,128]{4,2,3,1,0:T(4,128)}, u32[]{:S(2)}) %copy-start.3) | copy-done | bytes 12312
  3.1 0.2 shard_map.86
  3.3 3.1 %collective-permute-start = (f32[24,128]{1,0:T(8,128)S(1)}, f32[24,128]{1,0:T(8,128)S(1)}, u32[]{:S(2)}, u32[]{:S(2)}) collective-permute-start(f32[24,128]{1,0:T(8,128)S(1)} %get-tuple-element.35), channel_id=1, source_target_pairs={{0,1},{1,0},{2,3},{3,2},{4,5},{5,4},{6,7},{7,6},{8,9},{9,8},{10,11... | collective-permute-start | bytes 36872 | tf_op jit(solution)/shard_map/ppermute | solution.py:47
  6.4 0.0 collective-permute-start.1
  6.4 3.1 %collective-permute-start.2 = (f32[24,128]{1,0:T(8,128)S(1)}, f32[24,128]{1,0:T(8,128)S(1)}, u32[]{:S(2)}, u32[]{:S(2)}) collective-permute-start(f32[24,128]{1,0:T(8,128)S(1)} %get-tuple-element.37), channel_id=1, source_target_pairs={{0,1},{1,0},{2,3},{3,2},{4,8},{5,9},{6,10},{7,11},{8,4},{9,5},{10,... | collective-permute-start | bytes 36872 | tf_op jit(solution)/shard_map/ppermute | solution.py:47
  9.6 0.0 collective-permute-start.3
  9.6 0.0 copy-done.5
  9.6 0.0 copy-start.6
  9.6 0.0 copy-start.7
  9.6 0.6 %copy-done.6 = s32[1,1,4]{2,1,0:T(1,128)S(1)} copy-done((s32[1,1,4]{2,1,0:T(1,128)S(1)}, s32[1,1,4]{2,1,0:T(1,128)}, u32[]{:S(2)}) %copy-start.6) | copy-done | bytes 40
  10.3 0.0 copy-done.7
  10.3 0.1 fusion.1
  10.4 0.0 collective-permute-done.from_a
  10.4 0.0 collective-permute-done.1.from_b
  10.4 0.9 %collective-permute-done.2.from_c = f32[24,128]{1,0:T(8,128)S(1)} collective-permute-done((f32[24,128]{1,0:T(8,128)S(1)}, f32[24,128]{1,0:T(8,128)S(1)}, u32[]{:S(2)}, u32[]{:S(2)}) %collective-permute-start.2) | collective-permute-done | bytes 12320 | tf_op jit(solution)/shard_map/ppermute | solution.py:47
  11.3 0.0 collective-permute-done.3.from_d
  11.3 1.6 %shard_map.87 = (f32[256,128]{1,0:T(8,128)}, f32[64,128]{1,0:T(8,128)S(1)}, f32[64,128]{1,0:T(8,128)S(1)}, f32[64,128]{1,0:T(8,128)S(1)}, f32[64,128]{1,0:T(8,12...) custom-call(f32[4,16,128]{2,1,0:T(8,128)S(1)} %get-tuple-element.32., ...), custom_call_target="tpu_custom_call" | custom-call | tf_op jit(solution)/shard_map/pallas_call | solution.py:393
  12.8 3.7 %all-to-all-start = ((f32[32,8,128]{2,1,0:T(8,128)}), f32[32,8,128]{2,1,0:T(8,128)S(1)}, u32[]{:S(2)}, u32[]{:S(2)}) async-start(f32[32,8,128]{2,1,0:T(8,128)} %bitcast.7), calls=%async_computation | async-start | bytes 262144 | tf_op jit(solution)/shard_map/all_to_all | solution.py:440
  16.6 1.8 %collective-permute-start.5 = (f32[64,128]{1,0:T(8,128)S(1)}, f32[64,128]{1,0:T(8,128)S(1)}, u32[]{:S(2)}, u32[]{:S(2)}) collective-permute-start(f32[64,128]{1,0:T(8,128)S(1)} %get-tuple-element.42), channel_id=1, source_target_pairs={{0,1},{1,0},{2,3},{3,2},{4,5},{5,4},{6,7},{7,6},{8,9},{9,8},{10,11... | collective-permute-start | bytes 98312 | tf_op jit(solution)/shard_map/ppermute | solution.py:47
  18.4 0.0 collective-permute-start.6
  18.4 3.0 %collective-permute-start.7 = (f32[64,128]{1,0:T(8,128)S(1)}, f32[64,128]{1,0:T(8,128)S(1)}, u32[]{:S(2)}, u32[]{:S(2)}) collective-permute-start(f32[64,128]{1,0:T(8,128)S(1)} %get-tuple-element.44), channel_id=1, source_target_pairs={{0,1},{1,0},{2,3},{3,2},{4,8},{5,9},{6,10},{7,11},{8,4},{9,5},{10,... | collective-permute-start | bytes 98312 | tf_op jit(solution)/shard_map/ppermute | solution.py:47
  21.4 0.0 collective-permute-start.8
  21.4 3.8 %all-to-all-done = f32[32,8,128]{2,1,0:T(8,128)S(1)} async-done(((f32[32,8,128]{2,1,0:T(8,128)}), f32[32,8,128]{2,1,0:T(8,128)S(1)}, u32[]{:S(2)}, u32[]{:S(2)}) %all-to-all-start) | async-done | bytes 131104 | tf_op jit(solution)/shard_map/all_to_all | solution.py:440
  25.2 0.1 collective-permute-start.4
  25.3 0.1 reshape.61
  25.4 0.1 reshape.62.inverse
  25.6 0.0 collective-permute-done.5.from_a
  25.6 0.0 collective-permute-done.6.from_b
  25.6 0.0 collective-permute-done.7.from_c
  25.6 0.0 collective-permute-done.8.from_d
  25.6 0.4 shard_map.88
  26.0 0.5 %collective-permute-done.4.other = f32[64,128]{1,0:T(8,128)S(1)} collective-permute-done((f32[64,128]{1,0:T(8,128)S(1)}, f32[64,128]{1,0:T(8,128)S(1)}, u32[]{:S(2)}, u32[]{:S(2)}) %collective-permute-start.4) | collective-permute-done | bytes 32800 | tf_op jit(solution)/shard_map/ppermute | solution.py:450
  26.5 2.5 %shard_map.89 = (f32[32,1,128]{2,1,0:T(1,128)}, f32[16,128]{1,0:T(8,128)S(1)}, f32[16,128]{1,0:T(8,128)S(1)}, f32[16,128]{1,0:T(8,128)S(1)}, f32[16,128]{1,0:T(8...) custom-call(f32[64,128]{1,0:T(8,128)S(1)} %bitcast.20, ...), custom_call_target="tpu_custom_call" | custom-call | tf_op jit(solution)/shard_map/pallas_call | solution.py:393
  29.0 2.5 %all-to-all-start.1 = ((f32[32,1,128]{2,1,0:T(1,128)}), f32[32,1,128]{2,1,0:T(1,128)S(1)}, u32[]{:S(2)}, u32[]{:S(2)}) async-start(f32[32,1,128]{2,1,0:T(1,128)} %get-tuple-element.51), calls=%async_computation.1 | async-start | bytes 32768 | tf_op jit(solution)/shard_map/all_to_all | solution.py:458
  31.6 1.8 %collective-permute-start.9 = (f32[16,128]{1,0:T(8,128)S(1)}, f32[16,128]{1,0:T(8,128)S(1)}, u32[]{:S(2)}, u32[]{:S(2)}) collective-permute-start(f32[16,128]{1,0:T(8,128)S(1)} %get-tuple-element.56), channel_id=1, source_target_pairs={{0,1},{1,0},{2,3},{3,2},{4,5},{5,4},{6,7},{7,6},{8,9},{9,8},{10,11... | collective-permute-start | bytes 24584 | tf_op jit(solution)/shard_map/ppermute | solution.py:47
  33.3 0.0 collective-permute-start.10
  33.3 3.1 %collective-permute-start.11 = (f32[16,128]{1,0:T(8,128)S(1)}, f32[16,128]{1,0:T(8,128)S(1)}, u32[]{:S(2)}, u32[]{:S(2)}) collective-permute-start(f32[16,128]{1,0:T(8,128)S(1)} %get-tuple-element.58), channel_id=1, source_target_pairs={{0,1},{1,0},{2,3},{3,2},{4,8},{5,9},{6,10},{7,11},{8,4},{9,5},{10,... | collective-permute-start | bytes 24584 | tf_op jit(solution)/shard_map/ppermute | solution.py:47
  36.4 0.0 collective-permute-start.12
  36.4 0.0 collective-permute-done.9.from_a
  36.4 0.0 collective-permute-done.10.from_b
  36.4 1.6 %collective-permute-done.11.from_c = f32[16,128]{1,0:T(8,128)S(1)} collective-permute-done((f32[16,128]{1,0:T(8,128)S(1)}, f32[16,128]{1,0:T(8,128)S(1)}, u32[]{:S(2)}, u32[]{:S(2)}) %collective-permute-start.11) | collective-permute-done | bytes 8224 | tf_op jit(solution)/shard_map/ppermute | solution.py:47
  38.0 0.0 collective-permute-done.12.from_d
  38.0 0.2 shard_map.90.second_applied
  38.2 0.5 %all-to-all-done.1.scalars = f32[32,1,128]{2,1,0:T(1,128)S(1)} async-done(((f32[32,1,128]{2,1,0:T(1,128)}), f32[32,1,128]{2,1,0:T(1,128)S(1)}, u32[]{:S(2)}, u32[]{:S(2)}) %all-to-all-start.1) | async-done | bytes 16416 | tf_op jit(solution)/shard_map/all_to_all | solution.py:458
  38.7 0.8 %shard_map.91 = (f32[4,16,128]{2,1,0:T(8,128)}, f32[4,16,128]{2,1,0:T(8,128)}) custom-call(f32[32,1,128]{2,1,0:T(1,128)S(1)} %all-to-all-done.1.scalars, f32[16,512]{1,0:T(8,128)S(1)} %get-tuple-element.47.rhs, f32[16,512]{1,0:T(8,128)S(1)} %get-tuple-element.52.first, f32[16,512]{1,0:T(8,128)S(1)} %get-tuple-element.53.applied, ...), custom_call_target="tpu_custom_call" | custom-call | tf_op jit(solution)/shard_map/pallas_call | solution.py:393
  (10 shorter events, 0.1 us)
Async XLA Ops:
  0.6 1.0 %copy-start = (bf16[1,1,512,512]{3,2,1,0:T(8,128)(2,1)S(1)}, bf16[1,1,512,512]{3,2,1,0:T(8,128)(2,1)}, u32[]{:S(2)}) copy-start(bf16[1,1,512,512]{3,2,1,0:T(8,128)(2,1)} %param.7) | copy-start | bytes 1572868
  1.7 0.8 %copy-start.2 = (f32[1,1,4,16,128]{4,3,2,1,0:T(8,128)S(1)}, f32[1,1,4,16,128]{4,3,2,1,0:T(8,128)}, u32[]{:S(2)}) copy-start(f32[1,1,4,16,128]{4,3,2,1,0:T(8,128)} %param.8) | copy-start | bytes 98308
  2.4 0.7 %copy-start.3 = (f32[1,1,4,6,128]{4,2,3,1,0:T(4,128)S(1)}, f32[1,1,4,6,128]{4,2,3,1,0:T(4,128)}, u32[]{:S(2)}) copy-start(f32[1,1,4,6,128]{4,2,3,1,0:T(4,128)} %param.9) | copy-start | bytes 36868
  3.1 8.1 %copy-start.1 = (bf16[1,1,512,512]{3,2,1,0:T(8,128)(2,1)S(1)}, bf16[1,1,512,512]{3,2,1,0:T(8,128)(2,1)}, u32[]{:S(2)}) copy-start(bf16[1,1,512,512]{3,2,1,0:T(8,128)(2,1)} %param.7) | copy-start | bytes 1572868
  3.3 7.0 %collective-permute-start = (f32[24,128]{1,0:T(8,128)S(1)}, f32[24,128]{1,0:T(8,128)S(1)}, u32[]{:S(2)}, u32[]{:S(2)}) collective-permute-start(f32[24,128]{1,0:T(8,128)S(1)} %get-tuple-element.35), channel_id=1, source_target_pairs={{0,1},{1,0},{2,3},{3,2},{4,5},{5,4},{6,7},{7,6},{8,9},{9,8},{10,11... | collective-permute-start | bytes 36872 | tf_op jit(solution)/shard_map/ppermute | solution.py:47
  6.4 3.9 %collective-permute-start.1 = (f32[24,128]{1,0:T(8,128)S(1)}, f32[24,128]{1,0:T(8,128)S(1)}, u32[]{:S(2)}, u32[]{:S(2)}) collective-permute-start(f32[24,128]{1,0:T(8,128)S(1)} %get-tuple-element.36), channel_id=1, source_target_pairs={{0,4},{1,2},{2,1},{3,7},{4,0},{5,6},{6,5},{7,3},{8,12},{9,10},{10,... | collective-permute-start | bytes 36872 | tf_op jit(solution)/shard_map/ppermute | solution.py:47
  6.4 3.2 %copy-start.5 = (s32[1,1,4,128]{3,2,1,0:T(4,128)S(1)}, s32[1,1,4,128]{3,2,1,0:T(4,128)}, u32[]{:S(2)}) copy-start(s32[1,1,4,128]{3,2,1,0:T(4,128)} %param.11) | copy-start | bytes 6148
  6.4 4.8 %collective-permute-start.2 = (f32[24,128]{1,0:T(8,128)S(1)}, f32[24,128]{1,0:T(8,128)S(1)}, u32[]{:S(2)}, u32[]{:S(2)}) collective-permute-start(f32[24,128]{1,0:T(8,128)S(1)} %get-tuple-element.37), channel_id=1, source_target_pairs={{0,1},{1,0},{2,3},{3,2},{4,8},{5,9},{6,10},{7,11},{8,4},{9,5},{10,... | collective-permute-start | bytes 36872 | tf_op jit(solution)/shard_map/ppermute | solution.py:47
  9.6 1.7 %collective-permute-start.3 = (f32[24,128]{1,0:T(8,128)S(1)}, f32[24,128]{1,0:T(8,128)S(1)}, u32[]{:S(2)}, u32[]{:S(2)}) collective-permute-start(f32[24,128]{1,0:T(8,128)S(1)} %get-tuple-element.38), channel_id=1, source_target_pairs={{0,4},{1,5},{2,6},{3,7},{4,0},{5,1},{6,2},{7,3},{8,12},{9,13},{10,... | collective-permute-start | bytes 36872 | tf_op jit(solution)/shard_map/ppermute | solution.py:47
  9.6 0.7 %copy-start.6 = (s32[1,1,4]{2,1,0:T(1,128)S(1)}, s32[1,1,4]{2,1,0:T(1,128)}, u32[]{:S(2)}) copy-start(s32[1,1,4]{2,1,0:T(1,128)} %param.10) | copy-start | bytes 52
  9.6 0.7 %copy-start.7 = (f32[4]{0:T(128)S(1)}, f32[4]{0:T(128)}, u32[]{:S(2)}) copy-start(f32[4]{0:T(128)} %constant.6.clone) | copy-start | bytes 52
  12.8 12.3 %all-to-all-start = ((f32[32,8,128]{2,1,0:T(8,128)}), f32[32,8,128]{2,1,0:T(8,128)S(1)}, u32[]{:S(2)}, u32[]{:S(2)}) async-start(f32[32,8,128]{2,1,0:T(8,128)} %bitcast.7), calls=%async_computation | async-start | bytes 262144 | tf_op jit(solution)/shard_map/all_to_all | solution.py:440
  16.6 9.0 %collective-permute-start.5 = (f32[64,128]{1,0:T(8,128)S(1)}, f32[64,128]{1,0:T(8,128)S(1)}, u32[]{:S(2)}, u32[]{:S(2)}) collective-permute-start(f32[64,128]{1,0:T(8,128)S(1)} %get-tuple-element.42), channel_id=1, source_target_pairs={{0,1},{1,0},{2,3},{3,2},{4,5},{5,4},{6,7},{7,6},{8,9},{9,8},{10,11... | collective-permute-start | bytes 98312 | tf_op jit(solution)/shard_map/ppermute | solution.py:47
  18.4 7.2 %collective-permute-start.6 = (f32[64,128]{1,0:T(8,128)S(1)}, f32[64,128]{1,0:T(8,128)S(1)}, u32[]{:S(2)}, u32[]{:S(2)}) collective-permute-start(f32[64,128]{1,0:T(8,128)S(1)} %get-tuple-element.43), channel_id=1, source_target_pairs={{0,4},{1,2},{2,1},{3,7},{4,0},{5,6},{6,5},{7,3},{8,12},{9,10},{10,... | collective-permute-start | bytes 98312 | tf_op jit(solution)/shard_map/ppermute | solution.py:47
  18.4 7.2 %collective-permute-start.7 = (f32[64,128]{1,0:T(8,128)S(1)}, f32[64,128]{1,0:T(8,128)S(1)}, u32[]{:S(2)}, u32[]{:S(2)}) collective-permute-start(f32[64,128]{1,0:T(8,128)S(1)} %get-tuple-element.44), channel_id=1, source_target_pairs={{0,1},{1,0},{2,3},{3,2},{4,8},{5,9},{6,10},{7,11},{8,4},{9,5},{10,... | collective-permute-start | bytes 98312 | tf_op jit(solution)/shard_map/ppermute | solution.py:47
  21.4 3.9 %copy-start.4 = (f32[48,48]{1,0:T(8,128)S(1)}, f32[48,48]{1,0:T(8,128)}, u32[]{:S(2)}) copy-start(f32[48,48]{1,0:T(8,128)} %param.12) | copy-start | bytes 27652
  21.4 4.2 %collective-permute-start.8 = (f32[64,128]{1,0:T(8,128)S(1)}, f32[64,128]{1,0:T(8,128)S(1)}, u32[]{:S(2)}, u32[]{:S(2)}) collective-permute-start(f32[64,128]{1,0:T(8,128)S(1)} %get-tuple-element.45), channel_id=1, source_target_pairs={{0,4},{1,5},{2,6},{3,7},{4,0},{5,1},{6,2},{7,3},{8,12},{9,13},{10,... | collective-permute-start | bytes 98312 | tf_op jit(solution)/shard_map/ppermute | solution.py:47
  25.2 1.3 %collective-permute-start.4 = (f32[64,128]{1,0:T(8,128)S(1)}, f32[64,128]{1,0:T(8,128)S(1)}, u32[]{:S(2)}, u32[]{:S(2)}) collective-permute-start(f32[64,128]{1,0:T(8,128)S(1)} %bitcast.19), channel_id=1, source_target_pairs={{0,4},{1,5},{2,6},{3,7},{4,0},{5,1},{6,2},{7,3},{8,12},{9,13},{10,... | collective-permute-start | bytes 98312 | tf_op jit(solution)/shard_map/ppermute | solution.py:450
  29.0 9.7 %all-to-all-start.1 = ((f32[32,1,128]{2,1,0:T(1,128)}), f32[32,1,128]{2,1,0:T(1,128)S(1)}, u32[]{:S(2)}, u32[]{:S(2)}) async-start(f32[32,1,128]{2,1,0:T(1,128)} %get-tuple-element.51), calls=%async_computation.1 | async-start | bytes 32768 | tf_op jit(solution)/shard_map/all_to_all | solution.py:458
  31.6 4.8 %collective-permute-start.9 = (f32[16,128]{1,0:T(8,128)S(1)}, f32[16,128]{1,0:T(8,128)S(1)}, u32[]{:S(2)}, u32[]{:S(2)}) collective-permute-start(f32[16,128]{1,0:T(8,128)S(1)} %get-tuple-element.56), channel_id=1, source_target_pairs={{0,1},{1,0},{2,3},{3,2},{4,5},{5,4},{6,7},{7,6},{8,9},{9,8},{10,11... | collective-permute-start | bytes 24584 | tf_op jit(solution)/shard_map/ppermute | solution.py:47
  33.3 3.1 %collective-permute-start.10 = (f32[16,128]{1,0:T(8,128)S(1)}, f32[16,128]{1,0:T(8,128)S(1)}, u32[]{:S(2)}, u32[]{:S(2)}) collective-permute-start(f32[16,128]{1,0:T(8,128)S(1)} %get-tuple-element.57), channel_id=1, source_target_pairs={{0,4},{1,2},{2,1},{3,7},{4,0},{5,6},{6,5},{7,3},{8,12},{9,10},{10,... | collective-permute-start | bytes 24584 | tf_op jit(solution)/shard_map/ppermute | solution.py:47
  33.3 4.7 %collective-permute-start.11 = (f32[16,128]{1,0:T(8,128)S(1)}, f32[16,128]{1,0:T(8,128)S(1)}, u32[]{:S(2)}, u32[]{:S(2)}) collective-permute-start(f32[16,128]{1,0:T(8,128)S(1)} %get-tuple-element.58), channel_id=1, source_target_pairs={{0,1},{1,0},{2,3},{3,2},{4,8},{5,9},{6,10},{7,11},{8,4},{9,5},{10,... | collective-permute-start | bytes 24584 | tf_op jit(solution)/shard_map/ppermute | solution.py:47
  36.4 1.6 %collective-permute-start.12 = (f32[16,128]{1,0:T(8,128)S(1)}, f32[16,128]{1,0:T(8,128)S(1)}, u32[]{:S(2)}, u32[]{:S(2)}) collective-permute-start(f32[16,128]{1,0:T(8,128)S(1)} %get-tuple-element.59), channel_id=1, source_target_pairs={{0,4},{1,5},{2,6},{3,7},{4,0},{5,1},{6,2},{7,3},{8,12},{9,13},{10,... | collective-permute-start | bytes 24584 | tf_op jit(solution)/shard_map/ppermute | solution.py:47

commit v4 on v3

v4 whole, which is shorter than its diff:
```python
import functools

import jax
import jax.numpy as jnp
from jax import lax
from jax.experimental import pallas as pl
from jax.experimental.pallas import tpu as pltpu
from jax.sharding import PartitionSpec as P

AXES = ("clus", "sub")
F32 = jnp.float32
BF16 = jnp.bfloat16
FULL = lax.Precision.HIGHEST
STRIP = 8
PACK = 16
MIB = 1024 * 1024


def pair_even(index, count):
    other = index ^ 1
    return other if other < count else index


def pair_odd(index, count):
    other = ((index - 1) ^ 1) + 1
    return other if index > 0 and other < count else index


def swap_tables(clusters, subs):
    sub_even, sub_odd, clus_odd, clus_even = [], [], [], []
    for c in range(clusters):
        for s in range(subs):
            here = c * subs + s
            sub_even.append((here, c * subs + pair_even(s, subs)))
            odd = pair_odd(s, subs)
            target = c * subs + odd if odd != s else pair_even(c, clusters) * subs + s
            sub_odd.append((here, target))
            odd = pair_odd(c, clusters)
            target = odd * subs + s if odd != c else c * subs + pair_even(s, subs)
            clus_odd.append((here, target))
            clus_even.append((here, pair_even(c, clusters) * subs + s))
    return sub_even, sub_odd, clus_odd, clus_even


def swap(buffers):
    tables = swap_tables(lax.axis_size("clus"), lax.axis_size("sub"))
    return [lax.ppermute(buffer, AXES, table) for buffer, table in zip(buffers, tables)]


def parities():
    even_c = lax.rem(lax.axis_index("clus"), 2) == 0
    even_s = lax.rem(lax.axis_index("sub"), 2) == 0
    return even_c, even_s


def by_swap(values):
    even_c, even_s = parities()
    return [
        jnp.where(even_s, values[1], values[0]),
        jnp.where(even_s, values[0], values[1]),
        jnp.where(even_c, values[2], values[3]),
        jnp.where(even_c, values[3], values[2]),
    ]


def by_direction(values):
    even_c, even_s = parities()
    return [
        jnp.where(even_s, values[1], values[0]),
        jnp.where(even_s, values[0], values[1]),
        jnp.where(even_c, values[2], values[3]),
        jnp.where(even_c, values[3], values[2]),
    ]


def halves(values):
    high = values.astype(BF16)
    return high, (values - high.astype(F32)).astype(BF16)


def product(left, right):
    return jnp.dot(left, right, preferred_element_type=F32)


def full_product(left, right):
    return jnp.dot(left, right, preferred_element_type=F32, precision=FULL)


def full_product_t(left, right):
    return lax.dot_general(left, right, (((1,), (1,)), ((), ())), preferred_element_type=F32, precision=FULL)


def reorder(values, table):
    count = values.shape[0]
    high, rest = halves(values)
    low = (values - high.astype(F32) - rest.astype(F32)).astype(BF16)
    moved = product(jnp.concatenate([high, rest, low]), table)
    return moved[:count] + moved[count:2 * count] + moved[2 * count:]


def times_matrix(values, matrix):
    count = values.shape[0]
    high, low = halves(values)
    both = product(jnp.concatenate([high, low]), matrix)
    return both[:count] + both[count:]


def start_kernel(
    pair, modes, load_hbm, rigid_hbm, schur_hbm, to_a, to_b, to_c, to_d, load, rigid, buffer, blocks, arrivals
):
    cases = load.shape[1]
    copies = [
        pltpu.make_async_copy(load_hbm, load, arrivals.at[0]),
        pltpu.make_async_copy(rigid_hbm, rigid, arrivals.at[1]),
    ]
    for d in range(4):
        span = slice(d * pair, (d + 1) * pair)
        copies.append(pltpu.make_async_copy(schur_hbm.at[span, span], blocks.at[d], arrivals.at[2 + d]))
    for copy in copies:
        copy.start()
    eye = lax.broadcasted_iota(jnp.int32, (pair, pair), 0) == lax.broadcasted_iota(jnp.int32, (pair, pair), 1)
    buffer[...] = jnp.zeros_like(buffer)
    for copy in copies:
        copy.wait()
    for d in range(4):
        buffer[d, 0:cases] = load[d]
        buffer[d, cases:cases + modes] = rigid[:, d]
        buffer[d, cases + STRIP - 1:cases + STRIP] = jnp.sum(
            jnp.where(eye, blocks[d].astype(F32), 0.0), axis=0, keepdims=True
        )
    for out, values in zip((to_a, to_b, to_c, to_d), by_swap([buffer[d] for d in range(4)])):
        out[...] = values


def fetch_kernel(pair, schur_hbm, partner_hbm, lengths_hbm, schur, tables, sign_live, partner, lengths, arrivals):
    copies = [
        pltpu.make_async_copy(partner_hbm, partner, arrivals.at[0]),
        pltpu.make_async_copy(lengths_hbm, lengths, arrivals.at[1]),
        pltpu.make_async_copy(schur_hbm, schur, arrivals.at[2]),
    ]
    for copy in copies:
        copy.start()
    row = lax.broadcasted_iota(jnp.int32, (pair, pair), 0)
    lane = lax.broadcasted_iota(jnp.int32, (1, pair), 1)
    copies[0].wait()
    copies[1].wait()
    for d in range(4):
        tables[d] = jnp.where(partner[d:d + 1] == row, 1.0, 0.0).astype(BF16)
        sign_live[:, d * pair:(d + 1) * pair] = jnp.where(lane < lengths[:, d:d + 1], (-1.0, 1.0)[d % 2], 0.0)
    copies[2].wait()


def gram_kernel(
    pair, modes, clusters, subs, cases, schur, sign_live, tables, sent_a, sent_b, sent_c, sent_d, from_a, from_b,
    from_c, from_d, packed, to_a, to_b, to_c, to_d, rhs, first, weight, basis, image, operand, right, copies, ready
):
    span = 3 * STRIP
    own = by_direction([sent_a[...], sent_b[...], sent_c[...], sent_d[...]])
    arrived = by_direction([from_a[...], from_b[...], from_c[...], from_d[...]])
    distant = [reorder(arrived[d], tables[d]) for d in range(4)]
    is_mode = lax.broadcasted_iota(jnp.int32, (STRIP, pair), 0) < modes
    none = jnp.zeros((STRIP, pair), F32)
    right[...] = jnp.zeros_like(right)
    for d in range(4):
        lanes = slice(d * pair, (d + 1) * pair)
        sign = sign_live[:, lanes]
        own_tile, far_tile = own[d][cases:], distant[d][cases:]
        both = own_tile[STRIP - 1:] + far_tile[STRIP - 1:]
        is_live = sign != 0.0
        inverse = jnp.where(is_live, 1.0 / jnp.where(is_live, both, 1.0), 0.0)
        weight[:, lanes] = inverse
        own_rhs = sign * (own[d][:cases] - distant[d][:cases])
        own_first = inverse * own_rhs
        rhs[:, lanes] = own_rhs
        first[:, lanes] = own_first
        operand[2 * span:2 * span + cases, lanes] = sign * own_first
        operand[2 * span + cases:2 * span + 2 * cases, lanes] = sign * own_rhs
        near = jnp.where(is_mode, own_tile - far_tile if d < 2 else own_tile, 0.0) * sign
        far = jnp.where(is_mode, -far_tile, 0.0) * sign
        for slot, values in enumerate((far if d == 2 else none, near, far if d == 3 else none)):
            heavy = slice(slot * STRIP, (slot + 1) * STRIP)
            plain = slice(span + slot * STRIP, span + (slot + 1) * STRIP)
            basis[heavy, lanes] = inverse * values
            basis[plain, lanes] = values
            operand[heavy, lanes] = sign * (inverse * values)
            operand[plain, lanes] = sign * values
        right[6 * modes:7 * modes, lanes] = own_tile[:modes]
    image[...] = times_matrix(operand[0:2 * span + cases], schur[...])
    for g in range(6):
        right[g * modes:(g + 1) * modes] = image[g * STRIP:g * STRIP + modes]
    gram = full_product_t(operand[...], right[...])
    lane = lax.broadcasted_iota(jnp.int32, (STRIP, gram.shape[1]), 1)
    strips = []
    for g in range(6):
        strip = gram[g * STRIP:(g + 1) * STRIP]
        own = (lane >= g * modes) & (lane < (g + 1) * modes)
        strips.append(jnp.where(own, 0.5 * strip, strip))
    rows = []
    for row in pack_places(modes):
        total = jnp.zeros_like(strips[0])
        for g, begin, end, at in row:
            piece = strips[g] if at == begin else pltpu.roll(strips[g], (at - begin) % lane.shape[1], 1)
            total = jnp.where((lane >= at) & (lane < at + end - begin), piece, total)
        rows.append(total)
    total = jnp.concatenate(rows)
    lane = lax.broadcasted_iota(jnp.int32, total.shape, 1)
    at = 12 * modes
    with_first = gram[2 * span:2 * span + cases]
    with_rhs = gram[2 * span + cases:2 * span + 2 * cases]
    total = jnp.where(lane >= at, pltpu.roll(with_first, at, 1), total)
    total = jnp.where(lane >= at + 7 * modes, pltpu.roll(with_rhs, at + modes, 1), total)

    strips = [jnp.concatenate([total[h * STRIP:(h + 1) * STRIP]] * subs) for h in range(2)]
    for c in range(clusters):
        copies[c * subs * STRIP:(c + 1) * subs * STRIP] = strips[c % 2]
    copy = pltpu.make_async_copy(copies, packed, ready)
    copy.start()
    parts = [image[:, d * pair:(d + 1) * pair] for d in range(4)]
    for out, values in zip((to_a, to_b, to_c, to_d), by_swap(parts)):
        out[...] = values
    copy.wait()


def pack_places(modes):
    upper = [(0, 0, 7 * modes, 0), (2, 2 * modes, 7 * modes, 7 * modes)]
    lower = [
        (1, modes, 7 * modes, 0), (3, 3 * modes, 6 * modes, 6 * modes),
        (4, 4 * modes, 6 * modes, 9 * modes), (5, 5 * modes, 6 * modes, 11 * modes),
    ]
    return upper, lower


def basis_kernel(
    pair, clusters, basis, image, sign_live, tables, from_a, from_b, from_c, from_d, stacked, applied_first, wide
):
    span = 3 * STRIP
    rows = 4 * pair
    width = clusters * STRIP
    cluster_at = lax.axis_index("clus")
    arrived = by_direction([from_a[...], from_b[...], from_c[...], from_d[...]])
    wide[...] = jnp.zeros_like(wide)
    near = pl.ds(pl.multiple_of((cluster_at + 1) * STRIP, STRIP), span)
    signs = sign_live[...]
    wide[near, 0:rows] = basis[span:2 * span]
    wide[near, rows:2 * rows] = basis[0:span]
    for k in range(2):
        strips = image[k * span:(k + 1) * span]
        wide[near, (2 + k) * rows:(3 + k) * rows] = strips
        wide[near, (4 + k) * rows:(5 + k) * rows] = signs * strips
    for d in range(4):
        lanes = slice(d * pair, (d + 1) * pair)
        sign = sign_live[:, lanes]
        distant = sign * reorder(arrived[d], tables[d])
        at = pl.ds(pl.multiple_of((cluster_at + (1, 1, 0, 2)[d]) * STRIP, STRIP), span)
        for k in range(2):
            begin = (4 + k) * rows + d * pair
            wide[at, begin:begin + pair] -= distant[k * span:(k + 1) * span]
        applied_first[:, lanes] = sign * image[2 * span:, lanes] - distant[2 * span:]
    high, low = halves(wide[2 * STRIP:2 * STRIP + width])
    stacked[0:width] = high
    stacked[width:2 * width] = low
    stacked[2 * width:3 * width] = high


def unpack(half, strips, modes, clusters):
    width = clusters * STRIP
    lane = lax.broadcasted_iota(jnp.int32, (STRIP, 128), 1)
    upper, coupling, with_first, tails = {}, {}, {}, {}

    def put(store, key, values, begin, column):
        tile, offset = divmod(column, 128)
        shift = (offset - begin) % 128
        moved = pltpu.roll(values, shift, 1) if shift else values
        piece = jnp.where((lane >= offset) & (lane < offset + modes), moved, 0.0)
        key = key + (tile,)
        store[key] = store[key] + piece if key in store else piece

    def group(c, h):
        other = c - 1 + h % 3
        return other, (h // 3) * width + other * STRIP

    for c in range(clusters):
        values = strips[c]
        for g, begin, end, at in pack_places(modes)[half]:
            row_cluster, row_at = group(c, g)
            if not 0 <= row_cluster < clusters:
                continue
            for h in range(begin // modes, end // modes):
                source = at + h * modes - begin
                if h == 6:
                    put(coupling, (row_at // STRIP,), values, source, c * STRIP)
                    continue
                other, column = group(c, h)
                if 0 <= other < clusters:
                    put(upper, (row_at // STRIP,), values, source, column)
        for h in range(6):
            other, column = group(c, h)
            if 0 <= other < clusters:
                put(with_first, (half,), values, 12 * modes + h * modes, column)
        put(tails, (half,), values, 19 * modes, c * STRIP)
        put(tails, (2 + half,), values, 18 * modes, c * STRIP)
    return upper, coupling, with_first, tails


def spread(half, strips, modes, clusters, bases, outs):
    stores = unpack(half, [strips[c * STRIP:(c + 1) * STRIP] for c in range(clusters)], modes, clusters)
    for store, base, out in zip(stores, bases, outs):
        for i in range(out.shape[0] // STRIP):
            for t in range(out.shape[1] // 128):
                at = (slice(i * STRIP, (i + 1) * STRIP), slice(t * 128, (t + 1) * 128))
                values = jnp.zeros((STRIP, 128), F32) if base is None else base[at]
                out[at] = values + store[i, t] if (i, t) in store else values


def own_half_kernel(modes, clusters, mine, *outs):
    even_c, _ = parities()
    for half in range(2):
        @pl.when(even_c if half == 0 else jnp.logical_not(even_c))
        def _():
            spread(half, mine, modes, clusters, [None] * 4, outs)


def solve_kernel(
    pair, modes, clusters, other, part_upper, part_couple, part_rows, part_tails, inverse, stacked, rhs, first_part,
    applied_first, weight, sign_live, schur, scalars, to_a, to_b, to_c, to_d, first, applied, second, second_image,
    upper_ref, couple_ref, row_ref, tail_ref, copies, ready
):
    width = clusters * STRIP
    rows = 4 * pair
    even_c, _ = parities()
    for half in range(2):
        @pl.when(even_c if half == 1 else jnp.logical_not(even_c))
        def _():
            spread(
                half, other, modes, clusters, (part_upper, part_couple, part_rows, part_tails),
                (upper_ref, couple_ref, row_ref, tail_ref),
            )

    solver = inverse[...]
    couple_solver = full_product(couple_ref[:, :width], solver)

    def coeffs(straight, weighted):
        both = full_product(jnp.concatenate([straight, weighted]), solver)
        a = both[:PACK]
        return a, both[PACK:] - full_product(a, couple_solver)

    def combine(a, b, tables):
        high, low = halves(jnp.concatenate([a, b]))
        moved = product(jnp.concatenate([high, high, low], axis=1), tables)
        return [[moved[i * PACK:(i + 1) * PACK, k * rows:(k + 1) * rows] for k in range(4)] for i in range(2)]

    tail = tail_ref[:, :width]
    a_first, b_first = coeffs(tail[:PACK], tail[PACK:])
    c_first = jnp.concatenate([a_first, b_first], axis=1)
    upper_matrix = upper_ref[:, :2 * width]
    parts = row_ref[:, :2 * width] - full_product(c_first, upper_matrix) - full_product_t(c_first, upper_matrix)
    a_second, b_second = coeffs(parts[:, width:], parts[:, :width])

    a_of, b_of = combine(a_first, b_first, jnp.concatenate([stacked[:, :2 * rows], stacked[:, 4 * rows:]], axis=1))
    projected = rhs[...] - a_of[0]
    direction = first_part[...] - a_of[1] - b_of[0]
    image = applied_first[...] - a_of[2] - b_of[3]
    heavy = weight[...] * image
    heavy_image = times_matrix(sign_live[...] * heavy, schur[...])

    a_of, b_of = combine(a_second, b_second, stacked[:, :4 * rows])
    image_projected = image - a_of[0]
    last = heavy - a_of[1] - b_of[0]
    last_image = heavy_image - a_of[2] - b_of[3]

    def folded(values):
        return sum(values[:, d * pair:(d + 1) * pair] for d in range(4))

    terms = jnp.concatenate([
        folded(0.5 * (projected * direction)),
        folded(0.5 * (direction * image)),
        folded(0.5 * (projected * last + image_projected * direction)),
        folded(0.5 * (image_projected * last)),
        folded(0.5 * (image * last)),
        folded((sign_live[...] * last) * last_image),
        jnp.zeros((128 - 6 * PACK, pair), F32),
    ])
    ones = jnp.ones((STRIP, 2 * pair), BF16)
    row = lax.dot_general(
        ones, jnp.concatenate(halves(terms), axis=1), (((1,), (1,)), ((), ())), preferred_element_type=F32
    )[0:1]
    copies[...] = jnp.broadcast_to(row[:, None, :], copies.shape)
    copy = pltpu.make_async_copy(copies, scalars, ready)
    copy.start()
    first[...] = direction
    applied[...] = image
    second[...] = last
    second_image[...] = last_image
    parts = [last_image[:, d * pair:(d + 1) * pair] for d in range(4)]
    for out, values in zip((to_a, to_b, to_c, to_d), by_swap(parts)):
        out[...] = values
    copy.wait()


def far_kernel(pair, image, sign_live, tables, from_a, from_b, from_c, from_d, applied):
    arrived = by_direction([from_a[...], from_b[...], from_c[...], from_d[...]])
    for d in range(4):
        lanes = slice(d * pair, (d + 1) * pair)
        applied[:, lanes] = sign_live[:, lanes] * (image[:, lanes] - reorder(arrived[d], tables[d]))


def end_kernel(
    pair, scalars, rhs, first, applied, second, second_applied, multipliers, residual, first_buffer, second_buffer, done
):
    total = jnp.sum(scalars[...], axis=0)
    rho_one, delta_one, cross, square, mixed, delta_last = [
        total if i == 0 else pltpu.roll(total, 128 - i * PACK, 1) for i in range(6)
    ]
    alpha_one = rho_one / delta_one
    rho_two = rho_one - alpha_one * cross + alpha_one * alpha_one * square
    grow = 1.0 + rho_two / rho_one
    delta_two = grow * grow * delta_one - 2.0 * grow * alpha_one * mixed + alpha_one * alpha_one * delta_last
    alpha_two = rho_two / delta_two
    eye = lax.broadcasted_iota(jnp.int32, (PACK, 128), 0) == lax.broadcasted_iota(jnp.int32, (PACK, 128), 1)

    def column(values):
        return jnp.sum(jnp.where(eye, values, 0.0), axis=1, keepdims=True)

    keep = column(alpha_one + alpha_two * grow)
    drop = column(alpha_two * alpha_one)
    results = [
        keep * first[...] - drop * second[...],
        rhs[...] - keep * applied[...] + drop * second_applied[...],
    ]
    copies = []
    for i, (result, out, buffer) in enumerate(zip(results, (multipliers, residual), (first_buffer, second_buffer))):
        for d in range(4):
            buffer[d] = result[:, d * pair:(d + 1) * pair]
        copies.append(pltpu.make_async_copy(buffer, out, done.at[i]))
        copies[-1].start()
    for copy in copies:
        copy.wait()


def call(
    kernel, outs, scratch, *args, place=pltpu.VMEM, first_place=pltpu.VMEM, later_place=pltpu.VMEM, limit=32 * MIB
):
    places = [first_place] + [later_place] * (len(outs) - 1)
    return pl.pallas_call(
        kernel,
        out_shape=[place_out(shape, dtype) for place_out, (shape, dtype) in zip(places, outs)],
        in_specs=[pl.BlockSpec(memory_space=place)] * len(args),
        out_specs=[pl.BlockSpec(memory_space=place_out) for place_out in places],
        scratch_shapes=scratch,
        compiler_params=pltpu.CompilerParams(vmem_limit_bytes=limit),
    )(*[pltpu.with_memory_space_constraint(arg, place) if place is pltpu.HBM else arg for arg in args])


def shards(schur, load, rigid, lengths, partner, coarse_inverse):
    own_load, matrix = load[0, 0], schur[0, 0]
    own_rigid = jnp.swapaxes(rigid[0, 0], 0, 1)
    cases, pair = own_load.shape[1:]
    modes = own_rigid.shape[0]
    clusters, subs = lax.axis_size("clus"), lax.axis_size("sub")
    devices = clusters * subs
    rows = 4 * pair
    width = clusters * STRIP
    span = 3 * STRIP

    wide_inverse = jnp.pad(
        coarse_inverse.reshape(clusters, modes, clusters, modes),
        ((0, 0), (0, STRIP - modes), (0, 0), (0, STRIP - modes)),
    ).reshape(width, width)

    flat = ((cases, rows), F32)
    sent = call(
        functools.partial(start_kernel, pair, modes),
        [((cases + STRIP, pair), F32)] * 4,
        [pltpu.VMEM(own_load.shape, F32), pltpu.VMEM(own_rigid.shape, F32), pltpu.VMEM((4, cases + STRIP, pair), F32),
         pltpu.VMEM((4, pair, pair), BF16), pltpu.SemaphoreType.DMA((6,))],
        own_load, own_rigid, matrix, place=pltpu.HBM,
    )
    arrived = swap(sent)
    matrix, tables, sign_live = call(
        functools.partial(fetch_kernel, pair),
        [((rows, rows), BF16), ((4, pair, pair), BF16), ((1, rows), F32)],
        [pltpu.VMEM((4, pair), jnp.int32), pltpu.VMEM((1, 4), jnp.int32), pltpu.SemaphoreType.DMA((3,))],
        matrix, partner[0, 0], lengths[0], place=pltpu.HBM,
    )

    packed, *images, rhs, first_part, weight, basis, image = call(
        functools.partial(gram_kernel, pair, modes, clusters, subs, cases),
        [((devices * STRIP, 128), F32)] + [((2 * span + cases, pair), F32)] * 4
        + [flat, flat, ((1, rows), F32), ((2 * span, rows), F32), ((2 * span + cases, rows), F32)],
        [pltpu.VMEM((2 * span + 2 * cases, rows), F32), pltpu.VMEM((128, rows), F32),
         pltpu.VMEM((devices * STRIP, 128), F32), pltpu.SemaphoreType.DMA],
        matrix, sign_live, tables, *sent, *arrived, first_place=pltpu.HBM,
    )
    gathered = lax.all_to_all(packed, AXES, 0, 0, tiled=True)
    arrived = swap(images)
    stacked, applied_first = call(
        functools.partial(basis_kernel, pair, clusters),
        [((3 * width, 6 * rows), BF16), flat],
        [pltpu.VMEM((width + 4 * STRIP, 6 * rows), F32)],
        basis, image, sign_live, tables, *arrived,
    )
    gathered, stacked = lax.optimization_barrier((gathered, stacked))

    mine = jnp.sum(gathered.reshape(clusters, subs, STRIP, 128), axis=1).reshape(width, 128)
    other = lax.ppermute(mine, AXES, swap_tables(clusters, subs)[3])
    lanes = max(width, 128)
    shapes = [((2 * width, max(2 * width, 128)), F32), ((width, lanes), F32), ((PACK, max(2 * width, 128)), F32),
              ((2 * PACK, lanes), F32)]
    parts = call(functools.partial(own_half_kernel, modes, clusters), shapes, [], mine)
    scalars, *images, first, applied, second, second_image = call(
        functools.partial(solve_kernel, pair, modes, clusters),
        [((devices, 1, 128), F32)] + [((cases, pair), F32)] * 4 + [flat] * 4,
        [pltpu.VMEM(*shape) for shape in shapes]
        + [pltpu.VMEM((devices, 1, 128), F32), pltpu.SemaphoreType.DMA],
        other, *parts, wide_inverse, stacked, rhs, first_part, applied_first, weight, sign_live, matrix,
        first_place=pltpu.HBM,
    )
    gathered = lax.all_to_all(scalars, AXES, 0, 0, tiled=True)
    arrived = swap(images)
    (second_applied,) = call(
        functools.partial(far_kernel, pair), [flat], [], second_image, sign_live, tables, *arrived
    )
    multipliers, residual = call(
        functools.partial(end_kernel, pair), [((4, cases, pair), F32)] * 2,
        [pltpu.VMEM((4, cases, pair), F32)] * 2 + [pltpu.SemaphoreType.DMA((2,))],
        gathered, rhs, first, applied, second, second_applied, first_place=pltpu.HBM, later_place=pltpu.HBM,
    )
    return (multipliers[None, None], residual[None, None])


def solution(mesh):
    in_specs = (
        P("clus", "sub", None, None),
        P("clus", "sub", None, None, None),
        P("clus", "sub", None, None, None),
        P("clus", "sub", None),
        P("clus", "sub", None, None),
        P(),
    )
    out_specs = (P("clus", "sub", None, None, None), P("clus", "sub", None, None, None))
    return jax.shard_map(shards, mesh=mesh, in_specs=in_specs, out_specs=out_specs, check_vma=False)
```

time: 39.9 us -> 38.1 us (0.955)
  local copies, waits for them, and re-layouts: 3.42 us -> 0.26 us
  Pallas kernels: 5.68 us -> 7.86 us
  waiting for transfers between devices: 7.3 us -> 6.68 us
    unnamed x16 -> x2, local copies, waits for them, and re-layouts: 3.17 us -> 0.01 us
    all_to_all x1, waiting for transfers between devices: 3.8 us -> 1.34 us  [shards(): gathered = lax.all_to_all(packed, AXES, 0, 0, tiled=True)]
    pallas_call x6 -> x8, Pallas kernels: 5.68 us -> 7.86 us  [call(): pl.pallas_call(kernel, out_shape=[place_out(shape, dtype) for place_out,...]
    ppermute x12, waiting for transfers between devices: 2.52 us -> 4.16 us  [swap(): lax.ppermute(buffer, AXES, table)]
  transfers between devices with their start and end apart: 15 -> 15, of which waited for: 5 -> 6; matrix products, arithmetic and copies ran while one was open for 1% -> 1% of each run, Pallas kernels for 1% -> 5%
where the time goes in v4:
time: 38.1 us; the launch traced here: 37.8 us
  starting transfers between devices  22.2 us (58%)
  Pallas kernels  7.86 us (21%)
  waiting for transfers between devices  6.68 us (18%)
  between operations  0.78 us (2%)
    ppermute x12, starting transfers between devices, swap(): lax.ppermute(buffer, AXES, table)  15.9 us
    pallas_call x8, Pallas kernels, call(): pl.pallas_call(kernel, out_shape=[place_out(shape, dtype) for place_out,...  7.86 us
    ppermute x12, waiting for transfers between devices, swap(): lax.ppermute(buffer, AXES, table)  4.16 us
    all_to_all x1, starting transfers between devices, shards(): gathered = lax.all_to_all(packed, AXES, 0, 0, tiled=True)  3.72 us
    all_to_all x1, starting transfers between devices, shards(): gathered = lax.all_to_all(scalars, AXES, 0, 0, tiled=True)  2.56 us
    all_to_all x1, waiting for transfers between devices, shards(): gathered = lax.all_to_all(packed, AXES, 0, 0, tiled=True)  1.34 us
  transfers between devices with their start and end apart: 15, of which 6 were waited for; matrix products, arithmetic and copies ran while one was open for 1% of the time, Pallas kernels for 5%

profile of v4, /device:TPU:0, one launch (start us, length us, event | category | flops | bytes accessed | tf_op | source)
XLA Modules:
  0.0 37.8 jit_solution(7389189467265396295)
XLA Ops:
  0.6 1.0 %shard_map.78 = (f32[24,128]{1,0:T(8,128)S(1)}, f32[24,128]{1,0:T(8,128)S(1)}, f32[24,128]{1,0:T(8,128)S(1)}, f32[24,128]{1,0:T(8,128)S(1)}) custom-call(f32[4,16,128]{2,1,0:T(8,128)} %bitcast.21, f32[6,4,128]{2,1,0:T(4,128)} %bitcast.22, bf16[512,512]{1,0:T(8,128)(2,1)} %bitcast.17), custom_call_target="tpu_custom_call" | custom-call | tf_op jit(solution)/shard_map/pallas_call | solution.py:444
  1.6 0.0 copy-start
  1.6 3.1 %collective-permute-start = (f32[24,128]{1,0:T(8,128)S(1)}, f32[24,128]{1,0:T(8,128)S(1)}, u32[]{:S(2)}, u32[]{:S(2)}) collective-permute-start(f32[24,128]{1,0:T(8,128)S(1)} %get-tuple-element.41.sent_a), channel_id=1, source_target_pairs={{0,1},{1,0},{2,3},{3,2},{4,5},{5,4},{6,7},{7,6},{8,9},{9,8},{10,11... | collective-permute-start | bytes 36872 | tf_op jit(solution)/shard_map/ppermute | solution.py:47
  4.7 0.0 collective-permute-start.1
  4.7 3.1 %collective-permute-start.2 = (f32[24,128]{1,0:T(8,128)S(1)}, f32[24,128]{1,0:T(8,128)S(1)}, u32[]{:S(2)}, u32[]{:S(2)}) collective-permute-start(f32[24,128]{1,0:T(8,128)S(1)} %get-tuple-element.43.sent_c), channel_id=1, source_target_pairs={{0,1},{1,0},{2,3},{3,2},{4,8},{5,9},{6,10},{7,11},{8,4},{9,5},{10,... | collective-permute-start | bytes 36872 | tf_op jit(solution)/shard_map/ppermute | solution.py:47
  7.9 0.0 collective-permute-start.3
  7.9 1.1 %shard_map.77 = (bf16[512,512]{1,0:T(8,128)(2,1)S(1)}, bf16[4,128,128]{2,1,0:T(8,128)(2,1)S(1)}, f32[1,512]{1,0:T(1,128)S(1)}) custom-call(bf16[512,512]{1,0:T(8,128)(2,1)} %bitcast.18, s32[4,128]{1,0:T(4,128)} %bitcast.23, s32[1,4]{1,0:T(1,128)} %bitcast.24), custom_call_target="tpu_custom_call" | custom-call | tf_op jit(solution)/shard_map/pallas_call | solution.py:444
  9.0 0.0 collective-permute-done.from_a
  9.0 0.0 collective-permute-done.1.from_b
  9.0 0.5 %collective-permute-done.2.from_c = f32[24,128]{1,0:T(8,128)S(1)} collective-permute-done((f32[24,128]{1,0:T(8,128)S(1)}, f32[24,128]{1,0:T(8,128)S(1)}, u32[]{:S(2)}, u32[]{:S(2)}) %collective-permute-start.2) | collective-permute-done | bytes 12320 | tf_op jit(solution)/shard_map/ppermute | solution.py:47
  9.5 0.0 collective-permute-done.3.from_d
  9.5 1.6 %shard_map.79 = (f32[256,128]{1,0:T(8,128)}, f32[64,128]{1,0:T(8,128)S(1)}, f32[64,128]{1,0:T(8,128)S(1)}, f32[64,128]{1,0:T(8,128)S(1)}, f32[64,128]{1,0:T(8,12...) custom-call(bf16[512,512]{1,0:T(8,128)(2,1)S(1)} %get-tuple-element., ...), custom_call_target="tpu_custom_call" | custom-call | tf_op jit(solution)/shard_map/pallas_call | solution.py:444
  11.1 3.7 %all-to-all-start = ((f32[32,8,128]{2,1,0:T(8,128)}), f32[32,8,128]{2,1,0:T(8,128)S(1)}, u32[]{:S(2)}, u32[]{:S(2)}) async-start(f32[32,8,128]{2,1,0:T(8,128)} %bitcast.20), calls=%async_computation | async-start | bytes 262144 | tf_op jit(solution)/shard_map/all_to_all | solution.py:494
  14.8 1.8 %collective-permute-start.4 = (f32[64,128]{1,0:T(8,128)S(1)}, f32[64,128]{1,0:T(8,128)S(1)}, u32[]{:S(2)}, u32[]{:S(2)}) collective-permute-start(f32[64,128]{1,0:T(8,128)S(1)} %get-tuple-element.48), channel_id=1, source_target_pairs={{0,1},{1,0},{2,3},{3,2},{4,5},{5,4},{6,7},{7,6},{8,9},{9,8},{10,11... | collective-permute-start | bytes 98312 | tf_op jit(solution)/shard_map/ppermute | solution.py:47
  16.7 0.0 collective-permute-start.5
  16.7 3.0 %collective-permute-start.6 = (f32[64,128]{1,0:T(8,128)S(1)}, f32[64,128]{1,0:T(8,128)S(1)}, u32[]{:S(2)}, u32[]{:S(2)}) collective-permute-start(f32[64,128]{1,0:T(8,128)S(1)} %get-tuple-element.50), channel_id=1, source_target_pairs={{0,1},{1,0},{2,3},{3,2},{4,8},{5,9},{6,10},{7,11},{8,4},{9,5},{10,... | collective-permute-start | bytes 98312 | tf_op jit(solution)/shard_map/ppermute | solution.py:47
  19.6 0.0 collective-permute-start.7
  19.6 0.0 collective-permute-done.4.from_a
  19.6 0.0 collective-permute-done.5.from_b
  19.7 2.0 %collective-permute-done.6.from_c = f32[64,128]{1,0:T(8,128)S(1)} collective-permute-done((f32[64,128]{1,0:T(8,128)S(1)}, f32[64,128]{1,0:T(8,128)S(1)}, u32[]{:S(2)}, u32[]{:S(2)}) %collective-permute-start.6) | collective-permute-done | bytes 32800 | tf_op jit(solution)/shard_map/ppermute | solution.py:47
  21.6 0.0 collective-permute-done.7.from_d
  21.6 0.5 %shard_map.80 = (bf16[192,3072]{1,0:T(8,128)(2,1)S(1)}, f32[16,512]{1,0:T(8,128)S(1)}) custom-call(f32[48,512]{1,0:T(8,128)S(1)} %get-tuple-element.46.basis, f32[64,512]{1,0:T(8,128)S(1)} %get-tuple-element.47.image, f32[1,512]{1,0:T(1,128)S(1)} %get-tuple-element.39.sign_live, bf16[4,128,128]{2,1,0:T(8,128)(2,1)S(1)} %get-tuple-element.40.tables, ...), custom_call_target="tpu_custom_call" | custom-call | tf_op jit(solution)/shard_map/pallas_call | solution.py:444
  22.1 1.3 %all-to-all-done = f32[32,8,128]{2,1,0:T(8,128)S(1)} async-done(((f32[32,8,128]{2,1,0:T(8,128)}), f32[32,8,128]{2,1,0:T(8,128)S(1)}, u32[]{:S(2)}, u32[]{:S(2)}) %all-to-all-start) | async-done | bytes 131104 | tf_op jit(solution)/shard_map/all_to_all | solution.py:494
  23.5 0.1 collective-permute-start.8
  23.5 0.0 copy-done
  23.6 0.1 reshape.20
  23.7 0.1 reshape.21.inverse
  23.8 0.2 shard_map.81
  24.1 0.7 %collective-permute-done.8.other = f32[64,128]{1,0:T(8,128)S(1)} collective-permute-done((f32[64,128]{1,0:T(8,128)S(1)}, f32[64,128]{1,0:T(8,128)S(1)}, u32[]{:S(2)}, u32[]{:S(2)}) %collective-permute-start.8) | collective-permute-done | bytes 32800 | tf_op jit(solution)/shard_map/ppermute | solution.py:505
  24.7 2.5 %shard_map.82 = (f32[32,1,128]{2,1,0:T(1,128)}, f32[16,128]{1,0:T(8,128)S(1)}, f32[16,128]{1,0:T(8,128)S(1)}, f32[16,128]{1,0:T(8,128)S(1)}, f32[16,128]{1,0:T(8...) custom-call(f32[64,128]{1,0:T(8,128)S(1)} %collective-permute-done.8.o, ...), custom_call_target="tpu_custom_call" | custom-call | tf_op jit(solution)/shard_map/pallas_call | solution.py:444
  27.3 2.6 %all-to-all-start.1 = ((f32[32,1,128]{2,1,0:T(1,128)}), f32[32,1,128]{2,1,0:T(1,128)S(1)}, u32[]{:S(2)}, u32[]{:S(2)}) async-start(f32[32,1,128]{2,1,0:T(1,128)} %get-tuple-element.63), calls=%async_computation.1 | async-start | bytes 32768 | tf_op jit(solution)/shard_map/all_to_all | solution.py:518
  29.8 1.8 %collective-permute-start.9 = (f32[16,128]{1,0:T(8,128)S(1)}, f32[16,128]{1,0:T(8,128)S(1)}, u32[]{:S(2)}, u32[]{:S(2)}) collective-permute-start(f32[16,128]{1,0:T(8,128)S(1)} %get-tuple-element.68), channel_id=1, source_target_pairs={{0,1},{1,0},{2,3},{3,2},{4,5},{5,4},{6,7},{7,6},{8,9},{9,8},{10,11... | collective-permute-start | bytes 24584 | tf_op jit(solution)/shard_map/ppermute | solution.py:47
  31.7 0.0 collective-permute-start.10
  31.7 3.0 %collective-permute-start.11 = (f32[16,128]{1,0:T(8,128)S(1)}, f32[16,128]{1,0:T(8,128)S(1)}, u32[]{:S(2)}, u32[]{:S(2)}) collective-permute-start(f32[16,128]{1,0:T(8,128)S(1)} %get-tuple-element.70), channel_id=1, source_target_pairs={{0,1},{1,0},{2,3},{3,2},{4,8},{5,9},{6,10},{7,11},{8,4},{9,5},{10,... | collective-permute-start | bytes 24584 | tf_op jit(solution)/shard_map/ppermute | solution.py:47
  34.7 0.0 collective-permute-start.12
  34.7 0.0 collective-permute-done.9.from_a
  34.7 0.0 collective-permute-done.10.from_b
  34.7 1.6 %collective-permute-done.11.from_c = f32[16,128]{1,0:T(8,128)S(1)} collective-permute-done((f32[16,128]{1,0:T(8,128)S(1)}, f32[16,128]{1,0:T(8,128)S(1)}, u32[]{:S(2)}, u32[]{:S(2)}) %collective-permute-start.11) | collective-permute-done | bytes 8224 | tf_op jit(solution)/shard_map/ppermute | solution.py:47
  36.3 0.0 collective-permute-done.12.from_d
  36.3 0.2 shard_map.83.second_applied
  36.4 0.5 %all-to-all-done.1.scalars = f32[32,1,128]{2,1,0:T(1,128)S(1)} async-done(((f32[32,1,128]{2,1,0:T(1,128)}), f32[32,1,128]{2,1,0:T(1,128)S(1)}, u32[]{:S(2)}, u32[]{:S(2)}) %all-to-all-start.1) | async-done | bytes 16416 | tf_op jit(solution)/shard_map/all_to_all | solution.py:518
  37.0 0.9 %shard_map.84 = (f32[4,16,128]{2,1,0:T(8,128)}, f32[4,16,128]{2,1,0:T(8,128)}) custom-call(f32[32,1,128]{2,1,0:T(1,128)S(1)} %all-to-all-done.1.scalars, f32[16,512]{1,0:T(8,128)S(1)} %get-tuple-element.59.rhs, f32[16,512]{1,0:T(8,128)S(1)} %get-tuple-element.64.first, f32[16,512]{1,0:T(8,128)S(1)} %get-tuple-element.65.applied, ...), custom_call_target="tpu_custom_call" | custom-call | tf_op jit(solution)/shard_map/pallas_call | solution.py:444
  (2 shorter events, 0.0 us)
Async XLA Ops:
  1.6 21.9 %copy-start = (f32[48,48]{1,0:T(8,128)S(1)}, f32[48,48]{1,0:T(8,128)}, u32[]{:S(2)}) copy-start(f32[48,48]{1,0:T(8,128)} %param.11) | copy-start | bytes 27652
  1.6 7.4 %collective-permute-start = (f32[24,128]{1,0:T(8,128)S(1)}, f32[24,128]{1,0:T(8,128)S(1)}, u32[]{:S(2)}, u32[]{:S(2)}) collective-permute-start(f32[24,128]{1,0:T(8,128)S(1)} %get-tuple-element.41.sent_a), channel_id=1, source_target_pairs={{0,1},{1,0},{2,3},{3,2},{4,5},{5,4},{6,7},{7,6},{8,9},{9,8},{10,11... | collective-permute-start | bytes 36872 | tf_op jit(solution)/shard_map/ppermute | solution.py:47
  4.7 4.3 %collective-permute-start.1 = (f32[24,128]{1,0:T(8,128)S(1)}, f32[24,128]{1,0:T(8,128)S(1)}, u32[]{:S(2)}, u32[]{:S(2)}) collective-permute-start(f32[24,128]{1,0:T(8,128)S(1)} %get-tuple-element.42.sent_b), channel_id=1, source_target_pairs={{0,4},{1,2},{2,1},{3,7},{4,0},{5,6},{6,5},{7,3},{8,12},{9,10},{10,... | collective-permute-start | bytes 36872 | tf_op jit(solution)/shard_map/ppermute | solution.py:47
  4.7 4.8 %collective-permute-start.2 = (f32[24,128]{1,0:T(8,128)S(1)}, f32[24,128]{1,0:T(8,128)S(1)}, u32[]{:S(2)}, u32[]{:S(2)}) collective-permute-start(f32[24,128]{1,0:T(8,128)S(1)} %get-tuple-element.43.sent_c), channel_id=1, source_target_pairs={{0,1},{1,0},{2,3},{3,2},{4,8},{5,9},{6,10},{7,11},{8,4},{9,5},{10,... | collective-permute-start | bytes 36872 | tf_op jit(solution)/shard_map/ppermute | solution.py:47
  7.9 1.7 %collective-permute-start.3 = (f32[24,128]{1,0:T(8,128)S(1)}, f32[24,128]{1,0:T(8,128)S(1)}, u32[]{:S(2)}, u32[]{:S(2)}) collective-permute-start(f32[24,128]{1,0:T(8,128)S(1)} %get-tuple-element.44.sent_d), channel_id=1, source_target_pairs={{0,4},{1,5},{2,6},{3,7},{4,0},{5,1},{6,2},{7,3},{8,12},{9,13},{10,... | collective-permute-start | bytes 36872 | tf_op jit(solution)/shard_map/ppermute | solution.py:47
  11.1 12.3 %all-to-all-start = ((f32[32,8,128]{2,1,0:T(8,128)}), f32[32,8,128]{2,1,0:T(8,128)S(1)}, u32[]{:S(2)}, u32[]{:S(2)}) async-start(f32[32,8,128]{2,1,0:T(8,128)} %bitcast.20), calls=%async_computation | async-start | bytes 262144 | tf_op jit(solution)/shard_map/all_to_all | solution.py:494
  14.8 4.8 %collective-permute-start.4 = (f32[64,128]{1,0:T(8,128)S(1)}, f32[64,128]{1,0:T(8,128)S(1)}, u32[]{:S(2)}, u32[]{:S(2)}) collective-permute-start(f32[64,128]{1,0:T(8,128)S(1)} %get-tuple-element.48), channel_id=1, source_target_pairs={{0,1},{1,0},{2,3},{3,2},{4,5},{5,4},{6,7},{7,6},{8,9},{9,8},{10,11... | collective-permute-start | bytes 98312 | tf_op jit(solution)/shard_map/ppermute | solution.py:47
  16.7 3.0 %collective-permute-start.5 = (f32[64,128]{1,0:T(8,128)S(1)}, f32[64,128]{1,0:T(8,128)S(1)}, u32[]{:S(2)}, u32[]{:S(2)}) collective-permute-start(f32[64,128]{1,0:T(8,128)S(1)} %get-tuple-element.49), channel_id=1, source_target_pairs={{0,4},{1,2},{2,1},{3,7},{4,0},{5,6},{6,5},{7,3},{8,12},{9,10},{10,... | collective-permute-start | bytes 98312 | tf_op jit(solution)/shard_map/ppermute | solution.py:47
  16.7 5.0 %collective-permute-start.6 = (f32[64,128]{1,0:T(8,128)S(1)}, f32[64,128]{1,0:T(8,128)S(1)}, u32[]{:S(2)}, u32[]{:S(2)}) collective-permute-start(f32[64,128]{1,0:T(8,128)S(1)} %get-tuple-element.50), channel_id=1, source_target_pairs={{0,1},{1,0},{2,3},{3,2},{4,8},{5,9},{6,10},{7,11},{8,4},{9,5},{10,... | collective-permute-start | bytes 98312 | tf_op jit(solution)/shard_map/ppermute | solution.py:47
  19.6 2.0 %collective-permute-start.7 = (f32[64,128]{1,0:T(8,128)S(1)}, f32[64,128]{1,0:T(8,128)S(1)}, u32[]{:S(2)}, u32[]{:S(2)}) collective-permute-start(f32[64,128]{1,0:T(8,128)S(1)} %get-tuple-element.51), channel_id=1, source_target_pairs={{0,4},{1,5},{2,6},{3,7},{4,0},{5,1},{6,2},{7,3},{8,12},{9,13},{10,... | collective-permute-start | bytes 98312 | tf_op jit(solution)/shard_map/ppermute | solution.py:47
  23.5 1.3 %collective-permute-start.8 = (f32[64,128]{1,0:T(8,128)S(1)}, f32[64,128]{1,0:T(8,128)S(1)}, u32[]{:S(2)}, u32[]{:S(2)}) collective-permute-start(f32[64,128]{1,0:T(8,128)S(1)} %bitcast.15), channel_id=1, source_target_pairs={{0,4},{1,5},{2,6},{3,7},{4,0},{5,1},{6,2},{7,3},{8,12},{9,13},{10,... | collective-permute-start | bytes 98312 | tf_op jit(solution)/shard_map/ppermute | solution.py:505
  27.3 9.7 %all-to-all-start.1 = ((f32[32,1,128]{2,1,0:T(1,128)}), f32[32,1,128]{2,1,0:T(1,128)S(1)}, u32[]{:S(2)}, u32[]{:S(2)}) async-start(f32[32,1,128]{2,1,0:T(1,128)} %get-tuple-element.63), calls=%async_computation.1 | async-start | bytes 32768 | tf_op jit(solution)/shard_map/all_to_all | solution.py:518
  29.8 4.8 %collective-permute-start.9 = (f32[16,128]{1,0:T(8,128)S(1)}, f32[16,128]{1,0:T(8,128)S(1)}, u32[]{:S(2)}, u32[]{:S(2)}) collective-permute-start(f32[16,128]{1,0:T(8,128)S(1)} %get-tuple-element.68), channel_id=1, source_target_pairs={{0,1},{1,0},{2,3},{3,2},{4,5},{5,4},{6,7},{7,6},{8,9},{9,8},{10,11... | collective-permute-start | bytes 24584 | tf_op jit(solution)/shard_map/ppermute | solution.py:47
  31.7 3.0 %collective-permute-start.10 = (f32[16,128]{1,0:T(8,128)S(1)}, f32[16,128]{1,0:T(8,128)S(1)}, u32[]{:S(2)}, u32[]{:S(2)}) collective-permute-start(f32[16,128]{1,0:T(8,128)S(1)} %get-tuple-element.69), channel_id=1, source_target_pairs={{0,4},{1,2},{2,1},{3,7},{4,0},{5,6},{6,5},{7,3},{8,12},{9,10},{10,... | collective-permute-start | bytes 24584 | tf_op jit(solution)/shard_map/ppermute | solution.py:47
  31.7 4.6 %collective-permute-start.11 = (f32[16,128]{1,0:T(8,128)S(1)}, f32[16,128]{1,0:T(8,128)S(1)}, u32[]{:S(2)}, u32[]{:S(2)}) collective-permute-start(f32[16,128]{1,0:T(8,128)S(1)} %get-tuple-element.70), channel_id=1, source_target_pairs={{0,1},{1,0},{2,3},{3,2},{4,8},{5,9},{6,10},{7,11},{8,4},{9,5},{10,... | collective-permute-start | bytes 24584 | tf_op jit(solution)/shard_map/ppermute | solution.py:47
  34.7 1.6 %collective-permute-start.12 = (f32[16,128]{1,0:T(8,128)S(1)}, f32[16,128]{1,0:T(8,128)S(1)}, u32[]{:S(2)}, u32[]{:S(2)}) collective-permute-start(f32[16,128]{1,0:T(8,128)S(1)} %get-tuple-element.71), channel_id=1, source_target_pairs={{0,4},{1,5},{2,6},{3,7},{4,0},{5,1},{6,2},{7,3},{8,12},{9,13},{10,... | collective-permute-start | bytes 24584 | tf_op jit(solution)/shard_map/ppermute | solution.py:47

commit v5 on v4

--- a/solution.py
+++ b/solution.py
@@ -100,9 +100,18 @@
 
 def times_matrix(values, matrix):
     count = values.shape[0]
-    high, low = halves(values)
-    both = product(jnp.concatenate([high, low]), matrix)
+    both = product(jnp.concatenate(halves(values)), matrix)
     return both[:count] + both[count:]
+
+
+def products_by_row(left, right):
+    count, width = left.shape[0], right.shape[0]
+    both = lax.dot_general(
+        jnp.concatenate(halves(left)), jnp.concatenate(halves(right)), (((1,), (1,)), ((), ())),
+        preferred_element_type=F32,
+    )
+    wide = jnp.concatenate([both, jnp.zeros((2 * count, 128 - 2 * width), F32)], axis=1)
+    return wide[:count] + pltpu.roll(wide[:count], 128 - width, 1) + wide[count:]
 
 
 def start_kernel(
@@ -132,22 +141,30 @@
         out[...] = values
 
 
-def fetch_kernel(pair, schur_hbm, partner_hbm, lengths_hbm, schur, tables, sign_live, partner, lengths, arrivals):
+def fetch_kernel(
+    pair, modes, schur_hbm, partner_hbm, lengths_hbm, coarse_hbm, schur, tables, sign_live, wide_coarse, partner, lengths,
+    coarse, arrivals
+):
+    sources = (partner_hbm, lengths_hbm, coarse_hbm, schur_hbm)
     copies = [
-        pltpu.make_async_copy(partner_hbm, partner, arrivals.at[0]),
-        pltpu.make_async_copy(lengths_hbm, lengths, arrivals.at[1]),
-        pltpu.make_async_copy(schur_hbm, schur, arrivals.at[2]),
+        pltpu.make_async_copy(source, target, arrivals.at[i])
+        for i, (source, target) in enumerate(zip(sources, (partner, lengths, coarse, schur)))
     ]
     for copy in copies:
         copy.start()
+    shape = (wide_coarse.shape[0], coarse.shape[0])
+    wide, order = lax.broadcasted_iota(jnp.int32, shape, 0), lax.broadcasted_iota(jnp.int32, shape, 1)
+    mode = wide % STRIP
+    place = jnp.where((mode < modes) & (wide // STRIP * modes + mode == order), 1.0, 0.0)
     row = lax.broadcasted_iota(jnp.int32, (pair, pair), 0)
     lane = lax.broadcasted_iota(jnp.int32, (1, pair), 1)
-    copies[0].wait()
-    copies[1].wait()
+    for copy in copies[:3]:
+        copy.wait()
     for d in range(4):
         tables[d] = jnp.where(partner[d:d + 1] == row, 1.0, 0.0).astype(BF16)
         sign_live[:, d * pair:(d + 1) * pair] = jnp.where(lane < lengths[:, d:d + 1], (-1.0, 1.0)[d % 2], 0.0)
-    copies[2].wait()
+    wide_coarse[...] = full_product_t(full_product(place, coarse[...]), place)
+    copies[3].wait()
 
 
 def gram_kernel(
@@ -188,12 +205,14 @@
     image[...] = times_matrix(operand[0:2 * span + cases], schur[...])
     for g in range(6):
         right[g * modes:(g + 1) * modes] = image[g * STRIP:g * STRIP + modes]
-    gram = full_product_t(operand[...], right[...])
+    gram = products_by_row(operand[...], right[...])
     lane = lax.broadcasted_iota(jnp.int32, (STRIP, gram.shape[1]), 1)
     strips = []
     for g in range(6):
         strip = gram[g * STRIP:(g + 1) * STRIP]
         own = (lane >= g * modes) & (lane < (g + 1) * modes)
+        if g == 1:
+            own = own | (lane >= 6 * modes)
         strips.append(jnp.where(own, 0.5 * strip, strip))
     rows = []
     for row in pack_places(modes):
@@ -204,7 +223,7 @@
         rows.append(total)
     total = jnp.concatenate(rows)
     lane = lax.broadcasted_iota(jnp.int32, total.shape, 1)
-    at = 12 * modes
+    at = 13 * modes
     with_first = gram[2 * span:2 * span + cases]
     with_rhs = gram[2 * span + cases:2 * span + 2 * cases]
     total = jnp.where(lane >= at, pltpu.roll(with_first, at, 1), total)
@@ -222,10 +241,12 @@
 
 
 def pack_places(modes):
-    upper = [(0, 0, 7 * modes, 0), (2, 2 * modes, 7 * modes, 7 * modes)]
+    upper = [
+        (0, 0, 6 * modes, 0), (2, 2 * modes, 7 * modes, 6 * modes), (1, 6 * modes, 7 * modes, 11 * modes),
+    ]
     lower = [
-        (1, modes, 7 * modes, 0), (3, 3 * modes, 6 * modes, 6 * modes),
-        (4, 4 * modes, 6 * modes, 9 * modes), (5, 5 * modes, 6 * modes, 11 * modes),
+        (1, modes, 7 * modes, 0), (3, 3 * modes, 6 * modes, 6 * modes), (4, 4 * modes, 6 * modes, 9 * modes),
+        (5, 5 * modes, 6 * modes, 11 * modes), (2, 6 * modes, 7 * modes, 12 * modes),
     ]
     return upper, lower
 
@@ -265,7 +286,7 @@
 def unpack(half, strips, modes, clusters):
     width = clusters * STRIP
     lane = lax.broadcasted_iota(jnp.int32, (STRIP, 128), 1)
-    upper, coupling, with_first, tails = {}, {}, {}, {}
+    upper, with_first, tails, coupling = {}, {}, {}, {}
 
     def put(store, key, values, begin, column):
         tile, offset = divmod(column, 128)
@@ -296,10 +317,10 @@
         for h in range(6):
             other, column = group(c, h)
             if 0 <= other < clusters:
-                put(with_first, (half,), values, 12 * modes + h * modes, column)
+                put(with_first, (half,), values, 13 * modes + h * modes, column)
         put(tails, (half,), values, 19 * modes, c * STRIP)
-        put(tails, (2 + half,), values, 18 * modes, c * STRIP)
-    return upper, coupling, with_first, tails
+        put(tails, (half,), values, 20 * modes, width + c * STRIP)
+    return upper, with_first, tails, coupling
 
 
 def spread(half, strips, modes, clusters, bases, outs):
@@ -312,18 +333,36 @@
                 out[at] = values + store[i, t] if (i, t) in store else values
 
 
-def own_half_kernel(modes, clusters, mine, *outs):
+def stack_rows(values):
+    high, low = halves(values)
+    return jnp.concatenate([high, low, high])
+
+
+def stack_lanes(values, second):
+    high, low = halves(values)
+    return jnp.concatenate([high, low, high] if second else [high, high, low], axis=1)
+
+
+def own_half_kernel(modes, clusters, mine, inverse, upper, with_first, tails, solver, coupling):
     even_c, _ = parities()
     for half in range(2):
         @pl.when(even_c if half == 0 else jnp.logical_not(even_c))
         def _():
-            spread(half, mine, modes, clusters, [None] * 4, outs)
+            spread(half, mine, modes, clusters, [None] * 4, (upper, with_first, tails, coupling))
+    width = clusters * STRIP
+    coarse, half_couple = inverse[...], coupling[:, :width]
+    solved = full_product(coarse, half_couple) + full_product_t(coarse, half_couple)
+    solved = full_product(solved, coarse)
+    solver[...] = stack_rows(jnp.concatenate([
+        jnp.concatenate([jnp.zeros_like(coarse), coarse], axis=1),
+        jnp.concatenate([coarse, -solved], axis=1),
+    ]))
 
 
 def solve_kernel(
-    pair, modes, clusters, other, part_upper, part_couple, part_rows, part_tails, inverse, stacked, rhs, first_part,
+    pair, modes, clusters, other, part_upper, part_first, part_tails, solver, stacked, rhs, first_part,
     applied_first, weight, sign_live, schur, scalars, to_a, to_b, to_c, to_d, first, applied, second, second_image,
-    upper_ref, couple_ref, row_ref, tail_ref, copies, ready
+    upper_ref, first_ref, tail_ref, copies, ready
 ):
     width = clusters * STRIP
     rows = 4 * pair
@@ -332,38 +371,32 @@
         @pl.when(even_c if half == 1 else jnp.logical_not(even_c))
         def _():
             spread(
-                half, other, modes, clusters, (part_upper, part_couple, part_rows, part_tails),
-                (upper_ref, couple_ref, row_ref, tail_ref),
+                half, other, modes, clusters, (part_upper, part_first, part_tails), (upper_ref, first_ref, tail_ref)
             )
 
-    solver = inverse[...]
-    couple_solver = full_product(couple_ref[:, :width], solver)
-
-    def coeffs(straight, weighted):
-        both = full_product(jnp.concatenate([straight, weighted]), solver)
-        a = both[:PACK]
-        return a, both[PACK:] - full_product(a, couple_solver)
-
-    def combine(a, b, tables):
-        high, low = halves(jnp.concatenate([a, b]))
-        moved = product(jnp.concatenate([high, high, low], axis=1), tables)
-        return [[moved[i * PACK:(i + 1) * PACK, k * rows:(k + 1) * rows] for k in range(4)] for i in range(2)]
-
-    tail = tail_ref[:, :width]
-    a_first, b_first = coeffs(tail[:PACK], tail[PACK:])
-    c_first = jnp.concatenate([a_first, b_first], axis=1)
-    upper_matrix = upper_ref[:, :2 * width]
-    parts = row_ref[:, :2 * width] - full_product(c_first, upper_matrix) - full_product_t(c_first, upper_matrix)
-    a_second, b_second = coeffs(parts[:, width:], parts[:, :width])
-
-    a_of, b_of = combine(a_first, b_first, jnp.concatenate([stacked[:, :2 * rows], stacked[:, 4 * rows:]], axis=1))
+    def combine(coefficients, tables):
+        both = jnp.concatenate([coefficients[:, :width], coefficients[:, width:]])
+        both = stack_lanes(both, False)
+        moved = [product(both, stacked[:, k * rows:(k + 1) * rows]) for k in tables]
+        return [part[:PACK] for part in moved], [part[PACK:] for part in moved]
+
+    solve = solver[...]
+    upper_matrix = upper_ref[...]
+    coefficients = product(stack_lanes(tail_ref[...], False), solve)
+    split = stack_lanes(coefficients, False)
+    parts = first_ref[...] - product(split, stack_rows(upper_matrix)) - lax.dot_general(
+        split, stack_lanes(upper_matrix, True), (((1,), (1,)), ((), ())), preferred_element_type=F32
+    )
+    later_coefficients = product(stack_lanes(parts, False), solve)
+
+    a_of, b_of = combine(coefficients, (0, 1, 4, 5))
     projected = rhs[...] - a_of[0]
     direction = first_part[...] - a_of[1] - b_of[0]
     image = applied_first[...] - a_of[2] - b_of[3]
     heavy = weight[...] * image
     heavy_image = times_matrix(sign_live[...] * heavy, schur[...])
 
-    a_of, b_of = combine(a_second, b_second, stacked[:, :4 * rows])
+    a_of, b_of = combine(later_coefficients, (0, 1, 2, 3))
     image_projected = image - a_of[0]
     last = heavy - a_of[1] - b_of[0]
     last_image = heavy_image - a_of[2] - b_of[3]
@@ -378,12 +411,9 @@
         folded(0.5 * (image_projected * last)),
         folded(0.5 * (image * last)),
         folded((sign_live[...] * last) * last_image),
-        jnp.zeros((128 - 6 * PACK, pair), F32),
     ])
-    ones = jnp.ones((STRIP, 2 * pair), BF16)
-    row = lax.dot_general(
-        ones, jnp.concatenate(halves(terms), axis=1), (((1,), (1,)), ((), ())), preferred_element_type=F32
-    )[0:1]
+    eye = lax.broadcasted_iota(jnp.int32, terms.shape, 0) == lax.broadcasted_iota(jnp.int32, terms.shape, 1)
+    row = jnp.sum(jnp.where(eye, jnp.sum(terms, axis=1, keepdims=True), 0.0), axis=0, keepdims=True)
     copies[...] = jnp.broadcast_to(row[:, None, :], copies.shape)
     copy = pltpu.make_async_copy(copies, scalars, ready)
     copy.start()
@@ -462,11 +492,6 @@
     width = clusters * STRIP
     span = 3 * STRIP
 
-    wide_inverse = jnp.pad(
-        coarse_inverse.reshape(clusters, modes, clusters, modes),
-        ((0, 0), (0, STRIP - modes), (0, 0), (0, STRIP - modes)),
-    ).reshape(width, width)
-
     flat = ((cases, rows), F32)
     sent = call(
         functools.partial(start_kernel, pair, modes),
@@ -476,18 +501,19 @@
         own_load, own_rigid, matrix, place=pltpu.HBM,
     )
     arrived = swap(sent)
-    matrix, tables, sign_live = call(
-        functools.partial(fetch_kernel, pair),
-        [((rows, rows), BF16), ((4, pair, pair), BF16), ((1, rows), F32)],
-        [pltpu.VMEM((4, pair), jnp.int32), pltpu.VMEM((1, 4), jnp.int32), pltpu.SemaphoreType.DMA((3,))],
-        matrix, partner[0, 0], lengths[0], place=pltpu.HBM,
+    matrix, tables, sign_live, wide_inverse = call(
+        functools.partial(fetch_kernel, pair, modes),
+        [((rows, rows), BF16), ((4, pair, pair), BF16), ((1, rows), F32), ((width, width), F32)],
+        [pltpu.VMEM((4, pair), jnp.int32), pltpu.VMEM((1, 4), jnp.int32), pltpu.VMEM(coarse_inverse.shape, F32),
+         pltpu.SemaphoreType.DMA((4,))],
+        matrix, partner[0, 0], lengths[0], coarse_inverse, place=pltpu.HBM,
     )
 
     packed, *images, rhs, first_part, weight, basis, image = call(
         functools.partial(gram_kernel, pair, modes, clusters, subs, cases),
         [((devices * STRIP, 128), F32)] + [((2 * span + cases, pair), F32)] * 4
         + [flat, flat, ((1, rows), F32), ((2 * span, rows), F32), ((2 * span + cases, rows), F32)],
-        [pltpu.VMEM((2 * span + 2 * cases, rows), F32), pltpu.VMEM((128, rows), F32),
+        [pltpu.VMEM((2 * span + 2 * cases, rows), F32), pltpu.VMEM((48, rows), F32),
          pltpu.VMEM((devices * STRIP, 128), F32), pltpu.SemaphoreType.DMA],
         matrix, sign_live, tables, *sent, *arrived, first_place=pltpu.HBM,
     )
@@ -503,16 +529,17 @@
 
     mine = jnp.sum(gathered.reshape(clusters, subs, STRIP, 128), axis=1).reshape(width, 128)
     other = lax.ppermute(mine, AXES, swap_tables(clusters, subs)[3])
-    lanes = max(width, 128)
-    shapes = [((2 * width, max(2 * width, 128)), F32), ((width, lanes), F32), ((PACK, max(2 * width, 128)), F32),
-              ((2 * PACK, lanes), F32)]
-    parts = call(functools.partial(own_half_kernel, modes, clusters), shapes, [], mine)
+    shapes = [((2 * width, 2 * width), F32), ((PACK, 2 * width), F32), ((PACK, 2 * width), F32)]
+    parts = call(
+        functools.partial(own_half_kernel, modes, clusters), shapes + [((6 * width, 2 * width), BF16)],
+        [pltpu.VMEM((width, max(width, 128)), F32)], mine, wide_inverse,
+    )
     scalars, *images, first, applied, second, second_image = call(
         functools.partial(solve_kernel, pair, modes, clusters),
         [((devices, 1, 128), F32)] + [((cases, pair), F32)] * 4 + [flat] * 4,
         [pltpu.VMEM(*shape) for shape in shapes]
         + [pltpu.VMEM((devices, 1, 128), F32), pltpu.SemaphoreType.DMA],
-        other, *parts, wide_inverse, stacked, rhs, first_part, applied_first, weight, sign_live, matrix,
+        other, *parts, stacked, rhs, first_part, applied_first, weight, sign_live, matrix,
         first_place=pltpu.HBM,
     )
     gathered = lax.all_to_all(scalars, AXES, 0, 0, tiled=True)

time: 38.1 us -> 37.1 us (0.974)
  Pallas kernels: 7.86 us -> 7.45 us
    pallas_call x8, Pallas kernels: 7.86 us -> 7.45 us  [call(): pl.pallas_call(kernel, out_shape=[place_out(shape, dtype) for place_out,...]
  transfers between devices with their start and end apart: 15 -> 15, of which waited for: 6 -> 6; matrix products, arithmetic and copies ran while one was open for 1% -> 0% of each run, Pallas kernels for 5% -> 7%
where the time goes in v5:
time: 37.1 us; the launch traced here: 36.8 us
  starting transfers between devices  22.2 us (60%)
  Pallas kernels  7.45 us (20%)
  waiting for transfers between devices  6.42 us (17%)
  between operations  0.74 us (2%)
    ppermute x12, starting transfers between devices, swap(): lax.ppermute(buffer, AXES, table)  15.9 us
    pallas_call x8, Pallas kernels, call(): pl.pallas_call(kernel, out_shape=[place_out(shape, dtype) for place_out,...  7.45 us
    ppermute x12, waiting for transfers between devices, swap(): lax.ppermute(buffer, AXES, table)  4.07 us
    all_to_all x1, starting transfers between devices, shards(): gathered = lax.all_to_all(packed, AXES, 0, 0, tiled=True)  3.72 us
    all_to_all x1, starting transfers between devices, shards(): gathered = lax.all_to_all(scalars, AXES, 0, 0, tiled=True)  2.56 us
    all_to_all x1, waiting for transfers between devices, shards(): gathered = lax.all_to_all(packed, AXES, 0, 0, tiled=True)  1.34 us
  transfers between devices with their start and end apart: 15, of which 6 were waited for; matrix products, arithmetic and copies ran while one was open for 0% of the time, Pallas kernels for 7%

profile of v5, /device:TPU:0, one launch (start us, length us, event | category | flops | bytes accessed | tf_op | source)
XLA Modules:
  0.0 36.8 jit_solution(11148463713519475257)
XLA Ops:
  0.6 1.0 %shard_map.78 = (f32[24,128]{1,0:T(8,128)S(1)}, f32[24,128]{1,0:T(8,128)S(1)}, f32[24,128]{1,0:T(8,128)S(1)}, f32[24,128]{1,0:T(8,128)S(1)}) custom-call(f32[4,16,128]{2,1,0:T(8,128)} %bitcast.19, f32[6,4,128]{2,1,0:T(4,128)} %bitcast.20, bf16[512,512]{1,0:T(8,128)(2,1)} %bitcast.15), custom_call_target="tpu_custom_call" | custom-call | tf_op jit(solution)/shard_map/pallas_call | solution.py:474
  1.6 3.1 %collective-permute-start = (f32[24,128]{1,0:T(8,128)S(1)}, f32[24,128]{1,0:T(8,128)S(1)}, u32[]{:S(2)}, u32[]{:S(2)}) collective-permute-start(f32[24,128]{1,0:T(8,128)S(1)} %get-tuple-element.42.sent_a), channel_id=1, source_target_pairs={{0,1},{1,0},{2,3},{3,2},{4,5},{5,4},{6,7},{7,6},{8,9},{9,8},{10,11... | collective-permute-start | bytes 36872 | tf_op jit(solution)/shard_map/ppermute | solution.py:47
  4.7 0.0 collective-permute-start.1
  4.7 3.1 %collective-permute-start.2 = (f32[24,128]{1,0:T(8,128)S(1)}, f32[24,128]{1,0:T(8,128)S(1)}, u32[]{:S(2)}, u32[]{:S(2)}) collective-permute-start(f32[24,128]{1,0:T(8,128)S(1)} %get-tuple-element.44.sent_c), channel_id=1, source_target_pairs={{0,1},{1,0},{2,3},{3,2},{4,8},{5,9},{6,10},{7,11},{8,4},{9,5},{10,... | collective-permute-start | bytes 36872 | tf_op jit(solution)/shard_map/ppermute | solution.py:47
  7.8 0.0 collective-permute-start.3
  7.8 1.2 %shard_map.77 = (bf16[512,512]{1,0:T(8,128)(2,1)S(1)}, bf16[4,128,128]{2,1,0:T(8,128)(2,1)S(1)}, f32[1,512]{1,0:T(1,128)S(1)}, f32[64,64]{1,0:T(8,128)S(1)}) custom-call(bf16[512,512]{1,0:T(8,128)(2,1)} %bitcast.16, s32[4,128]{1,0:T(4,128)} %bitcast.21, s32[1,4]{1,0:T(1,128)} %bitcast.22, f32[48,48]{1,0:T(8,128)} %coarse_hbm.1), custom_call_target="tpu_custom_call" | custom-call | tf_op jit(solution)/shard_map/pallas_call | solution.py:474
  9.0 0.0 collective-permute-done.from_a
  9.0 0.0 collective-permute-done.1.from_b
  9.1 0.5 %collective-permute-done.2.from_c = f32[24,128]{1,0:T(8,128)S(1)} collective-permute-done((f32[24,128]{1,0:T(8,128)S(1)}, f32[24,128]{1,0:T(8,128)S(1)}, u32[]{:S(2)}, u32[]{:S(2)}) %collective-permute-start.2) | collective-permute-done | bytes 12320 | tf_op jit(solution)/shard_map/ppermute | solution.py:47
  9.5 0.0 collective-permute-done.3.from_d
  9.5 1.4 %shard_map.79 = (f32[256,128]{1,0:T(8,128)}, f32[64,128]{1,0:T(8,128)S(1)}, f32[64,128]{1,0:T(8,128)S(1)}, f32[64,128]{1,0:T(8,128)S(1)}, f32[64,128]{1,0:T(8,12...) custom-call(bf16[512,512]{1,0:T(8,128)(2,1)S(1)} %get-tuple-element., ...), custom_call_target="tpu_custom_call" | custom-call | tf_op jit(solution)/shard_map/pallas_call | solution.py:474
  10.9 3.7 %all-to-all-start = ((f32[32,8,128]{2,1,0:T(8,128)}), f32[32,8,128]{2,1,0:T(8,128)S(1)}, u32[]{:S(2)}, u32[]{:S(2)}) async-start(f32[32,8,128]{2,1,0:T(8,128)} %bitcast.18), calls=%async_computation | async-start | bytes 262144 | tf_op jit(solution)/shard_map/all_to_all | solution.py:520
  14.6 1.8 %collective-permute-start.4 = (f32[64,128]{1,0:T(8,128)S(1)}, f32[64,128]{1,0:T(8,128)S(1)}, u32[]{:S(2)}, u32[]{:S(2)}) collective-permute-start(f32[64,128]{1,0:T(8,128)S(1)} %get-tuple-element.49), channel_id=1, source_target_pairs={{0,1},{1,0},{2,3},{3,2},{4,5},{5,4},{6,7},{7,6},{8,9},{9,8},{10,11... | collective-permute-start | bytes 98312 | tf_op jit(solution)/shard_map/ppermute | solution.py:47
  16.5 0.0 collective-permute-start.5
  16.5 3.0 %collective-permute-start.6 = (f32[64,128]{1,0:T(8,128)S(1)}, f32[64,128]{1,0:T(8,128)S(1)}, u32[]{:S(2)}, u32[]{:S(2)}) collective-permute-start(f32[64,128]{1,0:T(8,128)S(1)} %get-tuple-element.51), channel_id=1, source_target_pairs={{0,1},{1,0},{2,3},{3,2},{4,8},{5,9},{6,10},{7,11},{8,4},{9,5},{10,... | collective-permute-start | bytes 98312 | tf_op jit(solution)/shard_map/ppermute | solution.py:47
  19.4 0.0 collective-permute-start.7
  19.4 0.0 collective-permute-done.4.from_a
  19.4 0.0 collective-permute-done.5.from_b
  19.5 2.0 %collective-permute-done.6.from_c = f32[64,128]{1,0:T(8,128)S(1)} collective-permute-done((f32[64,128]{1,0:T(8,128)S(1)}, f32[64,128]{1,0:T(8,128)S(1)}, u32[]{:S(2)}, u32[]{:S(2)}) %collective-permute-start.6) | collective-permute-done | bytes 32800 | tf_op jit(solution)/shard_map/ppermute | solution.py:47
  21.4 0.0 collective-permute-done.7.from_d
  21.4 0.5 %shard_map.80 = (bf16[192,3072]{1,0:T(8,128)(2,1)S(1)}, f32[16,512]{1,0:T(8,128)S(1)}) custom-call(f32[48,512]{1,0:T(8,128)S(1)} %get-tuple-element.47.basis, f32[64,512]{1,0:T(8,128)S(1)} %get-tuple-element.48.image, f32[1,512]{1,0:T(1,128)S(1)} %get-tuple-element.40.sign_live, bf16[4,128,128]{2,1,0:T(8,128)(2,1)S(1)} %get-tuple-element.41.tables, ...), custom_call_target="tpu_custom_call" | custom-call | tf_op jit(solution)/shard_map/pallas_call | solution.py:474
  21.9 1.3 %all-to-all-done = f32[32,8,128]{2,1,0:T(8,128)S(1)} async-done(((f32[32,8,128]{2,1,0:T(8,128)}), f32[32,8,128]{2,1,0:T(8,128)S(1)}, u32[]{:S(2)}, u32[]{:S(2)}) %all-to-all-start) | async-done | bytes 131104 | tf_op jit(solution)/shard_map/all_to_all | solution.py:520
  23.3 0.1 collective-permute-start.8
  23.3 0.7 %shard_map.81 = (f32[128,128]{1,0:T(8,128)S(1)}, f32[16,128]{1,0:T(8,128)S(1)}, f32[16,128]{1,0:T(8,128)S(1)}, bf16[384,128]{1,0:T(8,128)(2,1)S(1)}) custom-call(f32[64,128]{1,0:T(8,128)S(1)} %bitcast.14, f32[64,64]{1,0:T(8,128)S(1)} %get-tuple-element.55.inverse), custom_call_target="tpu_custom_call" | custom-call | tf_op jit(solution)/shard_map/pallas_call | solution.py:474
  24.0 0.5 %collective-permute-done.8.other = f32[64,128]{1,0:T(8,128)S(1)} collective-permute-done((f32[64,128]{1,0:T(8,128)S(1)}, f32[64,128]{1,0:T(8,128)S(1)}, u32[]{:S(2)}, u32[]{:S(2)}) %collective-permute-start.8) | collective-permute-done | bytes 32800 | tf_op jit(solution)/shard_map/ppermute | solution.py:531
  24.5 1.8 %shard_map.82 = (f32[32,1,128]{2,1,0:T(1,128)}, f32[16,128]{1,0:T(8,128)S(1)}, f32[16,128]{1,0:T(8,128)S(1)}, f32[16,128]{1,0:T(8,128)S(1)}, f32[16,128]{1,0:T(8...) custom-call(f32[64,128]{1,0:T(8,128)S(1)} %collective-permute-done.8.o, ...), custom_call_target="tpu_custom_call" | custom-call | tf_op jit(solution)/shard_map/pallas_call | solution.py:474
  26.3 2.6 %all-to-all-start.1 = ((f32[32,1,128]{2,1,0:T(1,128)}), f32[32,1,128]{2,1,0:T(1,128)S(1)}, u32[]{:S(2)}, u32[]{:S(2)}) async-start(f32[32,1,128]{2,1,0:T(1,128)} %get-tuple-element.65), calls=%async_computation.1 | async-start | bytes 32768 | tf_op jit(solution)/shard_map/all_to_all | solution.py:545
  28.9 1.8 %collective-permute-start.9 = (f32[16,128]{1,0:T(8,128)S(1)}, f32[16,128]{1,0:T(8,128)S(1)}, u32[]{:S(2)}, u32[]{:S(2)}) collective-permute-start(f32[16,128]{1,0:T(8,128)S(1)} %get-tuple-element.70), channel_id=1, source_target_pairs={{0,1},{1,0},{2,3},{3,2},{4,5},{5,4},{6,7},{7,6},{8,9},{9,8},{10,11... | collective-permute-start | bytes 24584 | tf_op jit(solution)/shard_map/ppermute | solution.py:47
  30.7 0.0 collective-permute-start.10
  30.7 3.0 %collective-permute-start.11 = (f32[16,128]{1,0:T(8,128)S(1)}, f32[16,128]{1,0:T(8,128)S(1)}, u32[]{:S(2)}, u32[]{:S(2)}) collective-permute-start(f32[16,128]{1,0:T(8,128)S(1)} %get-tuple-element.72), channel_id=1, source_target_pairs={{0,1},{1,0},{2,3},{3,2},{4,8},{5,9},{6,10},{7,11},{8,4},{9,5},{10,... | collective-permute-start | bytes 24584 | tf_op jit(solution)/shard_map/ppermute | solution.py:47
  33.7 0.0 collective-permute-start.12
  33.7 0.0 collective-permute-done.9.from_a
  33.7 0.0 collective-permute-done.10.from_b
  33.7 1.6 %collective-permute-done.11.from_c = f32[16,128]{1,0:T(8,128)S(1)} collective-permute-done((f32[16,128]{1,0:T(8,128)S(1)}, f32[16,128]{1,0:T(8,128)S(1)}, u32[]{:S(2)}, u32[]{:S(2)}) %collective-permute-start.11) | collective-permute-done | bytes 8224 | tf_op jit(solution)/shard_map/ppermute | solution.py:47
  35.3 0.0 collective-permute-done.12.from_d
  35.3 0.2 shard_map.83.second_applied
  35.5 0.5 %all-to-all-done.1.scalars = f32[32,1,128]{2,1,0:T(1,128)S(1)} async-done(((f32[32,1,128]{2,1,0:T(1,128)}), f32[32,1,128]{2,1,0:T(1,128)S(1)}, u32[]{:S(2)}, u32[]{:S(2)}) %all-to-all-start.1) | async-done | bytes 16416 | tf_op jit(solution)/shard_map/all_to_all | solution.py:545
  36.0 0.9 %shard_map.84 = (f32[4,16,128]{2,1,0:T(8,128)}, f32[4,16,128]{2,1,0:T(8,128)}) custom-call(f32[32,1,128]{2,1,0:T(1,128)S(1)} %all-to-all-done.1.scalars, f32[16,512]{1,0:T(8,128)S(1)} %get-tuple-element.61.rhs, f32[16,512]{1,0:T(8,128)S(1)} %get-tuple-element.66.first, f32[16,512]{1,0:T(8,128)S(1)} %get-tuple-element.67.applied, ...), custom_call_target="tpu_custom_call" | custom-call | tf_op jit(solution)/shard_map/pallas_call | solution.py:474
  (1 shorter events, 0.0 us)
Async XLA Ops:
  1.6 7.4 %collective-permute-start = (f32[24,128]{1,0:T(8,128)S(1)}, f32[24,128]{1,0:T(8,128)S(1)}, u32[]{:S(2)}, u32[]{:S(2)}) collective-permute-start(f32[24,128]{1,0:T(8,128)S(1)} %get-tuple-element.42.sent_a), channel_id=1, source_target_pairs={{0,1},{1,0},{2,3},{3,2},{4,5},{5,4},{6,7},{7,6},{8,9},{9,8},{10,11... | collective-permute-start | bytes 36872 | tf_op jit(solution)/shard_map/ppermute | solution.py:47
  4.7 4.4 %collective-permute-start.1 = (f32[24,128]{1,0:T(8,128)S(1)}, f32[24,128]{1,0:T(8,128)S(1)}, u32[]{:S(2)}, u32[]{:S(2)}) collective-permute-start(f32[24,128]{1,0:T(8,128)S(1)} %get-tuple-element.43.sent_b), channel_id=1, source_target_pairs={{0,4},{1,2},{2,1},{3,7},{4,0},{5,6},{6,5},{7,3},{8,12},{9,10},{10,... | collective-permute-start | bytes 36872 | tf_op jit(solution)/shard_map/ppermute | solution.py:47
  4.7 4.8 %collective-permute-start.2 = (f32[24,128]{1,0:T(8,128)S(1)}, f32[24,128]{1,0:T(8,128)S(1)}, u32[]{:S(2)}, u32[]{:S(2)}) collective-permute-start(f32[24,128]{1,0:T(8,128)S(1)} %get-tuple-element.44.sent_c), channel_id=1, source_target_pairs={{0,1},{1,0},{2,3},{3,2},{4,8},{5,9},{6,10},{7,11},{8,4},{9,5},{10,... | collective-permute-start | bytes 36872 | tf_op jit(solution)/shard_map/ppermute | solution.py:47
  7.8 1.7 %collective-permute-start.3 = (f32[24,128]{1,0:T(8,128)S(1)}, f32[24,128]{1,0:T(8,128)S(1)}, u32[]{:S(2)}, u32[]{:S(2)}) collective-permute-start(f32[24,128]{1,0:T(8,128)S(1)} %get-tuple-element.45.sent_d), channel_id=1, source_target_pairs={{0,4},{1,5},{2,6},{3,7},{4,0},{5,1},{6,2},{7,3},{8,12},{9,13},{10,... | collective-permute-start | bytes 36872 | tf_op jit(solution)/shard_map/ppermute | solution.py:47
  10.9 12.3 %all-to-all-start = ((f32[32,8,128]{2,1,0:T(8,128)}), f32[32,8,128]{2,1,0:T(8,128)S(1)}, u32[]{:S(2)}, u32[]{:S(2)}) async-start(f32[32,8,128]{2,1,0:T(8,128)} %bitcast.18), calls=%async_computation | async-start | bytes 262144 | tf_op jit(solution)/shard_map/all_to_all | solution.py:520
  14.6 4.8 %collective-permute-start.4 = (f32[64,128]{1,0:T(8,128)S(1)}, f32[64,128]{1,0:T(8,128)S(1)}, u32[]{:S(2)}, u32[]{:S(2)}) collective-permute-start(f32[64,128]{1,0:T(8,128)S(1)} %get-tuple-element.49), channel_id=1, source_target_pairs={{0,1},{1,0},{2,3},{3,2},{4,5},{5,4},{6,7},{7,6},{8,9},{9,8},{10,11... | collective-permute-start | bytes 98312 | tf_op jit(solution)/shard_map/ppermute | solution.py:47
  16.5 3.0 %collective-permute-start.5 = (f32[64,128]{1,0:T(8,128)S(1)}, f32[64,128]{1,0:T(8,128)S(1)}, u32[]{:S(2)}, u32[]{:S(2)}) collective-permute-start(f32[64,128]{1,0:T(8,128)S(1)} %get-tuple-element.50), channel_id=1, source_target_pairs={{0,4},{1,2},{2,1},{3,7},{4,0},{5,6},{6,5},{7,3},{8,12},{9,10},{10,... | collective-permute-start | bytes 98312 | tf_op jit(solution)/shard_map/ppermute | solution.py:47
  16.5 5.0 %collective-permute-start.6 = (f32[64,128]{1,0:T(8,128)S(1)}, f32[64,128]{1,0:T(8,128)S(1)}, u32[]{:S(2)}, u32[]{:S(2)}) collective-permute-start(f32[64,128]{1,0:T(8,128)S(1)} %get-tuple-element.51), channel_id=1, source_target_pairs={{0,1},{1,0},{2,3},{3,2},{4,8},{5,9},{6,10},{7,11},{8,4},{9,5},{10,... | collective-permute-start | bytes 98312 | tf_op jit(solution)/shard_map/ppermute | solution.py:47
  19.4 2.0 %collective-permute-start.7 = (f32[64,128]{1,0:T(8,128)S(1)}, f32[64,128]{1,0:T(8,128)S(1)}, u32[]{:S(2)}, u32[]{:S(2)}) collective-permute-start(f32[64,128]{1,0:T(8,128)S(1)} %get-tuple-element.52), channel_id=1, source_target_pairs={{0,4},{1,5},{2,6},{3,7},{4,0},{5,1},{6,2},{7,3},{8,12},{9,13},{10,... | collective-permute-start | bytes 98312 | tf_op jit(solution)/shard_map/ppermute | solution.py:47
  23.3 1.3 %collective-permute-start.8 = (f32[64,128]{1,0:T(8,128)S(1)}, f32[64,128]{1,0:T(8,128)S(1)}, u32[]{:S(2)}, u32[]{:S(2)}) collective-permute-start(f32[64,128]{1,0:T(8,128)S(1)} %bitcast.13), channel_id=1, source_target_pairs={{0,4},{1,5},{2,6},{3,7},{4,0},{5,1},{6,2},{7,3},{8,12},{9,13},{10,... | collective-permute-start | bytes 98312 | tf_op jit(solution)/shard_map/ppermute | solution.py:531
  26.3 9.7 %all-to-all-start.1 = ((f32[32,1,128]{2,1,0:T(1,128)}), f32[32,1,128]{2,1,0:T(1,128)S(1)}, u32[]{:S(2)}, u32[]{:S(2)}) async-start(f32[32,1,128]{2,1,0:T(1,128)} %get-tuple-element.65), calls=%async_computation.1 | async-start | bytes 32768 | tf_op jit(solution)/shard_map/all_to_all | solution.py:545
  28.9 4.8 %collective-permute-start.9 = (f32[16,128]{1,0:T(8,128)S(1)}, f32[16,128]{1,0:T(8,128)S(1)}, u32[]{:S(2)}, u32[]{:S(2)}) collective-permute-start(f32[16,128]{1,0:T(8,128)S(1)} %get-tuple-element.70), channel_id=1, source_target_pairs={{0,1},{1,0},{2,3},{3,2},{4,5},{5,4},{6,7},{7,6},{8,9},{9,8},{10,11... | collective-permute-start | bytes 24584 | tf_op jit(solution)/shard_map/ppermute | solution.py:47
  30.7 3.0 %collective-permute-start.10 = (f32[16,128]{1,0:T(8,128)S(1)}, f32[16,128]{1,0:T(8,128)S(1)}, u32[]{:S(2)}, u32[]{:S(2)}) collective-permute-start(f32[16,128]{1,0:T(8,128)S(1)} %get-tuple-element.71), channel_id=1, source_target_pairs={{0,4},{1,2},{2,1},{3,7},{4,0},{5,6},{6,5},{7,3},{8,12},{9,10},{10,... | collective-permute-start | bytes 24584 | tf_op jit(solution)/shard_map/ppermute | solution.py:47
  30.7 4.6 %collective-permute-start.11 = (f32[16,128]{1,0:T(8,128)S(1)}, f32[16,128]{1,0:T(8,128)S(1)}, u32[]{:S(2)}, u32[]{:S(2)}) collective-permute-start(f32[16,128]{1,0:T(8,128)S(1)} %get-tuple-element.72), channel_id=1, source_target_pairs={{0,1},{1,0},{2,3},{3,2},{4,8},{5,9},{6,10},{7,11},{8,4},{9,5},{10,... | collective-permute-start | bytes 24584 | tf_op jit(solution)/shard_map/ppermute | solution.py:47
  33.7 1.6 %collective-permute-start.12 = (f32[16,128]{1,0:T(8,128)S(1)}, f32[16,128]{1,0:T(8,128)S(1)}, u32[]{:S(2)}, u32[]{:S(2)}) collective-permute-start(f32[16,128]{1,0:T(8,128)S(1)} %get-tuple-element.73), channel_id=1, source_target_pairs={{0,4},{1,5},{2,6},{3,7},{4,0},{5,1},{6,2},{7,3},{8,12},{9,13},{10,... | collective-permute-start | bytes 24584 | tf_op jit(solution)/shard_map/ppermute | solution.py:47

commit v6 on v5

--- a/solution.py
+++ b/solution.py
@@ -8,6 +8,7 @@
 from jax.sharding import PartitionSpec as P
 
 AXES = ("clus", "sub")
+SWAPS = ("sub_odd", "sub_even", "clus_odd", "clus_even")
 F32 = jnp.float32
 BF16 = jnp.bfloat16
 FULL = lax.Precision.HIGHEST
@@ -27,24 +28,25 @@
 
 
 def swap_tables(clusters, subs):
-    sub_even, sub_odd, clus_odd, clus_even = [], [], [], []
+    tables = {"sub_even": [], "sub_odd": [], "clus_even": [], "clus_odd": []}
     for c in range(clusters):
         for s in range(subs):
-            here = c * subs + s
-            sub_even.append((here, c * subs + pair_even(s, subs)))
-            odd = pair_odd(s, subs)
-            target = c * subs + odd if odd != s else pair_even(c, clusters) * subs + s
-            sub_odd.append((here, target))
-            odd = pair_odd(c, clusters)
-            target = odd * subs + s if odd != c else c * subs + pair_even(s, subs)
-            clus_odd.append((here, target))
-            clus_even.append((here, pair_even(c, clusters) * subs + s))
-    return sub_even, sub_odd, clus_odd, clus_even
+            odd_c, odd_s = pair_odd(c, clusters), pair_odd(s, subs)
+            even_c, even_s = pair_even(c, clusters), pair_even(s, subs)
+            targets = {
+                "sub_even": (c, even_s),
+                "sub_odd": (c, odd_s) if odd_s != s else (even_c, s),
+                "clus_even": (even_c, s),
+                "clus_odd": (odd_c, s) if odd_c != c else (c, even_s),
+            }
+            for name, (to_c, to_s) in targets.items():
+                tables[name].append((c * subs + s, to_c * subs + to_s))
+    return tables
 
 
 def swap(buffers):
     tables = swap_tables(lax.axis_size("clus"), lax.axis_size("sub"))
-    return [lax.ppermute(buffer, AXES, table) for buffer, table in zip(buffers, tables)]
+    return [lax.ppermute(buffer, AXES, tables[name]) for buffer, name in zip(buffers, SWAPS)]
 
 
 def parities():
@@ -55,21 +57,23 @@
 
 def by_swap(values):
     even_c, even_s = parities()
-    return [
-        jnp.where(even_s, values[1], values[0]),
-        jnp.where(even_s, values[0], values[1]),
-        jnp.where(even_c, values[2], values[3]),
-        jnp.where(even_c, values[3], values[2]),
-    ]
+    named = {
+        "sub_even": jnp.where(even_s, values[1], values[0]),
+        "sub_odd": jnp.where(even_s, values[0], values[1]),
+        "clus_even": jnp.where(even_c, values[3], values[2]),
+        "clus_odd": jnp.where(even_c, values[2], values[3]),
+    }
+    return [named[name] for name in SWAPS]
 
 
 def by_direction(values):
     even_c, even_s = parities()
+    named = dict(zip(SWAPS, values))
     return [
-        jnp.where(even_s, values[1], values[0]),
-        jnp.where(even_s, values[0], values[1]),
-        jnp.where(even_c, values[2], values[3]),
-        jnp.where(even_c, values[3], values[2]),
+        jnp.where(even_s, named["sub_odd"], named["sub_even"]),
+        jnp.where(even_s, named["sub_even"], named["sub_odd"]),
+        jnp.where(even_c, named["clus_odd"], named["clus_even"]),
+        jnp.where(even_c, named["clus_even"], named["clus_odd"]),
     ]
 
 
@@ -115,12 +119,12 @@
 
 
 def start_kernel(
-    pair, modes, load_hbm, rigid_hbm, schur_hbm, to_a, to_b, to_c, to_d, load, rigid, buffer, blocks, arrivals
+    pair, modes, load_hbm, rigid_hbm, schur_hbm, to_a, to_b, to_c, to_d, load, rigid, blocks, arrivals
 ):
     cases = load.shape[1]
     copies = [
         pltpu.make_async_copy(load_hbm, load, arrivals.at[0]),
-        pltpu.make_async_copy(rigid_hbm, rigid, arrivals.at[1]),
+        pltpu.make_async_copy(rigid_hbm, rigid.at[0:modes], arrivals.at[1]),
     ]
     for d in range(4):
         span = slice(d * pair, (d + 1) * pair)
@@ -128,17 +132,17 @@
     for copy in copies:
         copy.start()
     eye = lax.broadcasted_iota(jnp.int32, (pair, pair), 0) == lax.broadcasted_iota(jnp.int32, (pair, pair), 1)
-    buffer[...] = jnp.zeros_like(buffer)
+    row = lax.broadcasted_iota(jnp.int32, (STRIP, pair), 0)
     for copy in copies:
         copy.wait()
+    tiles = []
     for d in range(4):
-        buffer[d, 0:cases] = load[d]
-        buffer[d, cases:cases + modes] = rigid[:, d]
-        buffer[d, cases + STRIP - 1:cases + STRIP] = jnp.sum(
-            jnp.where(eye, blocks[d].astype(F32), 0.0), axis=0, keepdims=True
-        )
-    for out, values in zip((to_a, to_b, to_c, to_d), by_swap([buffer[d] for d in range(4)])):
-        out[...] = values
+        diag = jnp.sum(jnp.where(eye, blocks[d].astype(F32), 0.0), axis=0, keepdims=True)
+        tiles.append(jnp.where(row == STRIP - 1, diag, jnp.where(row < modes, rigid[:, d], 0.0)))
+    loads = by_swap([load[d] for d in range(4)])
+    for out, own_load, tile in zip((to_a, to_b, to_c, to_d), loads, by_swap(tiles)):
+        out[0:cases] = own_load
+        out[cases:cases + STRIP] = tile
 
 
 def fetch_kernel(
@@ -496,7 +500,7 @@
     sent = call(
         functools.partial(start_kernel, pair, modes),
         [((cases + STRIP, pair), F32)] * 4,
-        [pltpu.VMEM(own_load.shape, F32), pltpu.VMEM(own_rigid.shape, F32), pltpu.VMEM((4, cases + STRIP, pair), F32),
+        [pltpu.VMEM(own_load.shape, F32), pltpu.VMEM((STRIP, 4, pair), F32),
          pltpu.VMEM((4, pair, pair), BF16), pltpu.SemaphoreType.DMA((6,))],
         own_load, own_rigid, matrix, place=pltpu.HBM,
     )
@@ -528,7 +532,7 @@
     gathered, stacked = lax.optimization_barrier((gathered, stacked))
 
     mine = jnp.sum(gathered.reshape(clusters, subs, STRIP, 128), axis=1).reshape(width, 128)
-    other = lax.ppermute(mine, AXES, swap_tables(clusters, subs)[3])
+    other = lax.ppermute(mine, AXES, swap_tables(clusters, subs)["clus_even"])
     shapes = [((2 * width, 2 * width), F32), ((PACK, 2 * width), F32), ((PACK, 2 * width), F32)]
     parts = call(
         functools.partial(own_half_kernel, modes, clusters), shapes + [((6 * width, 2 * width), BF16)],

time: 37.1 us -> 36.9 us (level)
  starting transfers between devices: 22.2 us -> 21.7 us
    ppermute x13, waiting for transfers between devices: 4.57 us -> 5.86 us  [the longest x12 5.36 us: swap(): lax.ppermute(buffer, AXES, tables[name])]
    all_to_all x1, starting transfers between devices: 3.72 us -> 3.03 us  [shards(): gathered = lax.all_to_all(packed, AXES, 0, 0, tiled=True)]
    all_to_all x1, waiting for transfers between devices: 1.34 us -> 0.84 us  [shards(): gathered = lax.all_to_all(packed, AXES, 0, 0, tiled=True)]
    all_to_all x1, waiting for transfers between devices: 0.5 us -> 0.03 us  [shards(): gathered = lax.all_to_all(scalars, AXES, 0, 0, tiled=True)]
where the time goes in v6:
time: 36.9 us; the launch traced here: 36.6 us
  starting transfers between devices  21.7 us (59%)
  Pallas kernels  7.43 us (20%)
  waiting for transfers between devices  6.73 us (18%)
  between operations  0.73 us (2%)
    ppermute x12, starting transfers between devices, swap(): lax.ppermute(buffer, AXES, tables[name])  16 us
    pallas_call x8, Pallas kernels, call(): pl.pallas_call(kernel, out_shape=[place_out(shape, dtype) for place_out,...  7.43 us
    ppermute x12, waiting for transfers between devices, swap(): lax.ppermute(buffer, AXES, tables[name])  5.36 us
    all_to_all x1, starting transfers between devices, shards(): gathered = lax.all_to_all(packed, AXES, 0, 0, tiled=True)  3.03 us
    all_to_all x1, starting transfers between devices, shards(): gathered = lax.all_to_all(scalars, AXES, 0, 0, tiled=True)  2.56 us
    all_to_all x1, waiting for transfers between devices, shards(): gathered = lax.all_to_all(packed, AXES, 0, 0, tiled=True)  0.84 us
  transfers between devices with their start and end apart: 15, of which 6 were waited for; matrix products, arithmetic and copies ran while one was open for 0% of the time, Pallas kernels for 7%

profile of v6, /device:TPU:0, one launch (start us, length us, event | category | flops | bytes accessed | tf_op | source)
XLA Modules:
  0.0 36.6 jit_solution(5643002169747514744)
XLA Ops:
  0.6 0.9 %shard_map.78 = (f32[24,128]{1,0:T(8,128)S(1)}, f32[24,128]{1,0:T(8,128)S(1)}, f32[24,128]{1,0:T(8,128)S(1)}, f32[24,128]{1,0:T(8,128)S(1)}) custom-call(f32[4,16,128]{2,1,0:T(8,128)} %bitcast.19, f32[6,4,128]{2,1,0:T(4,128)} %bitcast.20, bf16[512,512]{1,0:T(8,128)(2,1)} %bitcast.15), custom_call_target="tpu_custom_call" | custom-call | tf_op jit(solution)/shard_map/pallas_call | solution.py:478
  1.6 0.5 %collective-permute-start = (f32[24,128]{1,0:T(8,128)S(1)}, f32[24,128]{1,0:T(8,128)S(1)}, u32[]{:S(2)}, u32[]{:S(2)}) collective-permute-start(f32[24,128]{1,0:T(8,128)S(1)} %get-tuple-element.42.sent_a), channel_id=1, source_target_pairs={{0,4},{1,2},{2,1},{3,7},{4,0},{5,6},{6,5},{7,3},{8,12},{9,10},{10,... | collective-permute-start | bytes 36872 | tf_op jit(solution)/shard_map/ppermute | solution.py:49
  2.1 4.1 %collective-permute-start.1 = (f32[24,128]{1,0:T(8,128)S(1)}, f32[24,128]{1,0:T(8,128)S(1)}, u32[]{:S(2)}, u32[]{:S(2)}) collective-permute-start(f32[24,128]{1,0:T(8,128)S(1)} %get-tuple-element.43.sent_b), channel_id=1, source_target_pairs={{0,1},{1,0},{2,3},{3,2},{4,5},{5,4},{6,7},{7,6},{8,9},{9,8},{10,11... | collective-permute-start | bytes 36872 | tf_op jit(solution)/shard_map/ppermute | solution.py:49
  6.3 0.0 collective-permute-start.2
  6.3 1.6 %collective-permute-start.3 = (f32[24,128]{1,0:T(8,128)S(1)}, f32[24,128]{1,0:T(8,128)S(1)}, u32[]{:S(2)}, u32[]{:S(2)}) collective-permute-start(f32[24,128]{1,0:T(8,128)S(1)} %get-tuple-element.45.sent_d), channel_id=1, source_target_pairs={{0,4},{1,5},{2,6},{3,7},{4,0},{5,1},{6,2},{7,3},{8,12},{9,13},{10,... | collective-permute-start | bytes 36872 | tf_op jit(solution)/shard_map/ppermute | solution.py:49
  7.9 1.2 %shard_map.77 = (bf16[512,512]{1,0:T(8,128)(2,1)S(1)}, bf16[4,128,128]{2,1,0:T(8,128)(2,1)S(1)}, f32[1,512]{1,0:T(1,128)S(1)}, f32[64,64]{1,0:T(8,128)S(1)}) custom-call(bf16[512,512]{1,0:T(8,128)(2,1)} %bitcast.16, s32[4,128]{1,0:T(4,128)} %bitcast.21, s32[1,4]{1,0:T(1,128)} %bitcast.22, f32[48,48]{1,0:T(8,128)} %coarse_hbm.1), custom_call_target="tpu_custom_call" | custom-call | tf_op jit(solution)/shard_map/pallas_call | solution.py:478
  9.1 0.0 collective-permute-done.from_a
  9.1 0.0 collective-permute-done.1.from_b
  9.1 0.9 %collective-permute-done.2.from_c = f32[24,128]{1,0:T(8,128)S(1)} collective-permute-done((f32[24,128]{1,0:T(8,128)S(1)}, f32[24,128]{1,0:T(8,128)S(1)}, u32[]{:S(2)}, u32[]{:S(2)}) %collective-permute-start.2) | collective-permute-done | bytes 12320 | tf_op jit(solution)/shard_map/ppermute | solution.py:49
  9.9 0.0 collective-permute-done.3.from_d
  10.0 1.4 %shard_map.79 = (f32[256,128]{1,0:T(8,128)}, f32[64,128]{1,0:T(8,128)S(1)}, f32[64,128]{1,0:T(8,128)S(1)}, f32[64,128]{1,0:T(8,128)S(1)}, f32[64,128]{1,0:T(8,12...) custom-call(bf16[512,512]{1,0:T(8,128)(2,1)S(1)} %get-tuple-element., ...), custom_call_target="tpu_custom_call" | custom-call | tf_op jit(solution)/shard_map/pallas_call | solution.py:478
  11.3 3.0 %all-to-all-start = ((f32[32,8,128]{2,1,0:T(8,128)}), f32[32,8,128]{2,1,0:T(8,128)S(1)}, u32[]{:S(2)}, u32[]{:S(2)}) async-start(f32[32,8,128]{2,1,0:T(8,128)} %bitcast.18), calls=%async_computation | async-start | bytes 262144 | tf_op jit(solution)/shard_map/all_to_all | solution.py:524
  14.4 0.3 collective-permute-start.4
  14.7 3.0 %collective-permute-start.5 = (f32[64,128]{1,0:T(8,128)S(1)}, f32[64,128]{1,0:T(8,128)S(1)}, u32[]{:S(2)}, u32[]{:S(2)}) collective-permute-start(f32[64,128]{1,0:T(8,128)S(1)} %get-tuple-element.50), channel_id=1, source_target_pairs={{0,1},{1,0},{2,3},{3,2},{4,5},{5,4},{6,7},{7,6},{8,9},{9,8},{10,11... | collective-permute-start | bytes 98312 | tf_op jit(solution)/shard_map/ppermute | solution.py:49
  17.7 0.0 collective-permute-start.6
  17.7 1.5 %collective-permute-start.7 = (f32[64,128]{1,0:T(8,128)S(1)}, f32[64,128]{1,0:T(8,128)S(1)}, u32[]{:S(2)}, u32[]{:S(2)}) collective-permute-start(f32[64,128]{1,0:T(8,128)S(1)} %get-tuple-element.52), channel_id=1, source_target_pairs={{0,4},{1,5},{2,6},{3,7},{4,0},{5,1},{6,2},{7,3},{8,12},{9,13},{10,... | collective-permute-start | bytes 98312 | tf_op jit(solution)/shard_map/ppermute | solution.py:49
  19.3 0.0 collective-permute-done.4.from_a
  19.3 0.6 %collective-permute-done.5.from_b = f32[64,128]{1,0:T(8,128)S(1)} collective-permute-done((f32[64,128]{1,0:T(8,128)S(1)}, f32[64,128]{1,0:T(8,128)S(1)}, u32[]{:S(2)}, u32[]{:S(2)}) %collective-permute-start.5) | collective-permute-done | bytes 32800 | tf_op jit(solution)/shard_map/ppermute | solution.py:49
  19.8 1.9 %collective-permute-done.6.from_c = f32[64,128]{1,0:T(8,128)S(1)} collective-permute-done((f32[64,128]{1,0:T(8,128)S(1)}, f32[64,128]{1,0:T(8,128)S(1)}, u32[]{:S(2)}, u32[]{:S(2)}) %collective-permute-start.6) | collective-permute-done | bytes 32800 | tf_op jit(solution)/shard_map/ppermute | solution.py:49
  21.7 0.0 collective-permute-done.7.from_d
  21.7 0.5 %shard_map.80 = (bf16[192,3072]{1,0:T(8,128)(2,1)S(1)}, f32[16,512]{1,0:T(8,128)S(1)}) custom-call(f32[48,512]{1,0:T(8,128)S(1)} %get-tuple-element.47.basis, f32[64,512]{1,0:T(8,128)S(1)} %get-tuple-element.48.image, f32[1,512]{1,0:T(1,128)S(1)} %get-tuple-element.40.sign_live, bf16[4,128,128]{2,1,0:T(8,128)(2,1)S(1)} %get-tuple-element.41.tables, ...), custom_call_target="tpu_custom_call" | custom-call | tf_op jit(solution)/shard_map/pallas_call | solution.py:478
  22.1 0.8 %all-to-all-done = f32[32,8,128]{2,1,0:T(8,128)S(1)} async-done(((f32[32,8,128]{2,1,0:T(8,128)}), f32[32,8,128]{2,1,0:T(8,128)S(1)}, u32[]{:S(2)}, u32[]{:S(2)}) %all-to-all-start) | async-done | bytes 131104 | tf_op jit(solution)/shard_map/all_to_all | solution.py:524
  23.0 0.1 collective-permute-start.8
  23.1 0.7 %shard_map.81 = (f32[128,128]{1,0:T(8,128)S(1)}, f32[16,128]{1,0:T(8,128)S(1)}, f32[16,128]{1,0:T(8,128)S(1)}, bf16[384,128]{1,0:T(8,128)(2,1)S(1)}) custom-call(f32[64,128]{1,0:T(8,128)S(1)} %bitcast.14, f32[64,64]{1,0:T(8,128)S(1)} %get-tuple-element.55.inverse), custom_call_target="tpu_custom_call" | custom-call | tf_op jit(solution)/shard_map/pallas_call | solution.py:478
  23.8 0.5 %collective-permute-done.8.other = f32[64,128]{1,0:T(8,128)S(1)} collective-permute-done((f32[64,128]{1,0:T(8,128)S(1)}, f32[64,128]{1,0:T(8,128)S(1)}, u32[]{:S(2)}, u32[]{:S(2)}) %collective-permute-start.8) | collective-permute-done | bytes 32800 | tf_op jit(solution)/shard_map/ppermute | solution.py:535
  24.3 1.8 %shard_map.82 = (f32[32,1,128]{2,1,0:T(1,128)}, f32[16,128]{1,0:T(8,128)S(1)}, f32[16,128]{1,0:T(8,128)S(1)}, f32[16,128]{1,0:T(8,128)S(1)}, f32[16,128]{1,0:T(8...) custom-call(f32[64,128]{1,0:T(8,128)S(1)} %collective-permute-done.8.o, ...), custom_call_target="tpu_custom_call" | custom-call | tf_op jit(solution)/shard_map/pallas_call | solution.py:478
  26.1 2.6 %all-to-all-start.1 = ((f32[32,1,128]{2,1,0:T(1,128)}), f32[32,1,128]{2,1,0:T(1,128)S(1)}, u32[]{:S(2)}, u32[]{:S(2)}) async-start(f32[32,1,128]{2,1,0:T(1,128)} %get-tuple-element.65), calls=%async_computation.1 | async-start | bytes 32768 | tf_op jit(solution)/shard_map/all_to_all | solution.py:549
  28.6 0.3 collective-permute-start.9
  28.9 3.0 %collective-permute-start.10 = (f32[16,128]{1,0:T(8,128)S(1)}, f32[16,128]{1,0:T(8,128)S(1)}, u32[]{:S(2)}, u32[]{:S(2)}) collective-permute-start(f32[16,128]{1,0:T(8,128)S(1)} %get-tuple-element.71), channel_id=1, source_target_pairs={{0,1},{1,0},{2,3},{3,2},{4,5},{5,4},{6,7},{7,6},{8,9},{9,8},{10,11... | collective-permute-start | bytes 24584 | tf_op jit(solution)/shard_map/ppermute | solution.py:49
  31.9 0.0 collective-permute-start.11
  31.9 1.6 %collective-permute-start.12 = (f32[16,128]{1,0:T(8,128)S(1)}, f32[16,128]{1,0:T(8,128)S(1)}, u32[]{:S(2)}, u32[]{:S(2)}) collective-permute-start(f32[16,128]{1,0:T(8,128)S(1)} %get-tuple-element.73), channel_id=1, source_target_pairs={{0,4},{1,5},{2,6},{3,7},{4,0},{5,1},{6,2},{7,3},{8,12},{9,13},{10,... | collective-permute-start | bytes 24584 | tf_op jit(solution)/shard_map/ppermute | solution.py:49
  33.5 0.0 collective-permute-done.9.from_a
  33.5 0.0 collective-permute-done.10.from_b
  33.5 2.0 %collective-permute-done.11.from_c = f32[16,128]{1,0:T(8,128)S(1)} collective-permute-done((f32[16,128]{1,0:T(8,128)S(1)}, f32[16,128]{1,0:T(8,128)S(1)}, u32[]{:S(2)}, u32[]{:S(2)}) %collective-permute-start.11) | collective-permute-done | bytes 8224 | tf_op jit(solution)/shard_map/ppermute | solution.py:49
  35.6 0.0 collective-permute-done.12.from_d
  35.6 0.2 shard_map.83.second_applied
  35.7 0.0 all-to-all-done.1.scalars
  35.7 0.9 %shard_map.84 = (f32[4,16,128]{2,1,0:T(8,128)}, f32[4,16,128]{2,1,0:T(8,128)}) custom-call(f32[32,1,128]{2,1,0:T(1,128)S(1)} %all-to-all-done.1.scalars, f32[16,512]{1,0:T(8,128)S(1)} %get-tuple-element.61.rhs, f32[16,512]{1,0:T(8,128)S(1)} %get-tuple-element.66.first, f32[16,512]{1,0:T(8,128)S(1)} %get-tuple-element.67.applied, ...), custom_call_target="tpu_custom_call" | custom-call | tf_op jit(solution)/shard_map/pallas_call | solution.py:478
  (1 shorter events, 0.0 us)
Async XLA Ops:
  1.6 7.5 %collective-permute-start = (f32[24,128]{1,0:T(8,128)S(1)}, f32[24,128]{1,0:T(8,128)S(1)}, u32[]{:S(2)}, u32[]{:S(2)}) collective-permute-start(f32[24,128]{1,0:T(8,128)S(1)} %get-tuple-element.42.sent_a), channel_id=1, source_target_pairs={{0,4},{1,2},{2,1},{3,7},{4,0},{5,6},{6,5},{7,3},{8,12},{9,10},{10,... | collective-permute-start | bytes 36872 | tf_op jit(solution)/shard_map/ppermute | solution.py:49
  2.1 7.0 %collective-permute-start.1 = (f32[24,128]{1,0:T(8,128)S(1)}, f32[24,128]{1,0:T(8,128)S(1)}, u32[]{:S(2)}, u32[]{:S(2)}) collective-permute-start(f32[24,128]{1,0:T(8,128)S(1)} %get-tuple-element.43.sent_b), channel_id=1, source_target_pairs={{0,1},{1,0},{2,3},{3,2},{4,5},{5,4},{6,7},{7,6},{8,9},{9,8},{10,11... | collective-permute-start | bytes 36872 | tf_op jit(solution)/shard_map/ppermute | solution.py:49
  6.3 3.7 %collective-permute-start.2 = (f32[24,128]{1,0:T(8,128)S(1)}, f32[24,128]{1,0:T(8,128)S(1)}, u32[]{:S(2)}, u32[]{:S(2)}) collective-permute-start(f32[24,128]{1,0:T(8,128)S(1)} %get-tuple-element.44.sent_c), channel_id=1, source_target_pairs={{0,1},{1,0},{2,3},{3,2},{4,8},{5,9},{6,10},{7,11},{8,4},{9,5},{10,... | collective-permute-start | bytes 36872 | tf_op jit(solution)/shard_map/ppermute | solution.py:49
  6.3 3.7 %collective-permute-start.3 = (f32[24,128]{1,0:T(8,128)S(1)}, f32[24,128]{1,0:T(8,128)S(1)}, u32[]{:S(2)}, u32[]{:S(2)}) collective-permute-start(f32[24,128]{1,0:T(8,128)S(1)} %get-tuple-element.45.sent_d), channel_id=1, source_target_pairs={{0,4},{1,5},{2,6},{3,7},{4,0},{5,1},{6,2},{7,3},{8,12},{9,13},{10,... | collective-permute-start | bytes 36872 | tf_op jit(solution)/shard_map/ppermute | solution.py:49
  11.3 11.7 %all-to-all-start = ((f32[32,8,128]{2,1,0:T(8,128)}), f32[32,8,128]{2,1,0:T(8,128)S(1)}, u32[]{:S(2)}, u32[]{:S(2)}) async-start(f32[32,8,128]{2,1,0:T(8,128)} %bitcast.18), calls=%async_computation | async-start | bytes 262144 | tf_op jit(solution)/shard_map/all_to_all | solution.py:524
  14.4 4.9 %collective-permute-start.4 = (f32[64,128]{1,0:T(8,128)S(1)}, f32[64,128]{1,0:T(8,128)S(1)}, u32[]{:S(2)}, u32[]{:S(2)}) collective-permute-start(f32[64,128]{1,0:T(8,128)S(1)} %get-tuple-element.49), channel_id=1, source_target_pairs={{0,4},{1,2},{2,1},{3,7},{4,0},{5,6},{6,5},{7,3},{8,12},{9,10},{10,... | collective-permute-start | bytes 98312 | tf_op jit(solution)/shard_map/ppermute | solution.py:49
  14.7 5.1 %collective-permute-start.5 = (f32[64,128]{1,0:T(8,128)S(1)}, f32[64,128]{1,0:T(8,128)S(1)}, u32[]{:S(2)}, u32[]{:S(2)}) collective-permute-start(f32[64,128]{1,0:T(8,128)S(1)} %get-tuple-element.50), channel_id=1, source_target_pairs={{0,1},{1,0},{2,3},{3,2},{4,5},{5,4},{6,7},{7,6},{8,9},{9,8},{10,11... | collective-permute-start | bytes 98312 | tf_op jit(solution)/shard_map/ppermute | solution.py:49
  17.7 4.0 %collective-permute-start.6 = (f32[64,128]{1,0:T(8,128)S(1)}, f32[64,128]{1,0:T(8,128)S(1)}, u32[]{:S(2)}, u32[]{:S(2)}) collective-permute-start(f32[64,128]{1,0:T(8,128)S(1)} %get-tuple-element.51), channel_id=1, source_target_pairs={{0,1},{1,0},{2,3},{3,2},{4,8},{5,9},{6,10},{7,11},{8,4},{9,5},{10,... | collective-permute-start | bytes 98312 | tf_op jit(solution)/shard_map/ppermute | solution.py:49
  17.7 4.0 %collective-permute-start.7 = (f32[64,128]{1,0:T(8,128)S(1)}, f32[64,128]{1,0:T(8,128)S(1)}, u32[]{:S(2)}, u32[]{:S(2)}) collective-permute-start(f32[64,128]{1,0:T(8,128)S(1)} %get-tuple-element.52), channel_id=1, source_target_pairs={{0,4},{1,5},{2,6},{3,7},{4,0},{5,1},{6,2},{7,3},{8,12},{9,13},{10,... | collective-permute-start | bytes 98312 | tf_op jit(solution)/shard_map/ppermute | solution.py:49
  23.0 1.3 %collective-permute-start.8 = (f32[64,128]{1,0:T(8,128)S(1)}, f32[64,128]{1,0:T(8,128)S(1)}, u32[]{:S(2)}, u32[]{:S(2)}) collective-permute-start(f32[64,128]{1,0:T(8,128)S(1)} %bitcast.13), channel_id=1, source_target_pairs={{0,4},{1,5},{2,6},{3,7},{4,0},{5,1},{6,2},{7,3},{8,12},{9,13},{10,... | collective-permute-start | bytes 98312 | tf_op jit(solution)/shard_map/ppermute | solution.py:535
  26.1 9.7 %all-to-all-start.1 = ((f32[32,1,128]{2,1,0:T(1,128)}), f32[32,1,128]{2,1,0:T(1,128)S(1)}, u32[]{:S(2)}, u32[]{:S(2)}) async-start(f32[32,1,128]{2,1,0:T(1,128)} %get-tuple-element.65), calls=%async_computation.1 | async-start | bytes 32768 | tf_op jit(solution)/shard_map/all_to_all | solution.py:549
  28.6 4.9 %collective-permute-start.9 = (f32[16,128]{1,0:T(8,128)S(1)}, f32[16,128]{1,0:T(8,128)S(1)}, u32[]{:S(2)}, u32[]{:S(2)}) collective-permute-start(f32[16,128]{1,0:T(8,128)S(1)} %get-tuple-element.70), channel_id=1, source_target_pairs={{0,4},{1,2},{2,1},{3,7},{4,0},{5,6},{6,5},{7,3},{8,12},{9,10},{10,... | collective-permute-start | bytes 24584 | tf_op jit(solution)/shard_map/ppermute | solution.py:49
  28.9 4.6 %collective-permute-start.10 = (f32[16,128]{1,0:T(8,128)S(1)}, f32[16,128]{1,0:T(8,128)S(1)}, u32[]{:S(2)}, u32[]{:S(2)}) collective-permute-start(f32[16,128]{1,0:T(8,128)S(1)} %get-tuple-element.71), channel_id=1, source_target_pairs={{0,1},{1,0},{2,3},{3,2},{4,5},{5,4},{6,7},{7,6},{8,9},{9,8},{10,11... | collective-permute-start | bytes 24584 | tf_op jit(solution)/shard_map/ppermute | solution.py:49
  31.9 3.7 %collective-permute-start.11 = (f32[16,128]{1,0:T(8,128)S(1)}, f32[16,128]{1,0:T(8,128)S(1)}, u32[]{:S(2)}, u32[]{:S(2)}) collective-permute-start(f32[16,128]{1,0:T(8,128)S(1)} %get-tuple-element.72), channel_id=1, source_target_pairs={{0,1},{1,0},{2,3},{3,2},{4,8},{5,9},{6,10},{7,11},{8,4},{9,5},{10,... | collective-permute-start | bytes 24584 | tf_op jit(solution)/shard_map/ppermute | solution.py:49
  31.9 3.6 %collective-permute-start.12 = (f32[16,128]{1,0:T(8,128)S(1)}, f32[16,128]{1,0:T(8,128)S(1)}, u32[]{:S(2)}, u32[]{:S(2)}) collective-permute-start(f32[16,128]{1,0:T(8,128)S(1)} %get-tuple-element.73), channel_id=1, source_target_pairs={{0,4},{1,5},{2,6},{3,7},{4,0},{5,1},{6,2},{7,3},{8,12},{9,13},{10,... | collective-permute-start | bytes 24584 | tf_op jit(solution)/shard_map/ppermute | solution.py:49
